TPU v7x, 128 devices: a whole 4x4x4 slice. The times are simulated.
128 devices in a mesh: head: 4 (over z_hi, core), blk: 32 (over y, z_lo, x).
Axes of the slice: x: 4, y: 4, z: 4 (z_hi: 2, z_lo: 2; z = z_hi * 2 + z_lo), core: 2. Of those that a mesh axis runs over, the one named last changes fastest.
Arguments:
- inputs: bfloat16 [6144, 1, 3072], P('blk', None, 'head'), may hold values from -17.5 to 17.5
- out_grad: bfloat16 [6144, 1, 3072], P('blk', None, 'head'), may hold values from -6 to 6
- qkv_weight: bfloat16 [3072, 3, 1536], P(None, None, 'head'), may hold values from -0.108253175 to 0.108253175
- out_weight: bfloat16 [3072, 1536], P(None, 'head'), may hold values from -0.15625 to 0.15625
- text_keys: bfloat16 [256, 1, 1536], P(None, None, 'head'), may hold values from -6 to 6
- text_values: bfloat16 [256, 1, 1536], P(None, None, 'head'), may hold values from -6 to 6
- text_mask: int32 [256, 1], replicated, may hold values 0 or 1
Outputs:
- grad_inputs: bfloat16 [6144, 1, 3072], P('blk', None, 'head')
- grad_qkv_weight: float32 [3072, 3, 1536], P('blk', None, 'head')
- grad_out_weight: float32 [3072, 1536], P('blk', 'head')
- grad_text_keys: float32 [256, 1, 1536], P('blk', None, 'head')
- grad_text_values: float32 [256, 1, 1536], P('blk', None, 'head')
All inputs are finite; a program needn't handle non-finite values.
Results may differ from a plain program's by a relative error of at most 0.034.
Values may be sent and summed in bfloat16 or wider, within the bound.
No kernel may reach another device: no remote copies, remote signals or barrier semaphores. Data moves between devices by JAX's collectives and lax.ppermute only.
A program may use at most 128 MiB of HBM per device.

v0:
```python
import jax
import jax.numpy as jnp
from jax import lax
from jax.sharding import PartitionSpec as P

HD = 128


masked_fill = -1000000000.0


def masked_logits(query_heads, key_rows, valid_rows, score_scale):
    logits = (
        jnp.einsum("vsne,jsne->snvj", query_heads, key_rows, preferred_element_type=jnp.float32)
        * score_scale
    )
    if valid_rows is not None:
        logits = jnp.where(valid_rows.T[:, None, None, :], logits, masked_fill)
    return logits


def attend_block(softmax_state, query_heads, key_rows, value_rows, valid_rows, score_scale):
    running_max, running_sum, running_acc = softmax_state
    logits = masked_logits(query_heads, key_rows, valid_rows, score_scale)
    new_max = jnp.maximum(running_max, jnp.max(logits, axis=-1))
    factor = jnp.exp(running_max - new_max)
    weights = jnp.exp(logits - new_max[..., None])
    new_sum = running_sum * factor + jnp.sum(weights, axis=-1)
    update = jnp.einsum(
        "snvj,jsne->snve",
        weights.astype(jnp.bfloat16),
        value_rows,
        preferred_element_type=jnp.float32,
    )
    return (new_max, new_sum, running_acc * factor[..., None] + update)


def grad_block(
    query_heads, grad_heads, key_rows, value_rows, valid_rows, log_total, row_dot, score_scale
):
    logits = masked_logits(query_heads, key_rows, valid_rows, score_scale)
    probabilities = jnp.exp(logits - log_total[..., None])
    grad_values = jnp.einsum(
        "snvj,vsne->jsne",
        probabilities.astype(jnp.bfloat16),
        grad_heads,
        preferred_element_type=jnp.float32,
    )
    grad_probs = jnp.einsum(
        "vsne,jsne->snvj", grad_heads, value_rows, preferred_element_type=jnp.float32
    )
    grad_logits = (probabilities * (grad_probs - row_dot[..., None]) * score_scale).astype(
        jnp.bfloat16
    )
    grad_queries = jnp.einsum(
        "snvj,jsne->vsne", grad_logits, key_rows, preferred_element_type=jnp.float32
    )
    grad_keys = jnp.einsum(
        "snvj,vsne->jsne", grad_logits, query_heads, preferred_element_type=jnp.float32
    )
    return (grad_queries, jnp.stack([grad_keys, grad_values], axis=2))


def key_blocks(full_kv, shard_rows, shards, seq_count, head_count, head_dim):
    group_size = 1
    while group_size * shard_rows < 512 and group_size < shards:
        group_size = group_size * 2
    return full_kv.reshape(
        shards // group_size, group_size * shard_rows, seq_count, 2, head_count, head_dim
    )


def per_device(inputs, out_grad, qkv_weight, out_weight, text_keys, text_values, text_mask):
    full_in, full_grad = (
        lax.all_gather(inputs, "head", axis=2, tiled=True),
        lax.all_gather(out_grad, "head", axis=2, tiled=True),
    )
    shard_rows = inputs.shape[0]
    seq_count = inputs.shape[1]
    local_width = qkv_weight.shape[2]
    head_dim = HD
    head_count = local_width // head_dim
    score_scale = head_dim ** (-0.5)
    shards = lax.axis_size("blk")
    projected = jnp.einsum(
        "vsd,dch->vsch", full_in, qkv_weight, preferred_element_type=jnp.float32
    ).astype(jnp.bfloat16)
    grad_attn = jnp.einsum(
        "vsd,dh->vsh", full_grad, out_weight, preferred_element_type=jnp.float32
    ).astype(jnp.bfloat16)
    query_heads = projected[:, :, 0].reshape(shard_rows, seq_count, head_count, head_dim)
    grad_heads = grad_attn.reshape(shard_rows, seq_count, head_count, head_dim)
    kv_local = projected[:, :, 1:]
    text_rows = text_keys.shape[0]
    valid_text = text_mask == 1
    text_key_heads = text_keys.reshape(text_rows, seq_count, head_count, head_dim)
    text_value_heads = text_values.reshape(text_rows, seq_count, head_count, head_dim)
    start_state = (
        jnp.full((seq_count, head_count, shard_rows), -1e30, jnp.float32),
        jnp.zeros((seq_count, head_count, shard_rows), jnp.float32),
        jnp.zeros((seq_count, head_count, shard_rows, head_dim), jnp.float32),
    )
    softmax_state = attend_block(
        start_state, query_heads, text_key_heads, text_value_heads, valid_text, score_scale
    )
    kv_piece = lax.all_gather(kv_local, "blk", axis=0, tiled=True)
    key_slice = kv_piece.reshape(kv_piece.shape[0], seq_count, 2, head_count, head_dim)
    softmax_state = attend_block(
        softmax_state, query_heads, key_slice[:, :, 0], key_slice[:, :, 1], None, score_scale
    )
    run_max, run_sum, run_acc = softmax_state
    out_heads = jnp.transpose(run_acc / run_sum[..., None], (2, 0, 1, 3)).astype(jnp.bfloat16)
    attn_out = out_heads.reshape(shard_rows, seq_count, local_width)
    log_total = run_max + jnp.log(run_sum)
    row_dot = jnp.transpose(
        jnp.sum(grad_heads.astype(jnp.float32) * out_heads.astype(jnp.float32), axis=-1), (1, 2, 0)
    )
    text_query_grads, text_terms = grad_block(
        query_heads,
        grad_heads,
        text_key_heads,
        text_value_heads,
        valid_text,
        log_total,
        row_dot,
        score_scale,
    )
    text_sums = lax.psum_scatter(
        text_terms.reshape(text_rows, seq_count, 2, local_width).astype(jnp.bfloat16),
        "blk",
        scatter_dimension=0,
        tiled=True,
    ).astype(jnp.float32)
    full_kv = lax.all_gather(kv_local, "blk", axis=0, tiled=True)
    blocks = key_blocks(full_kv, shard_rows, shards, seq_count, head_count, head_dim)

    def backward_step(running, kv_block):
        partial_value, key_term = grad_block(
            query_heads,
            grad_heads,
            kv_block[:, :, 0],
            kv_block[:, :, 1],
            None,
            log_total,
            row_dot,
            score_scale,
        )
        return (running + partial_value, key_term)

    query_grads, key_terms = lax.scan(backward_step, text_query_grads, blocks)
    key_terms = key_terms.reshape(full_kv.shape[0], seq_count, 2, local_width)
    kv_grads = lax.psum_scatter(
        key_terms.astype(jnp.bfloat16), "blk", scatter_dimension=0, tiled=True
    )
    grad_projected = jnp.concatenate(
        [query_grads.astype(jnp.bfloat16).reshape(shard_rows, seq_count, 1, local_width), kv_grads],
        axis=2,
    )
    input_terms = jnp.einsum(
        "vsch,dch->vsd", grad_projected, qkv_weight, preferred_element_type=jnp.float32
    )
    grad_inputs = lax.psum_scatter(
        input_terms.astype(jnp.bfloat16), "head", scatter_dimension=2, tiled=True
    )
    qkv_part = jnp.einsum(
        "vsd,vsch->dch", full_in, grad_projected, preferred_element_type=jnp.float32
    )
    out_part = jnp.einsum("vsd,vsh->dh", full_grad, attn_out, preferred_element_type=jnp.float32)
    weight_grads = lax.psum_scatter(
        jnp.concatenate([qkv_part, out_part[:, None]], axis=1).astype(jnp.bfloat16),
        "blk",
        scatter_dimension=0,
        tiled=True,
    ).astype(jnp.float32)
    return (
        grad_inputs,
        weight_grads[:, :3],
        weight_grads[:, 3],
        text_sums[:, :, 0],
        text_sums[:, :, 1],
    )


def solution(mesh):
    return jax.shard_map(
        per_device,
        mesh=mesh,
        in_specs=(
            P("blk", None, "head"),
            P("blk", None, "head"),
            P(None, None, "head"),
            P(None, "head"),
            P(None, None, "head"),
            P(None, None, "head"),
            P(),
        ),
        out_specs=(
            P("blk", None, "head"),
            P("blk", None, "head"),
            P("blk", "head"),
            P("blk", None, "head"),
            P("blk", None, "head"),
        ),
        check_vma=False,
    )
```

profile of v0, /device:TPU:1, one launch (start us, length us, event | category | flops | bytes accessed | tf_op | source)
XLA Modules:
  0.0 982.5 jit_solution(9667658025365504058)
XLA Ops:
  8.7 26.2 %all-gather.4.cloned.1.call-done = bf16[192,1,3072]{2,0,1:T(8,128)(2,1)} async-done(((bf16[192,1,768]{2,0,1:T(8,128)(2,1)}), bf16[192,1,3072]{2,0,1:T(8,128)(2,1)}) %all-gather.4.cloned.1.call-update) | async-done | bytes 1179664 | tf_op jit(solution)/shard_map/all_gather | solution.py:75
  35.0 5.1 fusion.21
  40.1 0.7 slice.41
  40.9 0.8 copy.66
  42.1 15.5 %all-gather.8.cloned.1.call-done = bf16[192,1,3072]{2,0,1:T(8,128)(2,1)} async-done(((bf16[192,1,768]{2,0,1:T(8,128)(2,1)}), bf16[192,1,3072]{2,0,1:T(8,128)(2,1)}) %all-gather.8.cloned.1.call-update) | async-done | bytes 1179664 | tf_op jit(solution)/shard_map/all_gather | solution.py:76
  57.5 2.0 fusion.31
  60.7 148.9 %all-gather.6.cloned.1.call-done = bf16[6144,1,2,384]{3,0,2,1:T(8,128)(2,1)} async-done(((bf16[192,1,2,384]{3,0,2,1:T(8,128)(2,1)}), bf16[6144,1,2,384]{3,0,2,1:T(8,128)(2,1)}) %all-gather.6.cloned.1.call-update) | async-done | bytes 9437200 | tf_op jit(solution)/shard_map/all_gather | solution.py:106
  209.6 12.8 %copy.63 = bf16[6144,1,2,384]{0,3,2,1:T(8,128)(2,1)} copy(bf16[6144,1,2,384]{3,0,2,1:T(8,128)(2,1)} %all-gather.6.cloned.1.call-done) | data formatting | bytes 18874368 | tf_op jit(solution)/shard_map/all_gather | solution.py:106
  222.3 9.4 multiply_reduce_fusion
  231.8 8.3 fusion.9
  240.1 7.5 fusion.8
  249.6 24.5 %reshape.395 = bf16[8,768,1,2,3,128]{5,4,1,0,3,2:T(4,128)(2,1)} reshape(bf16[6144,1,2,384]{3,0,2,1:T(8,128)(2,1)} %all-gather.6.cloned.1.call-done) | data formatting | bytes 18874368 | tf_op jit(solution)/shard_map/reshape | solution.py:68
  274.1 10.8 %copy.74 = bf16[8,768,1,2,3,128]{5,1,4,3,2,0:T(8,128)(2,1)} copy(bf16[8,768,1,2,3,128]{5,4,1,0,3,2:T(4,128)(2,1)} %reshape.395) | data formatting | bytes 18874368 | tf_op jit(solution)/shard_map/while | solution.py:150
  284.9 38.7 %while.12 = (s32[]{:T(128)}, f32[192,1,3,128]{3,0,2,1:T(8,128)S(1)}, bf16[8,768,1,2,3,128]{5,1,4,3,2,0:T(8,128)(2,1)}, bf16[8,768,1,2,3,128]{5,1,4,3,2,0:T(8,128...) while((s32[]{:T(128)}, ...), condition=%wide.region_6.7_spmd, body=%wide.region_5.6_spmd.sunk | while | flops 571760640 | bytes 16818284 | solution.py:150
  284.9 1.3 dynamic-slice_bitcast_fusion.2
  288.6 1.1 fusion.93
  289.7 1.3 dynamic-slice_bitcast_fusion.2
  293.4 1.1 fusion.93
  294.5 1.3 dynamic-slice_bitcast_fusion.2
  298.3 1.1 fusion.93
  299.4 1.3 dynamic-slice_bitcast_fusion.2
  303.1 1.1 fusion.93
  304.2 1.3 dynamic-slice_bitcast_fusion.2
  307.9 1.1 fusion.93
  309.0 1.3 dynamic-slice_bitcast_fusion.2
  312.8 1.1 fusion.93
  313.9 1.3 dynamic-slice_bitcast_fusion.2
  317.6 1.1 fusion.93
  318.7 1.3 dynamic-slice_bitcast_fusion.2
  322.5 1.1 fusion.93
  323.6 14.0 %copy.93 = bf16[8,768,1,2,3,128]{5,4,1,0,3,2:T(4,128)(2,1)} copy(bf16[8,768,1,2,3,128]{5,1,4,3,2,0:T(8,128)(2,1)} %get-tuple-element.49) | data formatting | bytes 18874368 | tf_op jit(solution)/shard_map/convert_element_type | solution.py:153
  337.6 24.4 %reshape.396 = bf16[6144,1,2,384]{3,0,2,1:T(8,128)(2,1)} reshape(bf16[8,768,1,2,3,128]{5,4,1,0,3,2:T(4,128)(2,1)} %copy.93) | data formatting | bytes 18874368 | tf_op jit(solution)/shard_map/convert_element_type | solution.py:153
  362.1 0.8 copy-done.14
  362.9 0.8 copy.80
  363.9 0.8 reshape.390
  366.3 1.6 pad_maximum_fusion.1
  367.9 2.1 fusion.14
  370.0 171.5 %reduce-scatter.3.cloned.1.call-done = bf16[192,1,2,384]{3,0,2,1:T(8,128)(2,1)} async-done(((bf16[6144,1,2,384]{3,0,2,1:T(8,128)(2,1)}), bf16[192,1,2,384]{3,0,2,1:T(8,128)(2,1)}) %reduce-scatter.3.cloned.1.call-update) | async-done | bytes 294928 | tf_op jit(solution)/shard_map/reduce_scatter | solution.py:152
  541.5 6.3 convert_bitcast_fusion
  547.8 7.5 pad_maximum_fusion
  555.3 15.4 %copy.81 = bf16[3072,4,384]{2,1,0:T(4,128)(2,1)} copy(bf16[3072,4,384]{0,2,1:T(8,128)(2,1)} %pad_maximum_fusion) | data formatting | bytes 18874368 | tf_op jit(solution)/shard_map/concatenate | solution.py:170
  570.8 0.9 copy-done.16
  571.7 6.5 fusion.16
  580.1 341.2 %all-reduce.5.cloned.1.call-done = (bf16[3072,4,384]{2,1,0:T(4,128)(2,1)}, bf16[256,1,2,384]{3,2,1,0:T(2,128)(2,1)}) async-done(((bf16[3072,4,384]{2,1,0:T(4,128)(2,1)}, bf16[256,1,2,384]{3,2,1,0:T(2,128)(2,1)}), (bf16[3072,4,384]{2,1,0:T(4,128)(2,1)}, bf16[256,1,2,384]{3,2,1,0:T(2,128)(2,1)})) %all-reduce.5.cloned.1.call-update) | async-done | bytes 9830416
  921.3 1.0 dynamic-slice_convert_fusion
  922.5 0.8 copy.86
  924.0 0.7 dynamic-slice_convert_fusion.1
  925.4 50.3 %reduce-scatter.5.cloned.1.call-done = bf16[192,1,768]{2,0,1:T(8,128)(2,1)} async-done(((bf16[192,1,3072]{2,0,1:T(8,128)(2,1)}), bf16[192,1,768]{2,0,1:T(8,128)(2,1)}) %reduce-scatter.5.cloned.1.call-update) | async-done | bytes 294928 | tf_op jit(solution)/shard_map/reduce_scatter | solution.py:162
  (119 shorter events, 27.6 us)
Async XLA Ops:
  7.2 50.4 %copy-start = (bf16[3072,384]{1,0:T(8,128)(2,1)S(1)}, bf16[3072,384]{1,0:T(8,128)(2,1)}, u32[]{:S(2)}) copy-start(bf16[3072,384]{1,0:T(8,128)(2,1)} %param.12) | copy-start | bytes 7077892
  7.2 27.8 %all-gather.4.cloned.1.call-start = ((), (), s32[]{:S(2)}) async-start(), calls=%async_computation.2 | async-start | bytes 1474560 | tf_op jit(solution)/shard_map/all_gather | solution.py:75
  7.9 49.6 %all-gather.8.cloned.1.call-start = ((), (), s32[]{:S(2)}) async-start(), calls=%async_computation.4 | async-start | bytes 1474560 | tf_op jit(solution)/shard_map/all_gather | solution.py:76
  8.7 32.2 %copy-start.17 = (bf16[256,1,384]{2,0,1:T(8,128)(2,1)S(1)}, bf16[256,1,384]{2,0,1:T(8,128)(2,1)}, u32[]{:S(2)}) copy-start(bf16[256,1,384]{2,0,1:T(8,128)(2,1)} %param.14) | copy-start | bytes 589828
  8.7 33.1 %copy-start.18 = (bf16[256,1,384]{2,0,1:T(8,128)(2,1)S(1)}, bf16[256,1,384]{2,0,1:T(8,128)(2,1)}, u32[]{:S(2)}) copy-start(bf16[256,1,384]{2,0,1:T(8,128)(2,1)} %param.13) | copy-start | bytes 589828
  8.7 33.2 %copy-start.19 = (s32[256,1]{0,1:T(1,128)S(1)}, s32[256,1]{0,1:T(1,128)}, u32[]{:S(2)}) copy-start(s32[256,1]{0,1:T(1,128)} %param.15) | copy-start | bytes 3076
  8.7 200.9 %all-gather.6.cloned.1.call-start = ((), (), s32[]{:S(2)}) async-start(), calls=%async_computation.3 | async-start | bytes 9732096 | tf_op jit(solution)/shard_map/all_gather | solution.py:106
  40.8 500.7 %reduce-scatter.3.cloned.1.call-start = ((), (), s32[]{:S(2)}) async-start(), calls=%async_computation.5 | async-start | bytes 9732096 | tf_op jit(solution)/shard_map/reduce_scatter | solution.py:152
  41.9 180.4 %copy-start.6 = (bf16[256,1,384]{0,2,1:T(8,128)(2,1)}, bf16[256,1,384]{0,2,1:T(8,128)(2,1)S(1)}, u32[]{:S(2)}) copy-start(bf16[256,1,384]{0,2,1:T(8,128)(2,1)S(1)} %copy.60) | copy-start | bytes 589828
  42.0 180.3 %copy-start.4 = (bf16[192,3,128]{2,1,0:T(4,128)(2,1)}, bf16[192,3,128]{2,1,0:T(4,128)(2,1)S(1)}, u32[]{:S(2)}) copy-start(bf16[192,3,128]{2,1,0:T(4,128)(2,1)S(1)} %reshape.380) | copy-start | bytes 442372
  59.6 0.7 copy-start.8
  240.0 8.0 copy-start.12
  240.0 9.0 copy-start.9
  240.1 9.3 copy-start.7
  248.4 0.7 copy-start.13
  249.3 24.7 %copy-start.2 = (bf16[3,192,256]{2,1,0:T(8,128)(2,1)}, bf16[3,192,256]{2,1,0:T(8,128)(2,1)S(1)}, u32[]{:S(2)}) copy-start(bf16[3,192,256]{2,1,0:T(8,128)(2,1)S(1)} %fusion.20) | copy-start | bytes 884740
  362.0 0.9 copy-start.14
  362.0 2.7 copy-start.10
  362.0 3.5 copy-start.3
  362.0 3.5 copy-start.5
  362.1 559.3 %all-reduce.5.cloned.1.call-start = ((), (), s32[]{:S(2)}) async-start(), calls=%async_computation.7 | async-start | bytes 19660800
  363.8 4.2 copy-start.11
  365.1 176.5 %copy-start.15 = (bf16[192,1,1,384]{3,0,2,1:T(8,128)(2,1)S(1)}, bf16[192,1,1,384]{3,0,2,1:T(8,128)(2,1)}, u32[]{:S(2)}) copy-start(bf16[192,1,1,384]{3,0,2,1:T(8,128)(2,1)} %reshape.390) | copy-start | bytes 442372
  570.7 1.0 copy-start.16
  570.7 7.5 copy-start.20
  570.7 404.9 %copy-start.1 = (bf16[3072,384]{1,0:T(8,128)(2,1)S(1)}, bf16[3072,384]{1,0:T(8,128)(2,1)}, u32[]{:S(2)}) copy-start(bf16[3072,384]{1,0:T(8,128)(2,1)} %param.12) | copy-start | bytes 7077892
  570.7 404.9 %reduce-scatter.5.cloned.1.call-start = ((), (), s32[]{:S(2)}) async-start(), calls=%async_computation.6 | async-start | bytes 1474560 | tf_op jit(solution)/shard_map/reduce_scatter | solution.py:162
Sparse Core Ops, SparseCore 0:
  9.7 25.2 all-gather.3
  36.7 20.8 all-gather.7
  59.8 149.7 all-gather.5
  362.2 179.2 reduce-scatter.2
  570.8 350.4 all-reduce.4
  924.6 50.9 reduce-scatter.4
where the time goes:
time: 985 us; the launch traced here: 982 us
  waiting for transfers between devices  755 us (77%)
  local copies, waits for them, and re-layouts  123 us (12%)
  matrix products  60.4 us (6%)
  other arithmetic  27.9 us (3%)
  between operations  15.8 us (2%)
    unnamed x7, waiting for transfers between devices  343 us
    reduce_scatter x1, waiting for transfers between devices, per_device(): lax.psum_scatter(key_terms.astype(jnp.bfloat16), 'blk', scatter_dimension...  172 us
    all_gather x1, waiting for transfers between devices, per_device(): kv_piece = lax.all_gather(kv_local, 'blk', axis=0, tiled=True)  149 us
    reduce_scatter x1, waiting for transfers between devices, per_device(): lax.psum_scatter(input_terms.astype(jnp.bfloat16), 'head', scatter_dimens...  50.3 us
    convert_element_type x2, local copies, waits for them, and re-layouts, per_device(): key_terms.astype(jnp.bfloat16)  38.4 us
    all_gather x1, waiting for transfers between devices, per_device(): lax.all_gather(inputs, 'head', axis=2, tiled=True)  26.2 us
    reshape x1, local copies, waits for them, and re-layouts, key_blocks(): full_kv.reshape(shards // group_size, group_size * shard_rows, seq_count,...  24.5 us
  transfers between devices with their start and end apart: 6, of which 6 were waited for; matrix products, arithmetic and copies ran while one was open for 3% of the time, Pallas kernels for 0%

commit v1 on v0

v1 whole, which is shorter than its diff:
```python
import jax
import jax.numpy as jnp
from jax import lax
from jax.experimental import pallas as pl
from jax.experimental.pallas import tpu as pltpu
from jax.sharding import PartitionSpec as P

HD = 128
MASKED = -1000000000.0
F32 = jnp.float32
BF16 = jnp.bfloat16
NY = 4
NZX = 8


def nt_dot(a, b):
    return lax.dot_general(a, b, (((1,), (1,)), ((), ())), preferred_element_type=F32)


def nn_dot(a, b):
    return lax.dot_general(a, b, (((1,), (0,)), ((), ())), preferred_element_type=F32)


def tn_dot(a, b):
    return lax.dot_general(a, b, (((0,), (0,)), ((), ())), preferred_element_type=F32)


def rows_of(ref):
    block = ref[...]
    return block.reshape(-1, block.shape[-1])


def pick(parts, value):
    return jnp.concatenate([rows_of(part) for part in parts] + [value], axis=0)


def scores(keys, q, valid, video):
    s = nt_dot(keys, q) * HD**-0.5
    return jnp.concatenate([s[:video], jnp.where(valid, s[video:], MASKED)], axis=0)


def stats_kernel(q_ref, g_ref, *refs):
    ks, vs = refs[:NY], refs[NY : 2 * NY]
    tk_ref, tv_ref, mask_ref, stat_ref, out_ref = refs[2 * NY :]
    q, g = rows_of(q_ref), rows_of(g_ref)
    k, v = pick(ks, tk_ref[...]), pick(vs, tv_ref[...])
    s = scores(k, q, mask_ref[:, 0:1] == 1, k.shape[0] - tk_ref.shape[0])
    top = jnp.max(s, axis=0, keepdims=True)
    p = jnp.exp(s - top)
    total = jnp.sum(p, axis=0, keepdims=True)
    stat_ref[0, 0:1, :] = top
    stat_ref[0, 1:2, :] = total
    stat_ref[0, 2:3, :] = jnp.sum(p * nt_dot(v, g), axis=0, keepdims=True)
    out = tn_dot(v, p.astype(BF16)) / total
    out_ref[...] = out.T.astype(BF16).reshape(out_ref.shape)


def merged(stat_ref):
    tops = [stat_ref[i, 0, 0:1, :] for i in range(NZX)]
    top = tops[0]
    for other in tops[1:]:
        top = jnp.maximum(top, other)
    total = jnp.zeros_like(top)
    dot = jnp.zeros_like(top)
    shares = []
    for i in range(NZX):
        factor = jnp.exp(tops[i] - top)
        shares.append(factor * stat_ref[i, 0, 1:2, :])
        total += shares[i]
        dot += factor * stat_ref[i, 0, 2:3, :]
    return top, total, dot / total, shares


def combine_kernel(out_ref, stat_ref, o_ref):
    _, total, _, shares = merged(stat_ref)
    rows = out_ref.shape[1]
    acc = jnp.zeros((rows, HD), F32)
    for i in range(NZX):
        weight = jnp.broadcast_to(shares[i] / total, (HD, rows)).T
        acc += weight * out_ref[i].astype(F32)
    o_ref[...] = acc.astype(BF16)


def grads_kernel(q_ref, g_ref, *refs):
    ks, vs = refs[:NY], refs[NY : 2 * NY]
    tk_ref, tv_ref, mask_ref, stat_ref, dq_ref = refs[2 * NY : 2 * NY + 5]
    kv_refs, acc_ref = refs[2 * NY + 5 : -1], refs[-1]
    step, steps = pl.program_id(1), pl.num_programs(1)
    q, g = rows_of(q_ref), rows_of(g_ref)
    k, v = pick(ks, tk_ref[...]), pick(vs, tv_ref[...])
    keys = k.shape[0] - tk_ref.shape[0]
    top, total, dot, _ = merged(stat_ref)
    s = scores(k, q, mask_ref[:, 0:1] == 1, keys)
    p = jnp.exp(s - (top + jnp.log(total)))
    ds = (p * (nt_dot(v, g) - dot) * HD**-0.5).astype(BF16)
    dq = tn_dot(k, ds)
    dq_ref[...] = dq.T.astype(BF16).reshape(dq_ref.shape)

    @pl.when(step == 0)
    def _():
        acc_ref[...] = jnp.zeros_like(acc_ref)

    acc_ref[0] += nn_dot(ds, q)
    acc_ref[1] += nn_dot(p.astype(BF16), g)

    @pl.when(step == steps - 1)
    def _():
        per = keys // NY
        text = (acc_ref.shape[1] - keys) // NY
        for y in range(NY):
            kv_ref = kv_refs[y]
            kv_ref[:per] = acc_ref[0, y * per : (y + 1) * per].astype(BF16)
            kv_ref[per : 2 * per] = acc_ref[1, y * per : (y + 1) * per].astype(BF16)
            at = keys + y * text
            kv_ref[2 * per :] = jnp.concatenate(
                [acc_ref[0, at : at + text], acc_ref[1, at : at + text]], axis=0
            ).astype(BF16)


def weights_kernel(*refs):
    xs, gs, o_ref = refs[:NY], refs[NY : 2 * NY], refs[2 * NY]
    acc = tn_dot(xs[0][...], rows_of(gs[0]))
    for y in range(1, NY):
        acc += tn_dot(xs[y][...], rows_of(gs[y]))
    o_ref[:, 0] = acc.astype(BF16).reshape(o_ref.shape[0], o_ref.shape[2], o_ref.shape[3])


def per_device(inputs, out_grad, qkv_weight, out_weight, text_keys, text_values, text_mask):
    rows = inputs.shape[0]
    part = inputs.shape[2]
    width = qkv_weight.shape[2]
    heads = width // HD
    text = text_keys.shape[0]
    blk = lax.axis_index("blk")
    head = lax.axis_index("head")
    zx, y_at = lax.rem(blk, NZX), blk // NZX
    core, z_hi = lax.rem(head, 2), head // 2
    along_zx = [[y * NZX + i for i in range(NZX)] for y in range(NY)]
    core_swap = [(i, i ^ 1) for i in range(4)]
    z_swap = [(i, i ^ 2) for i in range(4)]

    def exchange(array):
        return lax.all_to_all(array, "blk", 0, 0, tiled=True, axis_index_groups=along_zx)

    def spread(array):
        return exchange(jnp.broadcast_to(array[None], (NZX,) + array.shape))

    def shift(array, by):
        return lax.ppermute(
            array, "blk", [(i, (i + by * NZX) % (NY * NZX)) for i in range(NY * NZX)]
        )

    def around(array):
        return [array] + [shift(array, by) for by in range(1, NY)]

    def head_gather(own):
        far = lax.ppermute(own, "head", z_swap)
        near = lax.ppermute(own, "head", core_swap)
        far_near = lax.ppermute(far, "head", core_swap)
        return [
            jnp.where(
                z_hi == z,
                jnp.where(core == c, own, near),
                jnp.where(core == c, far, far_near),
            )
            for z in range(2)
            for c in range(2)
        ]

    def slices_around(parts):
        def slice_for(y):
            return jnp.where(
                y < 2, jnp.where(y == 0, parts[0], parts[1]), jnp.where(y == 2, parts[2], parts[3])
            )

        own = slice_for(y_at)
        return [own] + [shift(slice_for(lax.rem(y_at + by, NY)), by) for by in range(1, NY)]

    in_parts = head_gather(inputs[:, 0])
    grad_parts = head_gather(out_grad[:, 0])
    projected = jnp.einsum(
        "vd,dch->cvh", jnp.concatenate(in_parts, axis=1), qkv_weight, preferred_element_type=F32
    ).astype(BF16)
    grad_attn = jnp.dot(
        jnp.concatenate(grad_parts, axis=1), out_weight, preferred_element_type=F32
    ).astype(BF16)

    kv_all = around(projected[1:])
    qg_all = spread(jnp.stack([projected[0], grad_attn]))

    text_own = text // (NY * NZX)
    text_per = NY * text_own
    slot = lax.broadcasted_iota(jnp.int32, (text_per, text), 0)
    source = lax.broadcasted_iota(jnp.int32, (text_per, text), 1)
    wanted = (lax.rem(y_at + NY - slot // text_own, NY) * NZX + zx) * text_own + lax.rem(
        slot, text_own
    )
    chosen = source == wanted
    select = chosen.astype(BF16)
    tk = jnp.dot(select, text_keys[:, 0], preferred_element_type=F32).astype(BF16)
    tv = jnp.dot(select, text_values[:, 0], preferred_element_type=F32).astype(BF16)
    mask = jnp.sum(jnp.where(chosen, text_mask[:, 0][None, :], 0), axis=1, keepdims=True)
    mask = jnp.broadcast_to(mask, (text_per, HD))

    half = NZX // 2
    q_rows = half * rows
    steps = NZX // half
    grid = (heads, steps)
    params = pltpu.CompilerParams(
        vmem_limit_bytes=56 * 1024 * 1024, dimension_semantics=("arbitrary", "arbitrary")
    )
    in_specs = (
        [
            pl.BlockSpec((half, 1, rows, HD), lambda h, i: (i, 0, 0, h)),
            pl.BlockSpec((half, 1, rows, HD), lambda h, i: (i, 1, 0, h)),
        ]
        + [pl.BlockSpec((1, rows, HD), lambda h, i: (0, 0, h))] * NY
        + [pl.BlockSpec((1, rows, HD), lambda h, i: (1, 0, h))] * NY
        + [
            pl.BlockSpec((text_per, HD), lambda h, i: (0, h)),
            pl.BlockSpec((text_per, HD), lambda h, i: (0, h)),
            pl.BlockSpec((text_per, HD), lambda h, i: (0, 0)),
        ]
    )
    x_in = slices_around(in_parts)
    x_grad = slices_around(grad_parts)
    operands = (qg_all, qg_all, *kv_all, *kv_all, tk, tv, mask)
    stats, out_terms = pl.pallas_call(
        stats_kernel,
        grid=grid,
        in_specs=in_specs,
        out_specs=[
            pl.BlockSpec((1, 3, q_rows), lambda h, i: (h, 0, i)),
            pl.BlockSpec((half, rows, HD), lambda h, i: (i, 0, h)),
        ],
        out_shape=[
            jax.ShapeDtypeStruct((heads, 3, steps * q_rows), F32),
            jax.ShapeDtypeStruct((NZX, rows, width), BF16),
        ],
        compiler_params=params,
        name="attention_stats",
    )(*operands)
    all_stats = spread(stats)
    out_all = exchange(out_terms)
    own_stats = lax.dynamic_index_in_dim(
        all_stats.reshape(NZX, heads, 3, NZX, rows), zx, 3, keepdims=False
    )
    attn_out = pl.pallas_call(
        combine_kernel,
        grid=(heads,),
        in_specs=[
            pl.BlockSpec((NZX, rows, HD), lambda h: (0, 0, h)),
            pl.BlockSpec((NZX, 1, 3, rows), lambda h: (0, h, 0, 0)),
        ],
        out_specs=pl.BlockSpec((rows, HD), lambda h: (0, h)),
        out_shape=jax.ShapeDtypeStruct((rows, width), BF16),
        compiler_params=pltpu.CompilerParams(vmem_limit_bytes=56 * 1024 * 1024),
        name="combine_out",
    )(out_all, own_stats)

    kv_rows = 2 * rows + 2 * text_own
    dq_terms, *kv_terms = pl.pallas_call(
        grads_kernel,
        grid=grid,
        in_specs=in_specs + [pl.BlockSpec((NZX, 1, 3, q_rows), lambda h, i: (0, h, 0, i))],
        out_specs=[pl.BlockSpec((half, rows, HD), lambda h, i: (i, 0, h))]
        + [pl.BlockSpec((kv_rows, HD), lambda h, i: (0, h))] * NY,
        out_shape=[jax.ShapeDtypeStruct((NZX, rows, width), BF16)]
        + [jax.ShapeDtypeStruct((kv_rows, width), BF16)] * NY,
        scratch_shapes=[pltpu.VMEM((2, NY * rows + text_per, HD), F32)],
        compiler_params=params,
        name="attention_grads",
    )(*operands, all_stats)

    kv_sum = kv_terms[0].astype(F32)
    for by in range(1, NY):
        kv_sum += shift(kv_terms[by], NY - by).astype(F32)
    dq = jnp.sum(exchange(dq_terms).astype(F32), axis=0).astype(BF16)
    kv = kv_sum[: 2 * rows].astype(BF16).reshape(2, rows, width)
    text_sum = kv_sum[2 * rows :].reshape(2, text_own, 1, width)
    grad_projected = jnp.concatenate([dq[None], kv])

    own = part // NZX

    def weight_grad(xs, gs):
        count = gs[0].shape[0]
        terms = pl.pallas_call(
            weights_kernel,
            grid=(count,),
            in_specs=[pl.BlockSpec((rows, part), lambda c: (0, 0))] * NY
            + [pl.BlockSpec((1, rows, width), lambda c: (c, 0, 0))] * NY,
            out_specs=pl.BlockSpec((NZX, 1, own, width), lambda c: (0, c, 0, 0)),
            out_shape=jax.ShapeDtypeStruct((NZX, count, own, width), BF16),
            compiler_params=pltpu.CompilerParams(vmem_limit_bytes=56 * 1024 * 1024),
            name="weight_grads",
        )(*xs, *gs)
        return jnp.sum(exchange(terms).astype(F32), axis=0)

    out_sum = weight_grad(x_grad, around(attn_out[None]))
    qkv_sum = weight_grad(x_in, around(grad_projected))

    terms = jnp.einsum(
        "cvh,sdch->svd",
        grad_projected,
        qkv_weight.reshape(4, part, 3, width),
        preferred_element_type=F32,
    ).astype(BF16)
    keep = [jnp.where(core == 0, terms[2 * z], terms[2 * z + 1]) for z in range(2)]
    give = [jnp.where(core == 0, terms[2 * z + 1], terms[2 * z]) for z in range(2)]
    pair = [
        keep[z].astype(F32) + lax.ppermute(give[z], "head", core_swap).astype(F32)
        for z in range(2)
    ]
    mine = jnp.where(z_hi == 0, pair[0], pair[1])
    other = jnp.where(z_hi == 0, pair[1], pair[0]).astype(BF16)
    grad_inputs = (mine + lax.ppermute(other, "head", z_swap).astype(F32)).astype(BF16)

    return (
        grad_inputs[:, None],
        jnp.transpose(qkv_sum, (1, 0, 2)),
        out_sum[0],
        text_sum[0],
        text_sum[1],
    )


def solution(mesh):
    return jax.shard_map(
        per_device,
        mesh=mesh,
        in_specs=(
            P("blk", None, "head"),
            P("blk", None, "head"),
            P(None, None, "head"),
            P(None, "head"),
            P(None, None, "head"),
            P(None, None, "head"),
            P(),
        ),
        out_specs=(
            P("blk", None, "head"),
            P("blk", None, "head"),
            P("blk", "head"),
            P("blk", None, "head"),
            P("blk", None, "head"),
        ),
        check_vma=False,
    )
```

time: 985 us -> 256 us (0.26)
  waiting for transfers between devices: 755 us -> 98.6 us
  local copies, waits for them, and re-layouts: 123 us -> 10.5 us
  starting transfers between devices: 0.24 us -> 58.6 us
  matrix products: 60.4 us -> 14 us
  Pallas kernels: 0 us -> 38.4 us
  blocking collectives: 0 us -> 18.6 us
  between operations: 15.8 us -> 1.07 us
  other arithmetic: 27.9 us -> 15.2 us
    unnamed x7 -> x0, waiting for transfers between devices: 343 us -> none
    reduce_scatter x2 -> x0, waiting for transfers between devices: 222 us -> none  [the longest x1 172 us: per_device(): lax.psum_scatter(key_terms.astype(jnp.bfloat16), 'blk', scatter_dimension...]
    all_gather x3 -> x0, waiting for transfers between devices: 191 us -> none  [the longest x1 149 us: per_device(): kv_piece = lax.all_gather(kv_local, 'blk', axis=0, tiled=True)]
    ppermute x0 -> x27, waiting for transfers between devices: none -> 84.5 us  [the longest x18 58.8 us: shift(): lax.ppermute(array, 'blk', [(i, (i + by * NZX) % (NY * NZX)) for i in ran...]
    dot_general x53 -> x5, matrix products: 60.4 us -> 14 us  [the longest x1 5.49 us: per_device(): jnp.einsum('cvh,sdch->svd', grad_projected, qkv_weight.reshape(4, part, 3...]
    convert_element_type x4 -> x0, local copies, waits for them, and re-layouts: 39.4 us -> none  [the longest x2 38.4 us: per_device(): key_terms.astype(jnp.bfloat16)]
    pallas_call x0 -> x5, Pallas kernels: none -> 38.4 us  [the longest x1 14.9 us: per_device(): pl.pallas_call(grads_kernel, grid=grid, in_specs=in_specs + [pl.BlockSpec...]
    ppermute x0 -> x27, starting transfers between devices: none -> 36.4 us  [the longest x18 20.5 us: shift(): lax.ppermute(array, 'blk', [(i, (i + by * NZX) % (NY * NZX)) for i in ran...]
  transfers between devices with their start and end apart: 6 -> 32, of which waited for: 6 -> 16; matrix products, arithmetic and copies ran while one was open for 3% -> 11% of each run, Pallas kernels for 0% -> 11%
where the time goes in v1:
time: 256 us; the launch traced here: 255 us
  waiting for transfers between devices  98.6 us (39%)
  starting transfers between devices  58.6 us (23%)
  Pallas kernels  38.4 us (15%)
  blocking collectives  18.6 us (7%)
  other arithmetic  15.2 us (6%)
  matrix products  14 us (5%)
  local copies, waits for them, and re-layouts  10.5 us (4%)
    ppermute x18, waiting for transfers between devices, shift(): lax.ppermute(array, 'blk', [(i, (i + by * NZX) % (NY * NZX)) for i in ran...  58.8 us
    all_to_all x5, starting transfers between devices, exchange(): lax.all_to_all(array, 'blk', 0, 0, tiled=True, axis_index_groups=along_zx)  22.2 us
    ppermute x18, starting transfers between devices, shift(): lax.ppermute(array, 'blk', [(i, (i + by * NZX) % (NY * NZX)) for i in ran...  20.5 us
    all_to_all x1, blocking collectives, exchange(): lax.all_to_all(array, 'blk', 0, 0, tiled=True, axis_index_groups=along_zx)  18.6 us
    pallas_call x1, Pallas kernels, per_device(): pl.pallas_call(grads_kernel, grid=grid, in_specs=in_specs + [pl.BlockSpec...  14.9 us
    all_to_all x5, waiting for transfers between devices, exchange(): lax.all_to_all(array, 'blk', 0, 0, tiled=True, axis_index_groups=along_zx)  14.1 us
    ppermute x1, waiting for transfers between devices, per_device(): lax.ppermute(other, 'head', z_swap).astype(F32)  13.9 us
    pallas_call x1, Pallas kernels, per_device(): pl.pallas_call(stats_kernel, grid=grid, in_specs=in_specs, out_specs=[pl....  11 us
  transfers between devices with their start and end apart: 32, of which 16 were waited for; matrix products, arithmetic and copies ran while one was open for 11% of the time, Pallas kernels for 11%

profile of v1, /device:TPU:1, one launch (start us, length us, event | category | flops | bytes accessed | tf_op | source)
XLA Modules:
  0.0 255.0 jit_solution(3611133761129405995)
XLA Ops:
  0.6 4.5 %collective-permute-start.1 = (bf16[192,768]{1,0:T(8,128)(2,1)}, bf16[192,768]{1,0:T(8,128)(2,1)S(1)}, u32[]{:S(2)}, u32[]{:S(2)}) collective-permute-start(bf16[192,768]{1,0:T(8,128)(2,1)} %bitcast.89), channel_id=1, source_target_pairs={{0,64},{32,96},{64,0},{96,32},{1,65},{33,97},{65,1},{97,33},{2,66}... | collective-permute-start | bytes 884744 | tf_op jit(solution)/shard_map/ppermute | solution.py:157
  6.2 5.9 %collective-permute-done.1 = bf16[192,768]{1,0:T(8,128)(2,1)S(1)} collective-permute-done((bf16[192,768]{1,0:T(8,128)(2,1)}, bf16[192,768]{1,0:T(8,128)(2,1)S(1)}, u32[]{:S(2)}, u32[]{:S(2)}) %collective-permute-start.1) | collective-permute-done | bytes 294944 | tf_op jit(solution)/shard_map/ppermute | solution.py:157
  12.1 2.1 collective-permute-start.2
  14.2 4.3 %collective-permute-done.4 = bf16[192,768]{1,0:T(8,128)(2,1)S(1)} collective-permute-done((bf16[192,768]{1,0:T(8,128)(2,1)}, bf16[192,768]{1,0:T(8,128)(2,1)S(1)}, u32[]{:S(2)}, u32[]{:S(2)}) %collective-permute-start.4) | collective-permute-done | bytes 294944 | tf_op jit(solution)/shard_map/ppermute | solution.py:157
  19.7 2.0 select_select_fusion.4
  21.7 5.2 %fusion.1 = bf16[3,192,384]{2,1,0:T(8,128)(2,1)S(1)} fusion(bf16[3072,3,384]{2,0,1:T(8,128)(2,1)} %param.9, bf16[192,768]{1,0:T(8,128)(2,1)S(1)} %get-tuple-element.43, bf16[192,768]{1,0:T(8,128)(2,1)S(1)} %get-tuple-element.42, bf16[192,768]{1,0:T(8,128)(2,1)S(1)} %get-tuple-element.41, bf16[192,768]{1,0:T(8,128)(2,1)S(1)} %get-tuple-element.40), kind=kOutput, calls=%fused_computation.4 | convolution fusion | flops 1363894272 | bytes 8699904 | tf_op jit(solution)/shard_map/vd,dch->cvh/dot_general | solution.py:181
  28.9 1.8 broadcast_in_dim.39
  30.7 4.9 %all-to-all-start = ((bf16[8,2,192,384]{3,2,1,0:T(8,128)(2,1)}), bf16[8,2,192,384]{3,2,1,0:T(8,128)(2,1)}, u32[]{:S(2)}, u32[]{:S(2)}) async-start(bf16[8,2,192,384]{3,2,1,0:T(8,128)(2,1)} %broadcast_in_dim.39), calls=%async_computation | async-start | bytes 4718592 | tf_op jit(solution)/shard_map/all_to_all | solution.py:143
  36.5 1.4 collective-permute-start.6
  37.8 2.6 %collective-permute-start.7 = (bf16[2,192,384]{2,1,0:T(8,128)(2,1)S(1)}, bf16[2,192,384]{2,1,0:T(8,128)(2,1)S(1)}, u32[]{:S(2)}, u32[]{:S(2)}) collective-permute-start(bf16[2,192,384]{2,1,0:T(8,128)(2,1)S(1)} %slice.47.refs_0_.refs_4_), channel_id=1, source_target_pairs={{0,16},{1,17},{2,18},{3,19},{4,20},{5,21},{6,22},{7,23},{8,24},{9,... | collective-permute-start | bytes 884744 | tf_op jit(solution)/shard_map/ppermute | solution.py:149
  41.7 1.8 convolution_convert_fusion.2.refs_8_
  43.5 2.8 %collective-permute-done.6.refs_1_.refs_5_ = bf16[2,192,384]{2,1,0:T(8,128)(2,1)S(1)} collective-permute-done((bf16[2,192,384]{2,1,0:T(8,128)(2,1)S(1)}, bf16[2,192,384]{2,1,0:T(8,128)(2,1)S(1)}, u32[]{:S(2)}, u32[]{:S(2)}) %collective-permute-start.6) | collective-permute-done | bytes 294944 | tf_op jit(solution)/shard_map/ppermute | solution.py:149
  46.3 7.4 %collective-permute-done.7.refs_2_.refs_6_ = bf16[2,192,384]{2,1,0:T(8,128)(2,1)S(1)} collective-permute-done((bf16[2,192,384]{2,1,0:T(8,128)(2,1)S(1)}, bf16[2,192,384]{2,1,0:T(8,128)(2,1)S(1)}, u32[]{:S(2)}, u32[]{:S(2)}) %collective-permute-start.7) | collective-permute-done | bytes 294944 | tf_op jit(solution)/shard_map/ppermute | solution.py:149
  53.7 11.9 %all-to-all-done.q_ref.g_ref = bf16[8,2,192,384]{3,2,1,0:T(8,128)(2,1)} async-done(((bf16[8,2,192,384]{3,2,1,0:T(8,128)(2,1)}), bf16[8,2,192,384]{3,2,1,0:T(8,128)(2,1)}, u32[]{:S(2)}, u32[]{:S(2)}) %all-to-all-start) | async-done | bytes 2359328 | tf_op jit(solution)/shard_map/all_to_all | solution.py:143
  66.3 11.0 %attention_stats.1 = (f32[3,3,1536]{2,1,0:T(4,128)}, bf16[8,192,384]{2,1,0:T(8,128)(2,1)}) custom-call(bf16[8,2,192,384]{3,2,1,0:T(8,128)(2,1)} %all-to-all-done.q_ref.g_ref, bf16[8,2,192,384]{3,2,1,0:T(8,128)(2,1)} %all-to-all-done.q_ref.g_ref, bf16[2,192,384]{2,1,0:T(8,128)(2,1)} %copy-done.1, bf16[2,192,384]{2,1,0:T(8,128)(2,1)} %copy-done.4, ...), custom_call_target="tpu_custom_call" | custom-call | tf_op jit(solution)/shard_map/attention_stats/pallas_call | solution.py:228
  78.3 18.6 %all_to_all.30.refs_11_ = f32[8,3,3,1536]{3,2,1,0:T(4,128)} all-to-all(f32[8,3,3,1536]{3,2,1,0:T(4,128)S(1)} %broadcast_in_dim.43), channel_id=1, replica_groups={{0,1,2,3,4,5,6,7},{8,9,10,11,12,13,14,15},{16,17,18,19,20,21,22,23},{24..., dimensions={0} | all-to-all | bytes 884736 | tf_op jit(solution)/shard_map/all_to_all | solution.py:143
  96.9 3.6 %all-to-all-start.4 = ((bf16[8,192,384]{2,1,0:T(8,128)(2,1)}), bf16[8,192,384]{2,1,0:T(8,128)(2,1)S(1)}, u32[]{:S(2)}, u32[]{:S(2)}) async-start(bf16[8,192,384]{2,1,0:T(8,128)(2,1)} %get-tuple-element.18), calls=%async_computation.4 | async-start | bytes 2359296 | tf_op jit(solution)/shard_map/all_to_all | solution.py:143
  100.5 14.9 %attention_grads.1 = (bf16[8,192,384]{2,1,0:T(8,128)(2,1)}, bf16[400,384]{1,0:T(8,128)(2,1)}, bf16[400,384]{1,0:T(8,128)(2,1)}, bf16[400,384]{1,0:T(8,128)(2,1)}, bf16[400,384]{1,0:T(8,128)(2,1)}) custom-call(bf16[8,2,192,384]{3,2,1,0:T(8,128)(2,1)} %all-to-all-done.q_ref.g_ref, bf16[8,2,192,384]{3,2,1,0:T(8,128)(2,1)} %all-to-all-done.q_ref.g_ref, ...), custom_call_target="tpu_custom_call" | custom-call | tf_op jit(solution)/shard_map/attention_grads/pallas_call | solution.py:262
  115.4 2.2 all-to-all-done.4.out_ref
  118.6 4.3 %all-to-all-start.2 = ((bf16[8,192,384]{2,1,0:T(8,128)(2,1)}), bf16[8,192,384]{2,1,0:T(8,128)(2,1)}, u32[]{:S(2)}, u32[]{:S(2)}) async-start(bf16[8,192,384]{2,1,0:T(8,128)(2,1)} %get-tuple-element.13), calls=%async_computation.2 | async-start | bytes 2359296 | tf_op jit(solution)/shard_map/all_to_all | solution.py:143
  122.9 2.4 select_select_fusion.1
  125.3 1.3 collective-permute-start.21
  126.6 2.6 %collective-permute-start.22 = (bf16[192,768]{1,0:T(8,128)(2,1)}, bf16[192,768]{1,0:T(8,128)(2,1)}, u32[]{:S(2)}, u32[]{:S(2)}) collective-permute-start(bf16[192,768]{1,0:T(8,128)(2,1)} %get-tuple-element.44), channel_id=1, source_target_pairs={{0,16},{1,17},{2,18},{3,19},{4,20},{5,21},{6,22},{7,23},{8,24},{9,... | collective-permute-start | bytes 884744 | tf_op jit(solution)/shard_map/ppermute | solution.py:149
  130.9 1.4 collective-permute-start.9
  132.3 2.3 select_select_fusion.5
  136.1 3.4 %combine_out.1 = bf16[192,384]{1,0:T(8,128)(2,1)} custom-call(bf16[8,192,384]{2,1,0:T(8,128)(2,1)} %copy-done.3, f32[8,3,3,192]{3,2,1,0:T(4,128)} %bitcast.88), custom_call_target="tpu_custom_call" | custom-call | tf_op jit(solution)/shard_map/combine_out/pallas_call | solution.py:248
  139.5 1.9 collective-permute-done.22.refs_2_
  141.4 6.6 %collective-permute-done.10 = bf16[400,384]{1,0:T(8,128)(2,1)} collective-permute-done((bf16[400,384]{1,0:T(8,128)(2,1)}, bf16[400,384]{1,0:T(8,128)(2,1)}, u32[]{:S(2)}, u32[]{:S(2)}) %collective-permute-start.10) | collective-permute-done | bytes 307232 | tf_op jit(solution)/shard_map/ppermute | solution.py:149
  148.0 5.4 %collective-permute-done.11 = bf16[400,384]{1,0:T(8,128)(2,1)} collective-permute-done((bf16[400,384]{1,0:T(8,128)(2,1)}, bf16[400,384]{1,0:T(8,128)(2,1)}, u32[]{:S(2)}, u32[]{:S(2)}) %collective-permute-start.11) | collective-permute-done | bytes 307232 | tf_op jit(solution)/shard_map/ppermute | solution.py:149
  153.4 1.6 collective-permute-start.25
  155.8 1.4 convert_add_fusion
  158.1 2.7 %collective-permute-done.24.refs_5_ = bf16[1,192,384]{2,1,0:T(8,128)(2,1)S(1)} collective-permute-done((bf16[1,192,384]{2,1,0:T(8,128)(2,1)}, bf16[1,192,384]{2,1,0:T(8,128)(2,1)S(1)}, u32[]{:S(2)}, u32[]{:S(2)}) %collective-permute-start.24) | collective-permute-done | bytes 147488 | tf_op jit(solution)/shard_map/ppermute | solution.py:149
  160.8 3.8 %collective-permute-done.25.refs_6_ = bf16[1,192,384]{2,1,0:T(8,128)(2,1)S(1)} collective-permute-done((bf16[1,192,384]{2,1,0:T(8,128)(2,1)}, bf16[1,192,384]{2,1,0:T(8,128)(2,1)S(1)}, u32[]{:S(2)}, u32[]{:S(2)}) %collective-permute-start.25) | collective-permute-done | bytes 147488 | tf_op jit(solution)/shard_map/ppermute | solution.py:149
  165.3 3.3 %weight_grads.3 = bf16[8,1,96,384]{3,2,1,0:T(8,128)(2,1)} custom-call(bf16[192,768]{1,0:T(8,128)(2,1)} %get-tuple-element.46.refs_0_, bf16[192,768]{1,0:T(8,128)(2,1)} %collective-permute-done.21.refs_1_, bf16[192,768]{1,0:T(8,128)(2,1)} %collective-permute-done.22.refs_2_, bf16[192,768]{1,0:T(8,128)(2,1)} %copy-done.21, bf16[1,192,384]{2,1,0:T(8,128)(2,1)} %bitcast.86, ...), custom_call_target="tpu_custom_call" | custom-call | tf_op jit(solution)/shard_map/weight_grads/pallas_call | solution.py:287
  168.6 4.7 %all-to-all-start.5 = ((bf16[8,1,96,384]{3,2,1,0:T(8,128)(2,1)}), bf16[8,1,96,384]{3,2,1,0:T(8,128)(2,1)S(1)}, u32[]{:S(2)}, u32[]{:S(2)}) async-start(bf16[8,1,96,384]{3,2,1,0:T(8,128)(2,1)} %weight_grads.3), calls=%async_computation.5 | async-start | bytes 1179648 | tf_op jit(solution)/shard_map/all_to_all | solution.py:143
  173.3 1.4 reduce_sum.40
  174.9 1.5 collective-permute-start.19
  176.4 2.0 collective-permute-start.20
  178.4 1.6 collective-permute-start.16
  180.6 17.4 %collective-permute-done.16.refs_2_ = bf16[192,768]{1,0:T(8,128)(2,1)S(1)} collective-permute-done((bf16[192,768]{1,0:T(8,128)(2,1)}, bf16[192,768]{1,0:T(8,128)(2,1)S(1)}, u32[]{:S(2)}, u32[]{:S(2)}) %collective-permute-start.16) | collective-permute-done | bytes 294944 | tf_op jit(solution)/shard_map/ppermute | solution.py:149
  197.9 10.7 %collective-permute-done.17.refs_3_ = bf16[192,768]{1,0:T(8,128)(2,1)S(1)} collective-permute-done((bf16[192,768]{1,0:T(8,128)(2,1)}, bf16[192,768]{1,0:T(8,128)(2,1)S(1)}, u32[]{:S(2)}, u32[]{:S(2)}) %collective-permute-start.17) | collective-permute-done | bytes 294944 | tf_op jit(solution)/shard_map/ppermute | solution.py:149
  209.9 5.8 %weight_grads.2 = bf16[8,3,96,384]{3,2,1,0:T(8,128)(2,1)} custom-call(bf16[192,768]{1,0:T(8,128)(2,1)} %get-tuple-element.49.refs_0_, bf16[192,768]{1,0:T(8,128)(2,1)} %collective-permute-done.15.refs_1_, bf16[192,768]{1,0:T(8,128)(2,1)} %copy-done.22, bf16[192,768]{1,0:T(8,128)(2,1)} %copy-done.23, bf16[3,192,384]{2,1,0:T(8,128)(2,1)} %copy-done.7, ...), custom_call_target="tpu_custom_call" | custom-call | tf_op jit(solution)/shard_map/weight_grads/pallas_call | solution.py:287
  215.7 4.7 %all-to-all-start.3 = ((bf16[8,3,96,384]{3,2,1,0:T(8,128)(2,1)}), bf16[8,3,96,384]{3,2,1,0:T(8,128)(2,1)}, u32[]{:S(2)}, u32[]{:S(2)}) async-start(bf16[8,3,96,384]{3,2,1,0:T(8,128)(2,1)} %weight_grads.2), calls=%async_computation.3 | async-start | bytes 3538944 | tf_op jit(solution)/shard_map/all_to_all | solution.py:143
  220.4 5.5 %fusion = bf16[4,192,768]{2,1,0:T(8,128)(2,1)S(1)} fusion(bf16[4,768,3,384]{3,1,0,2:T(8,128)(2,1)} %bitcast.94, bf16[2,192,384]{2,1,0:T(8,128)(2,1)S(1)} %bitcast.80, bf16[1,192,384]{2,1,0:T(8,128)(2,1)S(1)} %bitcast.82), kind=kOutput, calls=%fused_computation.2 | convolution fusion | flops 1360429056 | bytes 8699904 | tf_op jit(solution)/shard_map/cvh,sdch->svd/dot_general | solution.py:302
  226.0 3.6 %collective-permute-start.12 = (bf16[192,768]{1,0:T(8,128)(2,1)S(1)}, bf16[192,768]{1,0:T(8,128)(2,1)S(1)}, u32[]{:S(2)}, u32[]{:S(2)}) collective-permute-start(bf16[192,768]{1,0:T(8,128)(2,1)S(1)} %get-tuple-element.51), channel_id=1, source_target_pairs={{0,32},{32,0},{64,96},{96,64},{1,33},{33,1},{65,97},{97,65},{2,34}... | collective-permute-start | bytes 884744 | tf_op jit(solution)/shard_map/ppermute | solution.py:311
  231.5 3.4 %collective-permute-start.14 = (bf16[192,768]{1,0:T(8,128)(2,1)S(1)}, bf16[192,768]{1,0:T(8,128)(2,1)S(1)}, u32[]{:S(2)}, u32[]{:S(2)}) collective-permute-start(bf16[192,768]{1,0:T(8,128)(2,1)S(1)} %select_convert_fusion), channel_id=1, source_target_pairs={{0,64},{32,96},{64,0},{96,32},{1,65},{33,97},{65,1},{97,33},{2,66}... | collective-permute-start | bytes 884744 | tf_op jit(solution)/shard_map/ppermute | solution.py:316
  237.6 13.9 %collective-permute-done.14 = bf16[192,768]{1,0:T(8,128)(2,1)S(1)} collective-permute-done((bf16[192,768]{1,0:T(8,128)(2,1)S(1)}, bf16[192,768]{1,0:T(8,128)(2,1)S(1)}, u32[]{:S(2)}, u32[]{:S(2)}) %collective-permute-start.14) | collective-permute-done | bytes 294944 | tf_op jit(solution)/shard_map/ppermute | solution.py:316
  252.5 2.5 convert_reduce_fusion
  (115 shorter events, 22.1 us)
Async XLA Ops:
  0.6 27.2 %copy-start = (bf16[3072,384]{1,0:T(8,128)(2,1)S(1)}, bf16[3072,384]{1,0:T(8,128)(2,1)}, u32[]{:S(2)}) copy-start(bf16[3072,384]{1,0:T(8,128)(2,1)} %param.10) | copy-start | bytes 7077892
  0.6 11.4 %collective-permute-start.1 = (bf16[192,768]{1,0:T(8,128)(2,1)}, bf16[192,768]{1,0:T(8,128)(2,1)S(1)}, u32[]{:S(2)}, u32[]{:S(2)}) collective-permute-start(bf16[192,768]{1,0:T(8,128)(2,1)} %bitcast.89), channel_id=1, source_target_pairs={{0,64},{32,96},{64,0},{96,32},{1,65},{33,97},{65,1},{97,33},{2,66}... | collective-permute-start | bytes 884744 | tf_op jit(solution)/shard_map/ppermute | solution.py:157
  5.2 13.3 %collective-permute-start.4 = (bf16[192,768]{1,0:T(8,128)(2,1)}, bf16[192,768]{1,0:T(8,128)(2,1)S(1)}, u32[]{:S(2)}, u32[]{:S(2)}) collective-permute-start(bf16[192,768]{1,0:T(8,128)(2,1)} %bitcast.91), channel_id=1, source_target_pairs={{0,64},{32,96},{64,0},{96,32},{1,65},{33,97},{65,1},{97,33},{2,66}... | collective-permute-start | bytes 884744 | tf_op jit(solution)/shard_map/ppermute | solution.py:157
  5.2 14.4 %collective-permute-start = (bf16[192,768]{1,0:T(8,128)(2,1)}, bf16[192,768]{1,0:T(8,128)(2,1)}, u32[]{:S(2)}, u32[]{:S(2)}) collective-permute-start(bf16[192,768]{1,0:T(8,128)(2,1)} %bitcast.90), channel_id=1, source_target_pairs={{0,32},{32,0},{64,96},{96,64},{1,33},{33,1},{65,97},{97,65},{2,34}... | collective-permute-start | bytes 884744 | tf_op jit(solution)/shard_map/ppermute | solution.py:158
  12.1 7.6 %collective-permute-start.2 = (bf16[192,768]{1,0:T(8,128)(2,1)S(1)}, bf16[192,768]{1,0:T(8,128)(2,1)}, u32[]{:S(2)}, u32[]{:S(2)}) collective-permute-start(bf16[192,768]{1,0:T(8,128)(2,1)S(1)} %collective-permute-done.1), channel_id=1, source_target_pairs={{0,32},{32,0},{64,96},{96,64},{1,33},{33,1},{65,97},{97,65},{2,34}... | collective-permute-start | bytes 884744 | tf_op jit(solution)/shard_map/ppermute | solution.py:159
  14.2 12.8 %collective-permute-start.3 = (bf16[192,768]{1,0:T(8,128)(2,1)}, bf16[192,768]{1,0:T(8,128)(2,1)S(1)}, u32[]{:S(2)}, u32[]{:S(2)}) collective-permute-start(bf16[192,768]{1,0:T(8,128)(2,1)} %bitcast.92), channel_id=1, source_target_pairs={{0,32},{32,0},{64,96},{96,64},{1,33},{33,1},{65,97},{97,65},{2,34}... | collective-permute-start | bytes 884744 | tf_op jit(solution)/shard_map/ppermute | solution.py:158
  18.4 8.5 %collective-permute-start.5 = (bf16[192,768]{1,0:T(8,128)(2,1)S(1)}, bf16[192,768]{1,0:T(8,128)(2,1)S(1)}, u32[]{:S(2)}, u32[]{:S(2)}) collective-permute-start(bf16[192,768]{1,0:T(8,128)(2,1)S(1)} %collective-permute-done.4), channel_id=1, source_target_pairs={{0,32},{32,0},{64,96},{96,64},{1,33},{33,1},{65,97},{97,65},{2,34}... | collective-permute-start | bytes 884744 | tf_op jit(solution)/shard_map/ppermute | solution.py:159
  21.6 5.2 %copy-start.9 = (bf16[192,768]{1,0:T(8,128)(2,1)}, bf16[192,768]{1,0:T(8,128)(2,1)S(1)}, u32[]{:S(2)}) copy-start(bf16[192,768]{1,0:T(8,128)(2,1)S(1)} %get-tuple-element.40) | copy-start | bytes 884740
  21.7 5.2 %copy-start.10 = (bf16[192,768]{1,0:T(8,128)(2,1)}, bf16[192,768]{1,0:T(8,128)(2,1)S(1)}, u32[]{:S(2)}) copy-start(bf16[192,768]{1,0:T(8,128)(2,1)S(1)} %get-tuple-element.41) | copy-start | bytes 884740
  21.7 5.2 %copy-start.11 = (bf16[192,768]{1,0:T(8,128)(2,1)}, bf16[192,768]{1,0:T(8,128)(2,1)S(1)}, u32[]{:S(2)}) copy-start(bf16[192,768]{1,0:T(8,128)(2,1)S(1)} %get-tuple-element.42) | copy-start | bytes 884740
  21.7 5.2 %copy-start.12 = (bf16[192,768]{1,0:T(8,128)(2,1)}, bf16[192,768]{1,0:T(8,128)(2,1)S(1)}, u32[]{:S(2)}) copy-start(bf16[192,768]{1,0:T(8,128)(2,1)S(1)} %get-tuple-element.43) | copy-start | bytes 884740
  21.7 5.3 %copy-start.20 = (bf16[192,1,768]{2,0,1:T(8,128)(2,1)S(1)}, bf16[192,1,768]{2,0,1:T(8,128)(2,1)}, u32[]{:S(2)}) copy-start(bf16[192,1,768]{2,0,1:T(8,128)(2,1)} %param.8) | copy-start | bytes 884740
  30.7 4.9 %copy-start.28 = (bf16[256,1,384]{2,0,1:T(8,128)(2,1)S(1)}, bf16[256,1,384]{2,0,1:T(8,128)(2,1)}, u32[]{:S(2)}) copy-start(bf16[256,1,384]{2,0,1:T(8,128)(2,1)} %param.12) | copy-start | bytes 589828
  30.7 10.8 %copy-start.27 = (s32[256,1]{0,1:T(1,128)S(1)}, s32[256,1]{0,1:T(1,128)}, u32[]{:S(2)}) copy-start(s32[256,1]{0,1:T(1,128)} %param.13) | copy-start | bytes 3076
  30.7 34.9 %all-to-all-start = ((bf16[8,2,192,384]{3,2,1,0:T(8,128)(2,1)}), bf16[8,2,192,384]{3,2,1,0:T(8,128)(2,1)}, u32[]{:S(2)}, u32[]{:S(2)}) async-start(bf16[8,2,192,384]{3,2,1,0:T(8,128)(2,1)} %broadcast_in_dim.39), calls=%async_computation | async-start | bytes 4718592 | tf_op jit(solution)/shard_map/all_to_all | solution.py:143
  36.5 29.8 %copy-start.1 = (bf16[2,192,384]{2,1,0:T(8,128)(2,1)}, bf16[2,192,384]{2,1,0:T(8,128)(2,1)S(1)}, u32[]{:S(2)}) copy-start(bf16[2,192,384]{2,1,0:T(8,128)(2,1)S(1)} %slice.47.refs_0_.refs_4_) | copy-start | bytes 884740
  36.5 9.8 %collective-permute-start.6 = (bf16[2,192,384]{2,1,0:T(8,128)(2,1)S(1)}, bf16[2,192,384]{2,1,0:T(8,128)(2,1)S(1)}, u32[]{:S(2)}, u32[]{:S(2)}) collective-permute-start(bf16[2,192,384]{2,1,0:T(8,128)(2,1)S(1)} %slice.47.refs_0_.refs_4_), channel_id=1, source_target_pairs={{0,8},{1,9},{2,10},{3,11},{4,12},{5,13},{6,14},{7,15},{8,16},{9,17... | collective-permute-start | bytes 884744 | tf_op jit(solution)/shard_map/ppermute | solution.py:149
  37.8 15.9 %collective-permute-start.7 = (bf16[2,192,384]{2,1,0:T(8,128)(2,1)S(1)}, bf16[2,192,384]{2,1,0:T(8,128)(2,1)S(1)}, u32[]{:S(2)}, u32[]{:S(2)}) collective-permute-start(bf16[2,192,384]{2,1,0:T(8,128)(2,1)S(1)} %slice.47.refs_0_.refs_4_), channel_id=1, source_target_pairs={{0,16},{1,17},{2,18},{3,19},{4,20},{5,21},{6,22},{7,23},{8,24},{9,... | collective-permute-start | bytes 884744 | tf_op jit(solution)/shard_map/ppermute | solution.py:149
  40.5 13.3 %collective-permute-start.8 = (bf16[2,192,384]{2,1,0:T(8,128)(2,1)S(1)}, bf16[2,192,384]{2,1,0:T(8,128)(2,1)S(1)}, u32[]{:S(2)}, u32[]{:S(2)}) collective-permute-start(bf16[2,192,384]{2,1,0:T(8,128)(2,1)S(1)} %slice.47.refs_0_.refs_4_), channel_id=1, source_target_pairs={{0,24},{1,25},{2,26},{3,27},{4,28},{5,29},{6,30},{7,31},{8,0},{9,1... | collective-permute-start | bytes 884744 | tf_op jit(solution)/shard_map/ppermute | solution.py:149
  46.3 20.0 %copy-start.4 = (bf16[2,192,384]{2,1,0:T(8,128)(2,1)}, bf16[2,192,384]{2,1,0:T(8,128)(2,1)S(1)}, u32[]{:S(2)}) copy-start(bf16[2,192,384]{2,1,0:T(8,128)(2,1)S(1)} %collective-permute-done.6.refs_1_.refs_5_) | copy-start | bytes 884740
  53.7 12.6 %copy-start.5 = (bf16[2,192,384]{2,1,0:T(8,128)(2,1)}, bf16[2,192,384]{2,1,0:T(8,128)(2,1)S(1)}, u32[]{:S(2)}) copy-start(bf16[2,192,384]{2,1,0:T(8,128)(2,1)S(1)} %collective-permute-done.7.refs_2_.refs_6_) | copy-start | bytes 884740
  53.7 12.6 %copy-start.6 = (bf16[2,192,384]{2,1,0:T(8,128)(2,1)}, bf16[2,192,384]{2,1,0:T(8,128)(2,1)S(1)}, u32[]{:S(2)}) copy-start(bf16[2,192,384]{2,1,0:T(8,128)(2,1)S(1)} %collective-permute-done.8.refs_3_.refs_7_) | copy-start | bytes 884740
  96.9 20.7 %all-to-all-start.4 = ((bf16[8,192,384]{2,1,0:T(8,128)(2,1)}), bf16[8,192,384]{2,1,0:T(8,128)(2,1)S(1)}, u32[]{:S(2)}, u32[]{:S(2)}) async-start(bf16[8,192,384]{2,1,0:T(8,128)(2,1)} %get-tuple-element.18), calls=%async_computation.4 | async-start | bytes 2359296 | tf_op jit(solution)/shard_map/all_to_all | solution.py:143
  118.6 49.9 %all-to-all-start.2 = ((bf16[8,192,384]{2,1,0:T(8,128)(2,1)}), bf16[8,192,384]{2,1,0:T(8,128)(2,1)}, u32[]{:S(2)}, u32[]{:S(2)}) async-start(bf16[8,192,384]{2,1,0:T(8,128)(2,1)} %get-tuple-element.13), calls=%async_computation.2 | async-start | bytes 2359296 | tf_op jit(solution)/shard_map/all_to_all | solution.py:143
  122.9 11.8 %copy-start.2 = (f32[8,3,3,1536]{3,2,1,0:T(4,128)S(1)}, f32[8,3,3,1536]{3,2,1,0:T(4,128)}, u32[]{:S(2)}) copy-start(f32[8,3,3,1536]{3,2,1,0:T(4,128)} %all_to_all.30.refs_11_) | copy-start | bytes 1327108
  125.3 9.7 %collective-permute-start.21 = (bf16[192,768]{1,0:T(8,128)(2,1)}, bf16[192,768]{1,0:T(8,128)(2,1)}, u32[]{:S(2)}, u32[]{:S(2)}) collective-permute-start(bf16[192,768]{1,0:T(8,128)(2,1)} %get-tuple-element.45), channel_id=1, source_target_pairs={{0,8},{1,9},{2,10},{3,11},{4,12},{5,13},{6,14},{7,15},{8,16},{9,17... | collective-permute-start | bytes 884744 | tf_op jit(solution)/shard_map/ppermute | solution.py:149
  126.6 14.8 %collective-permute-start.22 = (bf16[192,768]{1,0:T(8,128)(2,1)}, bf16[192,768]{1,0:T(8,128)(2,1)}, u32[]{:S(2)}, u32[]{:S(2)}) collective-permute-start(bf16[192,768]{1,0:T(8,128)(2,1)} %get-tuple-element.44), channel_id=1, source_target_pairs={{0,16},{1,17},{2,18},{3,19},{4,20},{5,21},{6,22},{7,23},{8,24},{9,... | collective-permute-start | bytes 884744 | tf_op jit(solution)/shard_map/ppermute | solution.py:149
  129.3 18.7 %collective-permute-start.10 = (bf16[400,384]{1,0:T(8,128)(2,1)}, bf16[400,384]{1,0:T(8,128)(2,1)}, u32[]{:S(2)}, u32[]{:S(2)}) collective-permute-start(bf16[400,384]{1,0:T(8,128)(2,1)} %get-tuple-element.16), channel_id=1, source_target_pairs={{0,16},{1,17},{2,18},{3,19},{4,20},{5,21},{6,22},{7,23},{8,24},{9,... | collective-permute-start | bytes 921608 | tf_op jit(solution)/shard_map/ppermute | solution.py:149
  129.6 23.8 %collective-permute-start.11 = (bf16[400,384]{1,0:T(8,128)(2,1)}, bf16[400,384]{1,0:T(8,128)(2,1)}, u32[]{:S(2)}, u32[]{:S(2)}) collective-permute-start(bf16[400,384]{1,0:T(8,128)(2,1)} %get-tuple-element.17), channel_id=1, source_target_pairs={{0,8},{1,9},{2,10},{3,11},{4,12},{5,13},{6,14},{7,15},{8,16},{9,17... | collective-permute-start | bytes 921608 | tf_op jit(solution)/shard_map/ppermute | solution.py:149
  130.9 24.1 %collective-permute-start.9 = (bf16[400,384]{1,0:T(8,128)(2,1)}, bf16[400,384]{1,0:T(8,128)(2,1)}, u32[]{:S(2)}, u32[]{:S(2)}) collective-permute-start(bf16[400,384]{1,0:T(8,128)(2,1)} %get-tuple-element.15), channel_id=1, source_target_pairs={{0,24},{1,25},{2,26},{3,27},{4,28},{5,29},{6,30},{7,31},{8,0},{9,1... | collective-permute-start | bytes 921608 | tf_op jit(solution)/shard_map/ppermute | solution.py:149
  135.0 23.1 %collective-permute-start.23 = (bf16[192,768]{1,0:T(8,128)(2,1)}, bf16[192,768]{1,0:T(8,128)(2,1)S(1)}, u32[]{:S(2)}, u32[]{:S(2)}) collective-permute-start(bf16[192,768]{1,0:T(8,128)(2,1)} %get-tuple-element.34), channel_id=1, source_target_pairs={{0,24},{1,25},{2,26},{3,27},{4,28},{5,29},{6,30},{7,31},{8,0},{9,1... | collective-permute-start | bytes 884744 | tf_op jit(solution)/shard_map/ppermute | solution.py:149
  141.4 38.5 %collective-permute-start.15 = (bf16[192,768]{1,0:T(8,128)(2,1)}, bf16[192,768]{1,0:T(8,128)(2,1)}, u32[]{:S(2)}, u32[]{:S(2)}) collective-permute-start(bf16[192,768]{1,0:T(8,128)(2,1)} %get-tuple-element.48), channel_id=1, source_target_pairs={{0,8},{1,9},{2,10},{3,11},{4,12},{5,13},{6,14},{7,15},{8,16},{9,17... | collective-permute-start | bytes 884744 | tf_op jit(solution)/shard_map/ppermute | solution.py:149
  148.0 12.9 %collective-permute-start.24 = (bf16[1,192,384]{2,1,0:T(8,128)(2,1)}, bf16[1,192,384]{2,1,0:T(8,128)(2,1)S(1)}, u32[]{:S(2)}, u32[]{:S(2)}) collective-permute-start(bf16[1,192,384]{2,1,0:T(8,128)(2,1)} %bitcast.83), channel_id=1, source_target_pairs={{0,8},{1,9},{2,10},{3,11},{4,12},{5,13},{6,14},{7,15},{8,16},{9,17... | collective-permute-start | bytes 442376 | tf_op jit(solution)/shard_map/ppermute | solution.py:149
  153.4 11.2 %collective-permute-start.25 = (bf16[1,192,384]{2,1,0:T(8,128)(2,1)}, bf16[1,192,384]{2,1,0:T(8,128)(2,1)S(1)}, u32[]{:S(2)}, u32[]{:S(2)}) collective-permute-start(bf16[1,192,384]{2,1,0:T(8,128)(2,1)} %bitcast.84), channel_id=1, source_target_pairs={{0,16},{1,17},{2,18},{3,19},{4,20},{5,21},{6,22},{7,23},{8,24},{9,... | collective-permute-start | bytes 442376 | tf_op jit(solution)/shard_map/ppermute | solution.py:149
  155.0 9.6 %collective-permute-start.26 = (bf16[1,192,384]{2,1,0:T(8,128)(2,1)}, bf16[1,192,384]{2,1,0:T(8,128)(2,1)S(1)}, u32[]{:S(2)}, u32[]{:S(2)}) collective-permute-start(bf16[1,192,384]{2,1,0:T(8,128)(2,1)} %bitcast.85), channel_id=1, source_target_pairs={{0,24},{1,25},{2,26},{3,27},{4,28},{5,29},{6,30},{7,31},{8,0},{9,1... | collective-permute-start | bytes 442376 | tf_op jit(solution)/shard_map/ppermute | solution.py:149
  158.1 6.5 %copy-start.21 = (bf16[192,768]{1,0:T(8,128)(2,1)}, bf16[192,768]{1,0:T(8,128)(2,1)S(1)}, u32[]{:S(2)}) copy-start(bf16[192,768]{1,0:T(8,128)(2,1)S(1)} %collective-permute-done.23.refs_3_) | copy-start | bytes 884740
  168.6 47.1 %all-to-all-start.5 = ((bf16[8,1,96,384]{3,2,1,0:T(8,128)(2,1)}), bf16[8,1,96,384]{3,2,1,0:T(8,128)(2,1)S(1)}, u32[]{:S(2)}, u32[]{:S(2)}) async-start(bf16[8,1,96,384]{3,2,1,0:T(8,128)(2,1)} %weight_grads.3), calls=%async_computation.5 | async-start | bytes 1179648 | tf_op jit(solution)/shard_map/all_to_all | solution.py:143
  174.8 33.9 %copy-start.7 = (bf16[3,192,384]{2,1,0:T(8,128)(2,1)}, bf16[3,192,384]{2,1,0:T(8,128)(2,1)S(1)}, u32[]{:S(2)}) copy-start(bf16[3,192,384]{2,1,0:T(8,128)(2,1)S(1)} %pad_maximum_fusion.refs_4_) | copy-start | bytes 1327108
  174.8 33.8 %collective-permute-start.18 = (bf16[3,192,384]{2,1,0:T(8,128)(2,1)S(1)}, bf16[3,192,384]{2,1,0:T(8,128)(2,1)S(1)}, u32[]{:S(2)}, u32[]{:S(2)}) collective-permute-start(bf16[3,192,384]{2,1,0:T(8,128)(2,1)S(1)} %pad_maximum_fusion.refs_4_), channel_id=1, source_target_pairs={{0,8},{1,9},{2,10},{3,11},{4,12},{5,13},{6,14},{7,15},{8,16},{9,17... | collective-permute-start | bytes 1327112 | tf_op jit(solution)/shard_map/ppermute | solution.py:149
  174.9 33.7 %collective-permute-start.19 = (bf16[3,192,384]{2,1,0:T(8,128)(2,1)S(1)}, bf16[3,192,384]{2,1,0:T(8,128)(2,1)S(1)}, u32[]{:S(2)}, u32[]{:S(2)}) collective-permute-start(bf16[3,192,384]{2,1,0:T(8,128)(2,1)S(1)} %pad_maximum_fusion.refs_4_), channel_id=1, source_target_pairs={{0,16},{1,17},{2,18},{3,19},{4,20},{5,21},{6,22},{7,23},{8,24},{9,... | collective-permute-start | bytes 1327112 | tf_op jit(solution)/shard_map/ppermute | solution.py:149
  176.4 32.3 %collective-permute-start.20 = (bf16[3,192,384]{2,1,0:T(8,128)(2,1)S(1)}, bf16[3,192,384]{2,1,0:T(8,128)(2,1)S(1)}, u32[]{:S(2)}, u32[]{:S(2)}) collective-permute-start(bf16[3,192,384]{2,1,0:T(8,128)(2,1)S(1)} %pad_maximum_fusion.refs_4_), channel_id=1, source_target_pairs={{0,24},{1,25},{2,26},{3,27},{4,28},{5,29},{6,30},{7,31},{8,0},{9,1... | collective-permute-start | bytes 1327112 | tf_op jit(solution)/shard_map/ppermute | solution.py:149
  178.4 19.6 %collective-permute-start.16 = (bf16[192,768]{1,0:T(8,128)(2,1)}, bf16[192,768]{1,0:T(8,128)(2,1)S(1)}, u32[]{:S(2)}, u32[]{:S(2)}) collective-permute-start(bf16[192,768]{1,0:T(8,128)(2,1)} %get-tuple-element.47), channel_id=1, source_target_pairs={{0,16},{1,17},{2,18},{3,19},{4,20},{5,21},{6,22},{7,23},{8,24},{9,... | collective-permute-start | bytes 884744 | tf_op jit(solution)/shard_map/ppermute | solution.py:149
  179.9 28.7 %collective-permute-start.17 = (bf16[192,768]{1,0:T(8,128)(2,1)}, bf16[192,768]{1,0:T(8,128)(2,1)S(1)}, u32[]{:S(2)}, u32[]{:S(2)}) collective-permute-start(bf16[192,768]{1,0:T(8,128)(2,1)} %get-tuple-element.39), channel_id=1, source_target_pairs={{0,24},{1,25},{2,26},{3,27},{4,28},{5,29},{6,30},{7,31},{8,0},{9,1... | collective-permute-start | bytes 884744 | tf_op jit(solution)/shard_map/ppermute | solution.py:149
  197.9 10.8 %copy-start.22 = (bf16[192,768]{1,0:T(8,128)(2,1)}, bf16[192,768]{1,0:T(8,128)(2,1)S(1)}, u32[]{:S(2)}) copy-start(bf16[192,768]{1,0:T(8,128)(2,1)S(1)} %collective-permute-done.16.refs_2_) | copy-start | bytes 884740
  215.7 36.8 %all-to-all-start.3 = ((bf16[8,3,96,384]{3,2,1,0:T(8,128)(2,1)}), bf16[8,3,96,384]{3,2,1,0:T(8,128)(2,1)}, u32[]{:S(2)}, u32[]{:S(2)}) async-start(bf16[8,3,96,384]{3,2,1,0:T(8,128)(2,1)} %weight_grads.2), calls=%async_computation.3 | async-start | bytes 3538944 | tf_op jit(solution)/shard_map/all_to_all | solution.py:143
  226.0 4.9 %collective-permute-start.12 = (bf16[192,768]{1,0:T(8,128)(2,1)S(1)}, bf16[192,768]{1,0:T(8,128)(2,1)S(1)}, u32[]{:S(2)}, u32[]{:S(2)}) collective-permute-start(bf16[192,768]{1,0:T(8,128)(2,1)S(1)} %get-tuple-element.51), channel_id=1, source_target_pairs={{0,32},{32,0},{64,96},{96,64},{1,33},{33,1},{65,97},{97,65},{2,34}... | collective-permute-start | bytes 884744 | tf_op jit(solution)/shard_map/ppermute | solution.py:311
  229.6 1.6 collective-permute-start.13
  231.5 20.0 %collective-permute-start.14 = (bf16[192,768]{1,0:T(8,128)(2,1)S(1)}, bf16[192,768]{1,0:T(8,128)(2,1)S(1)}, u32[]{:S(2)}, u32[]{:S(2)}) collective-permute-start(bf16[192,768]{1,0:T(8,128)(2,1)S(1)} %select_convert_fusion), channel_id=1, source_target_pairs={{0,64},{32,96},{64,0},{96,32},{1,65},{33,97},{65,1},{97,33},{2,66}... | collective-permute-start | bytes 884744 | tf_op jit(solution)/shard_map/ppermute | solution.py:316
  (13 other events, 14.4 us)

commit v2 on v1

--- a/solution.py
+++ b/solution.py
@@ -6,7 +6,8 @@
 from jax.sharding import PartitionSpec as P
 
 HD = 128
-MASKED = -1000000000.0
+LOG2E = 1.4426950408889634
+MASKED = -1000000000.0 * LOG2E
 F32 = jnp.float32
 BF16 = jnp.bfloat16
 NY = 4
@@ -35,7 +36,7 @@
 
 
 def scores(keys, q, valid, video):
-    s = nt_dot(keys, q) * HD**-0.5
+    s = nt_dot(keys, q) * (HD**-0.5 * LOG2E)
     return jnp.concatenate([s[:video], jnp.where(valid, s[video:], MASKED)], axis=0)
 
 
@@ -46,33 +47,29 @@
     k, v = pick(ks, tk_ref[...]), pick(vs, tv_ref[...])
     s = scores(k, q, mask_ref[:, 0:1] == 1, k.shape[0] - tk_ref.shape[0])
     top = jnp.max(s, axis=0, keepdims=True)
-    p = jnp.exp(s - top)
+    p = jnp.exp2(s - top)
     total = jnp.sum(p, axis=0, keepdims=True)
-    stat_ref[0, 0:1, :] = top
-    stat_ref[0, 1:2, :] = total
-    stat_ref[0, 2:3, :] = jnp.sum(p * nt_dot(v, g), axis=0, keepdims=True)
+    stat_ref[0, 0:1, :] = top + jnp.log2(total)
+    stat_ref[0, 1:2, :] = jnp.sum(p * nt_dot(v, g), axis=0, keepdims=True) / total
     out = tn_dot(v, p.astype(BF16)) / total
     out_ref[...] = out.T.astype(BF16).reshape(out_ref.shape)
 
 
 def merged(stat_ref):
-    tops = [stat_ref[i, 0, 0:1, :] for i in range(NZX)]
-    top = tops[0]
-    for other in tops[1:]:
+    logs = [stat_ref[i, 0, 0:1, :] for i in range(NZX)]
+    top = logs[0]
+    for other in logs[1:]:
         top = jnp.maximum(top, other)
-    total = jnp.zeros_like(top)
-    dot = jnp.zeros_like(top)
-    shares = []
-    for i in range(NZX):
-        factor = jnp.exp(tops[i] - top)
-        shares.append(factor * stat_ref[i, 0, 1:2, :])
-        total += shares[i]
-        dot += factor * stat_ref[i, 0, 2:3, :]
-    return top, total, dot / total, shares
+    shares = [jnp.exp2(log - top) for log in logs]
+    total = sum(shares[1:], shares[0])
+    dot = shares[0] * stat_ref[0, 0, 1:2, :]
+    for i in range(1, NZX):
+        dot += shares[i] * stat_ref[i, 0, 1:2, :]
+    return top + jnp.log2(total), dot / total, shares, total
 
 
 def combine_kernel(out_ref, stat_ref, o_ref):
-    _, total, _, shares = merged(stat_ref)
+    _, _, shares, total = merged(stat_ref)
     rows = out_ref.shape[1]
     acc = jnp.zeros((rows, HD), F32)
     for i in range(NZX):
@@ -89,11 +86,11 @@
     q, g = rows_of(q_ref), rows_of(g_ref)
     k, v = pick(ks, tk_ref[...]), pick(vs, tv_ref[...])
     keys = k.shape[0] - tk_ref.shape[0]
-    top, total, dot, _ = merged(stat_ref)
+    log_total, dot, _, _ = merged(stat_ref)
     s = scores(k, q, mask_ref[:, 0:1] == 1, keys)
-    p = jnp.exp(s - (top + jnp.log(total)))
-    ds = (p * (nt_dot(v, g) - dot) * HD**-0.5).astype(BF16)
-    dq = tn_dot(k, ds)
+    p = jnp.exp2(s - log_total)
+    ds = (p * (nt_dot(v, g) - dot)).astype(BF16)
+    dq = tn_dot(k, ds) * HD**-0.5
     dq_ref[...] = dq.T.astype(BF16).reshape(dq_ref.shape)
 
     @pl.when(step == 0)
@@ -109,20 +106,29 @@
         text = (acc_ref.shape[1] - keys) // NY
         for y in range(NY):
             kv_ref = kv_refs[y]
-            kv_ref[:per] = acc_ref[0, y * per : (y + 1) * per].astype(BF16)
+            kv_ref[:per] = (acc_ref[0, y * per : (y + 1) * per] * HD**-0.5).astype(BF16)
             kv_ref[per : 2 * per] = acc_ref[1, y * per : (y + 1) * per].astype(BF16)
             at = keys + y * text
             kv_ref[2 * per :] = jnp.concatenate(
-                [acc_ref[0, at : at + text], acc_ref[1, at : at + text]], axis=0
+                [acc_ref[0, at : at + text] * HD**-0.5, acc_ref[1, at : at + text]], axis=0
             ).astype(BF16)
 
 
 def weights_kernel(*refs):
-    xs, gs, o_ref = refs[:NY], refs[NY : 2 * NY], refs[2 * NY]
-    acc = tn_dot(xs[0][...], rows_of(gs[0]))
-    for y in range(1, NY):
-        acc += tn_dot(xs[y][...], rows_of(gs[y]))
-    o_ref[:, 0] = acc.astype(BF16).reshape(o_ref.shape[0], o_ref.shape[2], o_ref.shape[3])
+    xs, gs, o_ref = refs[:NY], refs[NY:-1], refs[-1]
+
+    def store(gs):
+        acc = tn_dot(xs[0][...], rows_of(gs[0]))
+        for y in range(1, NY):
+            acc += tn_dot(xs[y][...], rows_of(gs[y]))
+        o_ref[:, 0] = acc.astype(BF16).reshape(o_ref.shape[0], o_ref.shape[2], o_ref.shape[3])
+
+    if len(gs) == NY:
+        store(gs)
+    else:
+        first = pl.program_id(0) == 0
+        pl.when(first)(lambda: store(gs[:NY]))
+        pl.when(jnp.logical_not(first))(lambda: store(gs[NY:]))
 
 
 def per_device(inputs, out_grad, qkv_weight, out_weight, text_keys, text_values, text_mask):
@@ -153,8 +159,7 @@
     def around(array):
         return [array] + [shift(array, by) for by in range(1, NY)]
 
-    def head_gather(own):
-        far = lax.ppermute(own, "head", z_swap)
+    def head_gather(own, far):
         near = lax.ppermute(own, "head", core_swap)
         far_near = lax.ppermute(far, "head", core_swap)
         return [
@@ -176,11 +181,14 @@
         own = slice_for(y_at)
         return [own] + [shift(slice_for(lax.rem(y_at + by, NY)), by) for by in range(1, NY)]
 
-    in_parts = head_gather(inputs[:, 0])
-    grad_parts = head_gather(out_grad[:, 0])
+    far_in = lax.ppermute(inputs[:, 0], "head", z_swap)
+    far_grad = lax.ppermute(out_grad[:, 0], "head", z_swap)
+    in_parts = head_gather(inputs[:, 0], far_in)
     projected = jnp.einsum(
         "vd,dch->cvh", jnp.concatenate(in_parts, axis=1), qkv_weight, preferred_element_type=F32
     ).astype(BF16)
+    far_grad, projected = lax.optimization_barrier((far_grad, projected))
+    grad_parts = head_gather(out_grad[:, 0], far_grad)
     grad_attn = jnp.dot(
         jnp.concatenate(grad_parts, axis=1), out_weight, preferred_element_type=F32
     ).astype(BF16)
@@ -230,27 +238,26 @@
         grid=grid,
         in_specs=in_specs,
         out_specs=[
-            pl.BlockSpec((1, 3, q_rows), lambda h, i: (h, 0, i)),
+            pl.BlockSpec((1, 2, q_rows), lambda h, i: (h, 0, i)),
             pl.BlockSpec((half, rows, HD), lambda h, i: (i, 0, h)),
         ],
         out_shape=[
-            jax.ShapeDtypeStruct((heads, 3, steps * q_rows), F32),
+            jax.ShapeDtypeStruct((heads, 2, steps * q_rows), F32),
             jax.ShapeDtypeStruct((NZX, rows, width), BF16),
         ],
         compiler_params=params,
         name="attention_stats",
     )(*operands)
+    stats, x_in, x_grad = lax.optimization_barrier((stats, x_in, x_grad))
     all_stats = spread(stats)
     out_all = exchange(out_terms)
-    own_stats = lax.dynamic_index_in_dim(
-        all_stats.reshape(NZX, heads, 3, NZX, rows), zx, 3, keepdims=False
-    )
+    own_stats = lax.dynamic_slice_in_dim(all_stats, zx * rows, rows, 3)
     attn_out = pl.pallas_call(
         combine_kernel,
         grid=(heads,),
         in_specs=[
             pl.BlockSpec((NZX, rows, HD), lambda h: (0, 0, h)),
-            pl.BlockSpec((NZX, 1, 3, rows), lambda h: (0, h, 0, 0)),
+            pl.BlockSpec((NZX, 1, 2, rows), lambda h: (0, h, 0, 0)),
         ],
         out_specs=pl.BlockSpec((rows, HD), lambda h: (0, h)),
         out_shape=jax.ShapeDtypeStruct((rows, width), BF16),
@@ -262,7 +269,7 @@
     dq_terms, *kv_terms = pl.pallas_call(
         grads_kernel,
         grid=grid,
-        in_specs=in_specs + [pl.BlockSpec((NZX, 1, 3, q_rows), lambda h, i: (0, h, 0, i))],
+        in_specs=in_specs + [pl.BlockSpec((NZX, 1, 2, q_rows), lambda h, i: (0, h, 0, i))],
         out_specs=[pl.BlockSpec((half, rows, HD), lambda h, i: (i, 0, h))]
         + [pl.BlockSpec((kv_rows, HD), lambda h, i: (0, h))] * NY,
         out_shape=[jax.ShapeDtypeStruct((NZX, rows, width), BF16)]
@@ -282,22 +289,24 @@
 
     own = part // NZX
 
-    def weight_grad(xs, gs):
-        count = gs[0].shape[0]
+    def weight_grad(xs, gs, more=()):
+        count = 1 + (more[0].shape[0] if more else 0)
         terms = pl.pallas_call(
             weights_kernel,
             grid=(count,),
             in_specs=[pl.BlockSpec((rows, part), lambda c: (0, 0))] * NY
-            + [pl.BlockSpec((1, rows, width), lambda c: (c, 0, 0))] * NY,
+            + [pl.BlockSpec((1, rows, width), lambda c: (0, 0, 0))] * NY
+            + [pl.BlockSpec((1, rows, width), lambda c: (jnp.maximum(c - 1, 0), 0, 0))] * len(more),
             out_specs=pl.BlockSpec((NZX, 1, own, width), lambda c: (0, c, 0, 0)),
             out_shape=jax.ShapeDtypeStruct((NZX, count, own, width), BF16),
             compiler_params=pltpu.CompilerParams(vmem_limit_bytes=56 * 1024 * 1024),
             name="weight_grads",
-        )(*xs, *gs)
+        )(*xs, *gs, *more)
         return jnp.sum(exchange(terms).astype(F32), axis=0)
 
-    out_sum = weight_grad(x_grad, around(attn_out[None]))
-    qkv_sum = weight_grad(x_in, around(grad_projected))
+    outs, kv = lax.optimization_barrier((around(attn_out[None]), kv))
+    out_sum = weight_grad(x_grad, outs)
+    qkv_sum = weight_grad(x_in, around(dq[None]), around(kv))
 
     terms = jnp.einsum(
         "cvh,sdch->svd",

time: 256 us -> 218 us (0.85)
  waiting for transfers between devices: 98.6 us -> 54.1 us
  starting transfers between devices: 58.6 us -> 69.9 us
  blocking collectives: 18.6 us -> 12.8 us
    ppermute x18 -> x21, waiting for transfers between devices: 58.8 us -> 31.5 us  [shift(): lax.ppermute(array, 'blk', [(i, (i + by * NZX) % (NY * NZX)) for i in ran...]
    all_to_all x5, waiting for transfers between devices: 14.1 us -> 2.7 us  [exchange(): lax.all_to_all(array, 'blk', 0, 0, tiled=True, axis_index_groups=along_zx)]
    ppermute x18 -> x21, starting transfers between devices: 20.5 us -> 27.2 us  [shift(): lax.ppermute(array, 'blk', [(i, (i + by * NZX) % (NY * NZX)) for i in ran...]
    all_to_all x1, blocking collectives: 18.6 us -> 12.8 us  [exchange(): lax.all_to_all(array, 'blk', 0, 0, tiled=True, axis_index_groups=along_zx)]
    ppermute x2, waiting for transfers between devices: 10.2 us -> 5.99 us  [the longest x1 5.99 us: per_device(): far_in = lax.ppermute(inputs[:, 0], 'head', z_swap)]
    ppermute x2, starting transfers between devices: 3.74 us -> 6.86 us  [per_device(): lax.ppermute(give[z], 'head', core_swap).astype(F32)]
    ppermute x2, starting transfers between devices: 4.6 us -> 7.47 us  [the longest x1 4.51 us: per_device(): far_in = lax.ppermute(inputs[:, 0], 'head', z_swap)]
    ppermute x1, waiting for transfers between devices: 13.9 us -> 11.1 us  [per_device(): lax.ppermute(other, 'head', z_swap).astype(F32)]
  transfers between devices with their start and end apart: 32 -> 35, of which waited for: 16 -> 15; matrix products, arithmetic and copies ran while one was open for 11% -> 14% of each run, Pallas kernels for 11% -> 17%
where the time goes in v2:
time: 218 us; the launch traced here: 217 us
  starting transfers between devices  69.9 us (32%)
  waiting for transfers between devices  54.1 us (25%)
  Pallas kernels  37.6 us (17%)
  other arithmetic  15.2 us (7%)
  matrix products  14 us (6%)
  blocking collectives  12.8 us (6%)
  local copies, waits for them, and re-layouts  12.1 us (6%)
    ppermute x21, waiting for transfers between devices, shift(): lax.ppermute(array, 'blk', [(i, (i + by * NZX) % (NY * NZX)) for i in ran...  31.5 us
    ppermute x21, starting transfers between devices, shift(): lax.ppermute(array, 'blk', [(i, (i + by * NZX) % (NY * NZX)) for i in ran...  27.2 us
    all_to_all x5, starting transfers between devices, exchange(): lax.all_to_all(array, 'blk', 0, 0, tiled=True, axis_index_groups=along_zx)  21.8 us
    pallas_call x1, Pallas kernels, per_device(): pl.pallas_call(grads_kernel, grid=grid, in_specs=in_specs + [pl.BlockSpec...  14.5 us
    all_to_all x1, blocking collectives, exchange(): lax.all_to_all(array, 'blk', 0, 0, tiled=True, axis_index_groups=along_zx)  12.8 us
    ppermute x1, waiting for transfers between devices, per_device(): lax.ppermute(other, 'head', z_swap).astype(F32)  11.1 us
    pallas_call x1, Pallas kernels, per_device(): pl.pallas_call(stats_kernel, grid=grid, in_specs=in_specs, out_specs=[pl....  10.5 us
    pallas_call x2, Pallas kernels, weight_grad(): pl.pallas_call(weights_kernel, grid=(count,), in_specs=[pl.BlockSpec((row...  9.18 us
  transfers between devices with their start and end apart: 35, of which 15 were waited for; matrix products, arithmetic and copies ran while one was open for 14% of the time, Pallas kernels for 17%

profile of v2, /device:TPU:1, one launch (start us, length us, event | category | flops | bytes accessed | tf_op | source)
XLA Modules:
  0.0 216.7 jit_solution(16533223824857382186)
XLA Ops:
  0.6 4.5 %collective-permute-start.2 = (bf16[192,768]{1,0:T(8,128)(2,1)}, bf16[192,768]{1,0:T(8,128)(2,1)S(1)}, u32[]{:S(2)}, u32[]{:S(2)}) collective-permute-start(bf16[192,768]{1,0:T(8,128)(2,1)} %bitcast.87), channel_id=1, source_target_pairs={{0,64},{32,96},{64,0},{96,32},{1,65},{33,97},{65,1},{97,33},{2,66}... | collective-permute-start | bytes 884744 | tf_op jit(solution)/shard_map/ppermute | solution.py:184
  6.1 6.0 %collective-permute-done.2 = bf16[192,768]{1,0:T(8,128)(2,1)S(1)} collective-permute-done((bf16[192,768]{1,0:T(8,128)(2,1)}, bf16[192,768]{1,0:T(8,128)(2,1)S(1)}, u32[]{:S(2)}, u32[]{:S(2)}) %collective-permute-start.2) | collective-permute-done | bytes 294944 | tf_op jit(solution)/shard_map/ppermute | solution.py:184
  12.1 1.2 collective-permute-start.3
  13.3 3.0 %collective-permute-start = (bf16[192,768]{1,0:T(8,128)(2,1)}, bf16[192,768]{1,0:T(8,128)(2,1)S(1)}, u32[]{:S(2)}, u32[]{:S(2)}) collective-permute-start(bf16[192,768]{1,0:T(8,128)(2,1)} %bitcast.89), channel_id=1, source_target_pairs={{0,64},{32,96},{64,0},{96,32},{1,65},{33,97},{65,1},{97,33},{2,66}... | collective-permute-start | bytes 884744 | tf_op jit(solution)/shard_map/ppermute | solution.py:185
  16.6 1.9 select_select_fusion.4
  18.5 5.2 %fusion.1 = bf16[3,192,384]{2,1,0:T(8,128)(2,1)S(1)} fusion(bf16[3072,3,384]{2,0,1:T(8,128)(2,1)} %param.9, bf16[192,768]{1,0:T(8,128)(2,1)S(1)} %get-tuple-element.70, bf16[192,768]{1,0:T(8,128)(2,1)S(1)} %get-tuple-element.69, bf16[192,768]{1,0:T(8,128)(2,1)S(1)} %get-tuple-element.68, bf16[192,768]{1,0:T(8,128)(2,1)S(1)} %get-tuple-element.67), kind=kOutput, calls=%fused_computation.4 | convolution fusion | flops 1363894272 | bytes 8699904 | tf_op jit(solution)/shard_map/vd,dch->cvh/dot_general | solution.py:187
  24.5 1.2 collective-permute-done.5
  27.6 1.8 broadcast_in_dim.40
  29.4 4.7 %all-to-all-start = ((bf16[8,2,192,384]{3,2,1,0:T(8,128)(2,1)}), bf16[8,2,192,384]{3,2,1,0:T(8,128)(2,1)}, u32[]{:S(2)}, u32[]{:S(2)}) async-start(bf16[8,2,192,384]{3,2,1,0:T(8,128)(2,1)} %broadcast_in_dim.40), calls=%async_computation | async-start | bytes 4718592 | tf_op jit(solution)/shard_map/all_to_all | solution.py:149
  34.2 1.4 collective-permute-start.6
  35.6 2.6 %collective-permute-start.7 = (bf16[2,192,384]{2,1,0:T(8,128)(2,1)S(1)}, bf16[2,192,384]{2,1,0:T(8,128)(2,1)S(1)}, u32[]{:S(2)}, u32[]{:S(2)}) collective-permute-start(bf16[2,192,384]{2,1,0:T(8,128)(2,1)S(1)} %slice.38.refs_0_.refs_4_), channel_id=1, source_target_pairs={{0,16},{1,17},{2,18},{3,19},{4,20},{5,21},{6,22},{7,23},{8,24},{9,... | collective-permute-start | bytes 884744 | tf_op jit(solution)/shard_map/ppermute | solution.py:155
  39.3 2.1 select_select_fusion.5
  41.6 1.7 convolution_convert_fusion.1.refs_9_
  43.7 2.3 %select_select_fusion.1 = (bf16[192,768]{1,0:T(8,128)(2,1)}, bf16[192,768]{1,0:T(8,128)(2,1)}, bf16[192,768]{1,0:T(8,128)(2,1)}) fusion(bf16[192,768]{1,0:T(8,128)(2,1)} %copy-done.13, bf16[192,768]{1,0:T(8,128)(2,1)} %copy-done.14, bf16[192,768]{1,0:T(8,128)(2,1)} %copy-done.11, bf16[192,768]{1,0:T(8,128)(2,1)} %copy-done.12, pred[]{:T(512)S(6)} %eq.36, ...), kind=kLoop, calls=%fused_computation.40 | loop fusion | flops 1327104 | bytes 2064393 | tf_op jit(solution)/shard_map/jit(_where)/select_n | solution.py:177
  46.0 11.3 %collective-permute-done.10.refs_2_ = bf16[192,768]{1,0:T(8,128)(2,1)S(1)} collective-permute-done((bf16[192,768]{1,0:T(8,128)(2,1)S(1)}, bf16[192,768]{1,0:T(8,128)(2,1)S(1)}, u32[]{:S(2)}, u32[]{:S(2)}) %collective-permute-start.10) | collective-permute-done | bytes 294944 | tf_op jit(solution)/shard_map/ppermute | solution.py:155
  57.3 1.7 collective-permute-start.11
  59.1 1.6 collective-permute-start.13
  60.7 2.0 collective-permute-start.14
  64.8 10.5 %attention_stats.1 = (f32[3,2,1536]{2,1,0:T(2,128)}, bf16[8,192,384]{2,1,0:T(8,128)(2,1)}) custom-call(bf16[8,2,192,384]{3,2,1,0:T(8,128)(2,1)} %all-to-all-done.q_ref.g_ref, bf16[8,2,192,384]{3,2,1,0:T(8,128)(2,1)} %all-to-all-done.q_ref.g_ref, bf16[2,192,384]{2,1,0:T(8,128)(2,1)} %copy-done.1, bf16[2,192,384]{2,1,0:T(8,128)(2,1)} %copy-done.2, ...), custom_call_target="tpu_custom_call" | custom-call | tf_op jit(solution)/shard_map/attention_stats/pallas_call | solution.py:236
  77.5 12.8 %all_to_all.30.refs_11_ = f32[8,3,2,1536]{3,2,1,0:T(2,128)} all-to-all(f32[8,3,2,1536]{3,2,1,0:T(2,128)S(1)} %broadcast_in_dim.44), channel_id=1, replica_groups={{0,1,2,3,4,5,6,7},{8,9,10,11,12,13,14,15},{16,17,18,19,20,21,22,23},{24..., dimensions={0} | all-to-all | bytes 589824 | tf_op jit(solution)/shard_map/all_to_all | solution.py:149
  90.3 3.7 %all-to-all-start.3 = ((bf16[8,192,384]{2,1,0:T(8,128)(2,1)}), bf16[8,192,384]{2,1,0:T(8,128)(2,1)S(1)}, u32[]{:S(2)}, u32[]{:S(2)}) async-start(bf16[8,192,384]{2,1,0:T(8,128)(2,1)} %get-tuple-element.41), calls=%async_computation.3 | async-start | bytes 2359296 | tf_op jit(solution)/shard_map/all_to_all | solution.py:149
  94.1 14.5 %attention_grads.1 = (bf16[8,192,384]{2,1,0:T(8,128)(2,1)}, bf16[400,384]{1,0:T(8,128)(2,1)}, bf16[400,384]{1,0:T(8,128)(2,1)}, bf16[400,384]{1,0:T(8,128)(2,1)}, bf16[400,384]{1,0:T(8,128)(2,1)}) custom-call(bf16[8,2,192,384]{3,2,1,0:T(8,128)(2,1)} %all-to-all-done.q_ref.g_ref, bf16[8,2,192,384]{3,2,1,0:T(8,128)(2,1)} %all-to-all-done.q_ref.g_ref, ...), custom_call_target="tpu_custom_call" | custom-call | tf_op jit(solution)/shard_map/attention_grads/pallas_call | solution.py:269
  108.6 2.3 %all-to-all-done.3.out_ref = bf16[8,192,384]{2,1,0:T(8,128)(2,1)S(1)} async-done(((bf16[8,192,384]{2,1,0:T(8,128)(2,1)}), bf16[8,192,384]{2,1,0:T(8,128)(2,1)S(1)}, u32[]{:S(2)}, u32[]{:S(2)}) %all-to-all-start.3) | async-done | bytes 1179680 | tf_op jit(solution)/shard_map/all_to_all | solution.py:149
  112.0 3.6 %all-to-all-start.2 = ((bf16[8,192,384]{2,1,0:T(8,128)(2,1)}), bf16[8,192,384]{2,1,0:T(8,128)(2,1)S(1)}, u32[]{:S(2)}, u32[]{:S(2)}) async-start(bf16[8,192,384]{2,1,0:T(8,128)(2,1)} %get-tuple-element.32), calls=%async_computation.2 | async-start | bytes 2359296 | tf_op jit(solution)/shard_map/all_to_all | solution.py:149
  115.5 2.9 %collective-permute-start.15 = (bf16[400,384]{1,0:T(8,128)(2,1)}, bf16[400,384]{1,0:T(8,128)(2,1)}, u32[]{:S(2)}, u32[]{:S(2)}) collective-permute-start(bf16[400,384]{1,0:T(8,128)(2,1)} %get-tuple-element.34), channel_id=1, source_target_pairs={{0,24},{1,25},{2,26},{3,27},{4,28},{5,29},{6,30},{7,31},{8,0},{9,1... | collective-permute-start | bytes 921608 | tf_op jit(solution)/shard_map/ppermute | solution.py:155
  119.5 1.6 constant_dynamic-slice_fusion.stat_ref
  121.1 3.4 %combine_out.1 = bf16[192,384]{1,0:T(8,128)(2,1)} custom-call(bf16[8,192,384]{2,1,0:T(8,128)(2,1)} %copy-done.5, f32[8,3,2,192]{3,2,1,0:T(2,128)} %constant_dynamic-slice_fusion.stat_ref), custom_call_target="tpu_custom_call" | custom-call | tf_op jit(solution)/shard_map/combine_out/pallas_call | solution.py:255
  124.5 1.5 collective-permute-start.24
  126.1 1.6 collective-permute-start.25
  127.7 1.6 collective-permute-start.26
  129.3 6.6 %collective-permute-done.17 = bf16[400,384]{1,0:T(8,128)(2,1)} collective-permute-done((bf16[400,384]{1,0:T(8,128)(2,1)}, bf16[400,384]{1,0:T(8,128)(2,1)}, u32[]{:S(2)}, u32[]{:S(2)}) %collective-permute-start.17) | collective-permute-done | bytes 307232 | tf_op jit(solution)/shard_map/ppermute | solution.py:155
  136.0 1.4 convert_add_fusion
  139.0 1.7 collective-permute-done.24.refs_5_
  141.4 3.2 %weight_grads.3 = bf16[8,1,96,384]{3,2,1,0:T(8,128)(2,1)} custom-call(bf16[192,768]{1,0:T(8,128)(2,1)} %get-tuple-element.43.refs_0_, bf16[192,768]{1,0:T(8,128)(2,1)} %collective-permute-done.12.refs_1_, bf16[192,768]{1,0:T(8,128)(2,1)} %collective-permute-done.13.refs_2_, bf16[192,768]{1,0:T(8,128)(2,1)} %collective-permute-done.14.refs_3_, ...), custom_call_target="tpu_custom_call" | custom-call | tf_op jit(solution)/shard_map/weight_grads/pallas_call | solution.py:294
  144.6 4.5 %all-to-all-start.5 = ((bf16[8,1,96,384]{3,2,1,0:T(8,128)(2,1)}), bf16[8,1,96,384]{3,2,1,0:T(8,128)(2,1)}, u32[]{:S(2)}, u32[]{:S(2)}) async-start(bf16[8,1,96,384]{3,2,1,0:T(8,128)(2,1)} %weight_grads.3), calls=%async_computation.5 | async-start | bytes 1179648 | tf_op jit(solution)/shard_map/all_to_all | solution.py:149
  150.0 3.9 %collective-permute-start.28 = (bf16[2,192,384]{2,1,0:T(8,128)(2,1)}, bf16[2,192,384]{2,1,0:T(8,128)(2,1)S(1)}, u32[]{:S(2)}, u32[]{:S(2)}) collective-permute-start(bf16[2,192,384]{2,1,0:T(8,128)(2,1)} %bitcast.73), channel_id=1, source_target_pairs={{0,16},{1,17},{2,18},{3,19},{4,20},{5,21},{6,22},{7,23},{8,24},{9,... | collective-permute-start | bytes 884744 | tf_op jit(solution)/shard_map/ppermute | solution.py:155
  153.8 1.2 collective-permute-start.22
  155.4 2.3 %collective-permute-start.23 = (bf16[1,192,384]{2,1,0:T(8,128)(2,1)}, bf16[1,192,384]{2,1,0:T(8,128)(2,1)S(1)}, u32[]{:S(2)}, u32[]{:S(2)}) collective-permute-start(bf16[1,192,384]{2,1,0:T(8,128)(2,1)} %bitcast.79), channel_id=1, source_target_pairs={{0,24},{1,25},{2,26},{3,27},{4,28},{5,29},{6,30},{7,31},{8,0},{9,1... | collective-permute-start | bytes 442376 | tf_op jit(solution)/shard_map/ppermute | solution.py:155
  157.7 7.8 %collective-permute-done.22.refs_6_ = bf16[1,192,384]{2,1,0:T(8,128)(2,1)S(1)} collective-permute-done((bf16[1,192,384]{2,1,0:T(8,128)(2,1)}, bf16[1,192,384]{2,1,0:T(8,128)(2,1)S(1)}, u32[]{:S(2)}, u32[]{:S(2)}) %collective-permute-start.22) | collective-permute-done | bytes 147488 | tf_op jit(solution)/shard_map/ppermute | solution.py:155
  165.5 2.4 %collective-permute-done.23.refs_7_ = bf16[1,192,384]{2,1,0:T(8,128)(2,1)S(1)} collective-permute-done((bf16[1,192,384]{2,1,0:T(8,128)(2,1)}, bf16[1,192,384]{2,1,0:T(8,128)(2,1)S(1)}, u32[]{:S(2)}, u32[]{:S(2)}) %collective-permute-start.23) | collective-permute-done | bytes 147488 | tf_op jit(solution)/shard_map/ppermute | solution.py:155
  169.5 5.9 %weight_grads.2 = bf16[8,3,96,384]{3,2,1,0:T(8,128)(2,1)} custom-call(bf16[192,768]{1,0:T(8,128)(2,1)} %get-tuple-element.37.refs_0_, bf16[192,768]{1,0:T(8,128)(2,1)} %collective-permute-done.9.refs_1_, bf16[192,768]{1,0:T(8,128)(2,1)} %copy-done.18, bf16[192,768]{1,0:T(8,128)(2,1)} %collective-permute-done.11.refs_3_, bf16[1,192,384]{2,1,0:T(8,128)(2,1)} %bitcast.80, ...), custom_call_target="tpu_custom_call" | custom-call | tf_op jit(solution)/shard_map/weight_grads/pallas_call | solution.py:294
  175.4 5.2 %all-to-all-start.4 = ((bf16[8,3,96,384]{3,2,1,0:T(8,128)(2,1)}), bf16[8,3,96,384]{3,2,1,0:T(8,128)(2,1)}, u32[]{:S(2)}, u32[]{:S(2)}) async-start(bf16[8,3,96,384]{3,2,1,0:T(8,128)(2,1)} %weight_grads.2), calls=%async_computation.4 | async-start | bytes 3538944 | tf_op jit(solution)/shard_map/all_to_all | solution.py:149
  180.6 5.5 %fusion = bf16[4,192,768]{2,1,0:T(8,128)(2,1)S(1)} fusion(bf16[4,768,3,384]{3,1,0,2:T(8,128)(2,1)} %bitcast.92, bf16[2,192,384]{2,1,0:T(8,128)(2,1)S(1)} %bitcast.76, bf16[1,192,384]{2,1,0:T(8,128)(2,1)S(1)} %bitcast.81), kind=kOutput, calls=%fused_computation.2 | convolution fusion | flops 1360429056 | bytes 8699904 | tf_op jit(solution)/shard_map/cvh,sdch->svd/dot_general | solution.py:311
  186.2 6.8 %collective-permute-start.18 = (bf16[192,768]{1,0:T(8,128)(2,1)S(1)}, bf16[192,768]{1,0:T(8,128)(2,1)S(1)}, u32[]{:S(2)}, u32[]{:S(2)}) collective-permute-start(bf16[192,768]{1,0:T(8,128)(2,1)S(1)} %get-tuple-element.72), channel_id=1, source_target_pairs={{0,32},{32,0},{64,96},{96,64},{1,33},{33,1},{65,97},{97,65},{2,34}... | collective-permute-start | bytes 884744 | tf_op jit(solution)/shard_map/ppermute | solution.py:320
  194.8 3.4 %collective-permute-start.20 = (bf16[192,768]{1,0:T(8,128)(2,1)S(1)}, bf16[192,768]{1,0:T(8,128)(2,1)S(1)}, u32[]{:S(2)}, u32[]{:S(2)}) collective-permute-start(bf16[192,768]{1,0:T(8,128)(2,1)S(1)} %select_convert_fusion), channel_id=1, source_target_pairs={{0,64},{32,96},{64,0},{96,32},{1,65},{33,97},{65,1},{97,33},{2,66}... | collective-permute-start | bytes 884744 | tf_op jit(solution)/shard_map/ppermute | solution.py:325
  200.2 1.8 convert_reduce_fusion.1
  202.0 11.1 %collective-permute-done.20 = bf16[192,768]{1,0:T(8,128)(2,1)S(1)} collective-permute-done((bf16[192,768]{1,0:T(8,128)(2,1)S(1)}, bf16[192,768]{1,0:T(8,128)(2,1)S(1)}, u32[]{:S(2)}, u32[]{:S(2)}) %collective-permute-start.20) | collective-permute-done | bytes 294944 | tf_op jit(solution)/shard_map/ppermute | solution.py:325
  214.2 2.5 %convert_reduce_fusion = f32[3,96,384]{2,1,0:T(8,128)} fusion(bf16[8,3,96,384]{3,2,1,0:T(8,128)(2,1)} %all-to-all-done.4), kind=kLoop, calls=%fused_computation | loop fusion | flops 1658880 | bytes 2211840 | tf_op jit(solution)/shard_map/reduce_sum | solution.py:305
  (119 shorter events, 21.9 us)
Async XLA Ops:
  0.6 25.9 %copy-start = (bf16[3072,384]{1,0:T(8,128)(2,1)S(1)}, bf16[3072,384]{1,0:T(8,128)(2,1)}, u32[]{:S(2)}) copy-start(bf16[3072,384]{1,0:T(8,128)(2,1)} %param.10) | copy-start | bytes 7077892
  0.6 11.4 %collective-permute-start.2 = (bf16[192,768]{1,0:T(8,128)(2,1)}, bf16[192,768]{1,0:T(8,128)(2,1)S(1)}, u32[]{:S(2)}, u32[]{:S(2)}) collective-permute-start(bf16[192,768]{1,0:T(8,128)(2,1)} %bitcast.87), channel_id=1, source_target_pairs={{0,64},{32,96},{64,0},{96,32},{1,65},{33,97},{65,1},{97,33},{2,66}... | collective-permute-start | bytes 884744 | tf_op jit(solution)/shard_map/ppermute | solution.py:184
  5.2 11.4 %collective-permute-start.1 = (bf16[192,768]{1,0:T(8,128)(2,1)}, bf16[192,768]{1,0:T(8,128)(2,1)S(1)}, u32[]{:S(2)}, u32[]{:S(2)}) collective-permute-start(bf16[192,768]{1,0:T(8,128)(2,1)} %bitcast.88), channel_id=1, source_target_pairs={{0,32},{32,0},{64,96},{96,64},{1,33},{33,1},{65,97},{97,65},{2,34}... | collective-permute-start | bytes 884744 | tf_op jit(solution)/shard_map/ppermute | solution.py:163
  12.1 4.5 %collective-permute-start.3 = (bf16[192,768]{1,0:T(8,128)(2,1)S(1)}, bf16[192,768]{1,0:T(8,128)(2,1)}, u32[]{:S(2)}, u32[]{:S(2)}) collective-permute-start(bf16[192,768]{1,0:T(8,128)(2,1)S(1)} %collective-permute-done.2), channel_id=1, source_target_pairs={{0,32},{32,0},{64,96},{96,64},{1,33},{33,1},{65,97},{97,65},{2,34}... | collective-permute-start | bytes 884744 | tf_op jit(solution)/shard_map/ppermute | solution.py:164
  13.3 10.4 %collective-permute-start = (bf16[192,768]{1,0:T(8,128)(2,1)}, bf16[192,768]{1,0:T(8,128)(2,1)S(1)}, u32[]{:S(2)}, u32[]{:S(2)}) collective-permute-start(bf16[192,768]{1,0:T(8,128)(2,1)} %bitcast.89), channel_id=1, source_target_pairs={{0,64},{32,96},{64,0},{96,32},{1,65},{33,97},{65,1},{97,33},{2,66}... | collective-permute-start | bytes 884744 | tf_op jit(solution)/shard_map/ppermute | solution.py:185
  16.3 8.2 %collective-permute-start.4 = (bf16[192,768]{1,0:T(8,128)(2,1)}, bf16[192,768]{1,0:T(8,128)(2,1)S(1)}, u32[]{:S(2)}, u32[]{:S(2)}) collective-permute-start(bf16[192,768]{1,0:T(8,128)(2,1)} %bitcast.90), channel_id=1, source_target_pairs={{0,32},{32,0},{64,96},{96,64},{1,33},{33,1},{65,97},{97,65},{2,34}... | collective-permute-start | bytes 884744 | tf_op jit(solution)/shard_map/ppermute | solution.py:163
  18.5 5.2 %copy-start.8 = (bf16[192,768]{1,0:T(8,128)(2,1)}, bf16[192,768]{1,0:T(8,128)(2,1)S(1)}, u32[]{:S(2)}) copy-start(bf16[192,768]{1,0:T(8,128)(2,1)S(1)} %get-tuple-element.68) | copy-start | bytes 884740
  18.5 5.2 %copy-start.9 = (bf16[192,768]{1,0:T(8,128)(2,1)}, bf16[192,768]{1,0:T(8,128)(2,1)S(1)}, u32[]{:S(2)}) copy-start(bf16[192,768]{1,0:T(8,128)(2,1)S(1)} %get-tuple-element.69) | copy-start | bytes 884740
  18.5 5.2 %copy-start.10 = (bf16[192,768]{1,0:T(8,128)(2,1)}, bf16[192,768]{1,0:T(8,128)(2,1)S(1)}, u32[]{:S(2)}) copy-start(bf16[192,768]{1,0:T(8,128)(2,1)S(1)} %get-tuple-element.70) | copy-start | bytes 884740
  18.5 7.2 %copy-start.17 = (bf16[192,1,768]{2,0,1:T(8,128)(2,1)S(1)}, bf16[192,1,768]{2,0,1:T(8,128)(2,1)}, u32[]{:S(2)}) copy-start(bf16[192,1,768]{2,0,1:T(8,128)(2,1)} %param.8) | copy-start | bytes 884740
  23.7 1.9 collective-permute-start.5
  29.4 34.7 %all-to-all-start = ((bf16[8,2,192,384]{3,2,1,0:T(8,128)(2,1)}), bf16[8,2,192,384]{3,2,1,0:T(8,128)(2,1)}, u32[]{:S(2)}, u32[]{:S(2)}) async-start(bf16[8,2,192,384]{3,2,1,0:T(8,128)(2,1)} %broadcast_in_dim.40), calls=%async_computation | async-start | bytes 4718592 | tf_op jit(solution)/shard_map/all_to_all | solution.py:149
  34.2 29.6 %copy-start.1 = (bf16[2,192,384]{2,1,0:T(8,128)(2,1)}, bf16[2,192,384]{2,1,0:T(8,128)(2,1)S(1)}, u32[]{:S(2)}) copy-start(bf16[2,192,384]{2,1,0:T(8,128)(2,1)S(1)} %slice.38.refs_0_.refs_4_) | copy-start | bytes 884740
  34.2 28.6 %copy-start.28 = (s32[256,1]{0,1:T(1,128)S(1)}, s32[256,1]{0,1:T(1,128)}, u32[]{:S(2)}) copy-start(s32[256,1]{0,1:T(1,128)} %param.13) | copy-start | bytes 3076
  34.2 28.7 %copy-start.29 = (bf16[256,1,384]{2,0,1:T(8,128)(2,1)S(1)}, bf16[256,1,384]{2,0,1:T(8,128)(2,1)}, u32[]{:S(2)}) copy-start(bf16[256,1,384]{2,0,1:T(8,128)(2,1)} %param.11) | copy-start | bytes 589828
  34.2 24.8 %collective-permute-start.6 = (bf16[2,192,384]{2,1,0:T(8,128)(2,1)S(1)}, bf16[2,192,384]{2,1,0:T(8,128)(2,1)S(1)}, u32[]{:S(2)}, u32[]{:S(2)}) collective-permute-start(bf16[2,192,384]{2,1,0:T(8,128)(2,1)S(1)} %slice.38.refs_0_.refs_4_), channel_id=1, source_target_pairs={{0,8},{1,9},{2,10},{3,11},{4,12},{5,13},{6,14},{7,15},{8,16},{9,17... | collective-permute-start | bytes 884744 | tf_op jit(solution)/shard_map/ppermute | solution.py:155
  35.6 23.5 %collective-permute-start.7 = (bf16[2,192,384]{2,1,0:T(8,128)(2,1)S(1)}, bf16[2,192,384]{2,1,0:T(8,128)(2,1)S(1)}, u32[]{:S(2)}, u32[]{:S(2)}) collective-permute-start(bf16[2,192,384]{2,1,0:T(8,128)(2,1)S(1)} %slice.38.refs_0_.refs_4_), channel_id=1, source_target_pairs={{0,16},{1,17},{2,18},{3,19},{4,20},{5,21},{6,22},{7,23},{8,24},{9,... | collective-permute-start | bytes 884744 | tf_op jit(solution)/shard_map/ppermute | solution.py:155
  38.2 22.5 %collective-permute-start.8 = (bf16[2,192,384]{2,1,0:T(8,128)(2,1)S(1)}, bf16[2,192,384]{2,1,0:T(8,128)(2,1)S(1)}, u32[]{:S(2)}, u32[]{:S(2)}) collective-permute-start(bf16[2,192,384]{2,1,0:T(8,128)(2,1)S(1)} %slice.38.refs_0_.refs_4_), channel_id=1, source_target_pairs={{0,24},{1,25},{2,26},{3,27},{4,28},{5,29},{6,30},{7,31},{8,0},{9,1... | collective-permute-start | bytes 884744 | tf_op jit(solution)/shard_map/ppermute | solution.py:155
  41.4 15.9 %collective-permute-start.10 = (bf16[192,768]{1,0:T(8,128)(2,1)S(1)}, bf16[192,768]{1,0:T(8,128)(2,1)S(1)}, u32[]{:S(2)}, u32[]{:S(2)}) collective-permute-start(bf16[192,768]{1,0:T(8,128)(2,1)S(1)} %get-tuple-element.76), channel_id=1, source_target_pairs={{0,16},{1,17},{2,18},{3,19},{4,20},{5,21},{6,22},{7,23},{8,24},{9,... | collective-permute-start | bytes 884744 | tf_op jit(solution)/shard_map/ppermute | solution.py:155
  43.4 31.9 %collective-permute-start.9 = (bf16[192,768]{1,0:T(8,128)(2,1)}, bf16[192,768]{1,0:T(8,128)(2,1)}, u32[]{:S(2)}, u32[]{:S(2)}) collective-permute-start(bf16[192,768]{1,0:T(8,128)(2,1)} %get-tuple-element.77), channel_id=1, source_target_pairs={{0,8},{1,9},{2,10},{3,11},{4,12},{5,13},{6,14},{7,15},{8,16},{9,17... | collective-permute-start | bytes 884744 | tf_op jit(solution)/shard_map/ppermute | solution.py:155
  57.3 18.0 %collective-permute-start.11 = (bf16[192,768]{1,0:T(8,128)(2,1)}, bf16[192,768]{1,0:T(8,128)(2,1)}, u32[]{:S(2)}, u32[]{:S(2)}) collective-permute-start(bf16[192,768]{1,0:T(8,128)(2,1)} %get-tuple-element.66), channel_id=1, source_target_pairs={{0,24},{1,25},{2,26},{3,27},{4,28},{5,29},{6,30},{7,31},{8,0},{9,1... | collective-permute-start | bytes 884744 | tf_op jit(solution)/shard_map/ppermute | solution.py:155
  59.1 5.7 %copy-start.2 = (bf16[2,192,384]{2,1,0:T(8,128)(2,1)}, bf16[2,192,384]{2,1,0:T(8,128)(2,1)S(1)}, u32[]{:S(2)}) copy-start(bf16[2,192,384]{2,1,0:T(8,128)(2,1)S(1)} %collective-permute-done.6.refs_1_.refs_5_) | copy-start | bytes 884740
  59.1 16.3 %collective-permute-start.12 = (bf16[192,768]{1,0:T(8,128)(2,1)}, bf16[192,768]{1,0:T(8,128)(2,1)}, u32[]{:S(2)}, u32[]{:S(2)}) collective-permute-start(bf16[192,768]{1,0:T(8,128)(2,1)} %get-tuple-element.74), channel_id=1, source_target_pairs={{0,8},{1,9},{2,10},{3,11},{4,12},{5,13},{6,14},{7,15},{8,16},{9,17... | collective-permute-start | bytes 884744 | tf_op jit(solution)/shard_map/ppermute | solution.py:155
  59.1 5.7 %copy-start.3 = (bf16[2,192,384]{2,1,0:T(8,128)(2,1)}, bf16[2,192,384]{2,1,0:T(8,128)(2,1)S(1)}, u32[]{:S(2)}) copy-start(bf16[2,192,384]{2,1,0:T(8,128)(2,1)S(1)} %collective-permute-done.7.refs_2_.refs_6_) | copy-start | bytes 884740
  59.1 17.3 %collective-permute-start.13 = (bf16[192,768]{1,0:T(8,128)(2,1)}, bf16[192,768]{1,0:T(8,128)(2,1)}, u32[]{:S(2)}, u32[]{:S(2)}) collective-permute-start(bf16[192,768]{1,0:T(8,128)(2,1)} %get-tuple-element.73), channel_id=1, source_target_pairs={{0,16},{1,17},{2,18},{3,19},{4,20},{5,21},{6,22},{7,23},{8,24},{9,... | collective-permute-start | bytes 884744 | tf_op jit(solution)/shard_map/ppermute | solution.py:155
  60.7 15.9 %collective-permute-start.14 = (bf16[192,768]{1,0:T(8,128)(2,1)}, bf16[192,768]{1,0:T(8,128)(2,1)}, u32[]{:S(2)}, u32[]{:S(2)}) collective-permute-start(bf16[192,768]{1,0:T(8,128)(2,1)} %get-tuple-element.61), channel_id=1, source_target_pairs={{0,24},{1,25},{2,26},{3,27},{4,28},{5,29},{6,30},{7,31},{8,0},{9,1... | collective-permute-start | bytes 884744 | tf_op jit(solution)/shard_map/ppermute | solution.py:155
  90.3 20.6 %all-to-all-start.3 = ((bf16[8,192,384]{2,1,0:T(8,128)(2,1)}), bf16[8,192,384]{2,1,0:T(8,128)(2,1)S(1)}, u32[]{:S(2)}, u32[]{:S(2)}) async-start(bf16[8,192,384]{2,1,0:T(8,128)(2,1)} %get-tuple-element.41), calls=%async_computation.3 | async-start | bytes 2359296 | tf_op jit(solution)/shard_map/all_to_all | solution.py:149
  112.0 32.6 %all-to-all-start.2 = ((bf16[8,192,384]{2,1,0:T(8,128)(2,1)}), bf16[8,192,384]{2,1,0:T(8,128)(2,1)S(1)}, u32[]{:S(2)}, u32[]{:S(2)}) async-start(bf16[8,192,384]{2,1,0:T(8,128)(2,1)} %get-tuple-element.32), calls=%async_computation.2 | async-start | bytes 2359296 | tf_op jit(solution)/shard_map/all_to_all | solution.py:149
  115.5 12.1 %collective-permute-start.15 = (bf16[400,384]{1,0:T(8,128)(2,1)}, bf16[400,384]{1,0:T(8,128)(2,1)}, u32[]{:S(2)}, u32[]{:S(2)}) collective-permute-start(bf16[400,384]{1,0:T(8,128)(2,1)} %get-tuple-element.34), channel_id=1, source_target_pairs={{0,24},{1,25},{2,26},{3,27},{4,28},{5,29},{6,30},{7,31},{8,0},{9,1... | collective-permute-start | bytes 921608 | tf_op jit(solution)/shard_map/ppermute | solution.py:155
  118.4 10.9 %collective-permute-start.16 = (bf16[400,384]{1,0:T(8,128)(2,1)}, bf16[400,384]{1,0:T(8,128)(2,1)}, u32[]{:S(2)}, u32[]{:S(2)}) collective-permute-start(bf16[400,384]{1,0:T(8,128)(2,1)} %get-tuple-element.35), channel_id=1, source_target_pairs={{0,16},{1,17},{2,18},{3,19},{4,20},{5,21},{6,22},{7,23},{8,24},{9,... | collective-permute-start | bytes 921608 | tf_op jit(solution)/shard_map/ppermute | solution.py:155
  118.8 17.2 %collective-permute-start.17 = (bf16[400,384]{1,0:T(8,128)(2,1)}, bf16[400,384]{1,0:T(8,128)(2,1)}, u32[]{:S(2)}, u32[]{:S(2)}) collective-permute-start(bf16[400,384]{1,0:T(8,128)(2,1)} %get-tuple-element.36), channel_id=1, source_target_pairs={{0,8},{1,9},{2,10},{3,11},{4,12},{5,13},{6,14},{7,15},{8,16},{9,17... | collective-permute-start | bytes 921608 | tf_op jit(solution)/shard_map/ppermute | solution.py:155
  124.5 16.1 %collective-permute-start.24 = (bf16[1,192,384]{2,1,0:T(8,128)(2,1)}, bf16[1,192,384]{2,1,0:T(8,128)(2,1)S(1)}, u32[]{:S(2)}, u32[]{:S(2)}) collective-permute-start(bf16[1,192,384]{2,1,0:T(8,128)(2,1)} %bitcast.82), channel_id=1, source_target_pairs={{0,8},{1,9},{2,10},{3,11},{4,12},{5,13},{6,14},{7,15},{8,16},{9,17... | collective-permute-start | bytes 442376 | tf_op jit(solution)/shard_map/ppermute | solution.py:155
  126.1 14.6 %collective-permute-start.25 = (bf16[1,192,384]{2,1,0:T(8,128)(2,1)}, bf16[1,192,384]{2,1,0:T(8,128)(2,1)S(1)}, u32[]{:S(2)}, u32[]{:S(2)}) collective-permute-start(bf16[1,192,384]{2,1,0:T(8,128)(2,1)} %bitcast.83), channel_id=1, source_target_pairs={{0,16},{1,17},{2,18},{3,19},{4,20},{5,21},{6,22},{7,23},{8,24},{9,... | collective-permute-start | bytes 442376 | tf_op jit(solution)/shard_map/ppermute | solution.py:155
  127.7 12.9 %collective-permute-start.26 = (bf16[1,192,384]{2,1,0:T(8,128)(2,1)}, bf16[1,192,384]{2,1,0:T(8,128)(2,1)S(1)}, u32[]{:S(2)}, u32[]{:S(2)}) collective-permute-start(bf16[1,192,384]{2,1,0:T(8,128)(2,1)} %bitcast.84), channel_id=1, source_target_pairs={{0,24},{1,25},{2,26},{3,27},{4,28},{5,29},{6,30},{7,31},{8,0},{9,1... | collective-permute-start | bytes 442376 | tf_op jit(solution)/shard_map/ppermute | solution.py:155
  144.6 30.8 %all-to-all-start.5 = ((bf16[8,1,96,384]{3,2,1,0:T(8,128)(2,1)}), bf16[8,1,96,384]{3,2,1,0:T(8,128)(2,1)}, u32[]{:S(2)}, u32[]{:S(2)}) async-start(bf16[8,1,96,384]{3,2,1,0:T(8,128)(2,1)} %weight_grads.3), calls=%async_computation.5 | async-start | bytes 1179648 | tf_op jit(solution)/shard_map/all_to_all | solution.py:149
  150.0 5.4 %collective-permute-start.21 = (bf16[1,192,384]{2,1,0:T(8,128)(2,1)}, bf16[1,192,384]{2,1,0:T(8,128)(2,1)S(1)}, u32[]{:S(2)}, u32[]{:S(2)}) collective-permute-start(bf16[1,192,384]{2,1,0:T(8,128)(2,1)} %bitcast.77), channel_id=1, source_target_pairs={{0,8},{1,9},{2,10},{3,11},{4,12},{5,13},{6,14},{7,15},{8,16},{9,17... | collective-permute-start | bytes 442376 | tf_op jit(solution)/shard_map/ppermute | solution.py:155
  150.0 17.9 %collective-permute-start.27 = (bf16[2,192,384]{2,1,0:T(8,128)(2,1)}, bf16[2,192,384]{2,1,0:T(8,128)(2,1)S(1)}, u32[]{:S(2)}, u32[]{:S(2)}) collective-permute-start(bf16[2,192,384]{2,1,0:T(8,128)(2,1)} %bitcast.72), channel_id=1, source_target_pairs={{0,8},{1,9},{2,10},{3,11},{4,12},{5,13},{6,14},{7,15},{8,16},{9,17... | collective-permute-start | bytes 884744 | tf_op jit(solution)/shard_map/ppermute | solution.py:155
  150.0 17.9 %collective-permute-start.28 = (bf16[2,192,384]{2,1,0:T(8,128)(2,1)}, bf16[2,192,384]{2,1,0:T(8,128)(2,1)S(1)}, u32[]{:S(2)}, u32[]{:S(2)}) collective-permute-start(bf16[2,192,384]{2,1,0:T(8,128)(2,1)} %bitcast.73), channel_id=1, source_target_pairs={{0,16},{1,17},{2,18},{3,19},{4,20},{5,21},{6,22},{7,23},{8,24},{9,... | collective-permute-start | bytes 884744 | tf_op jit(solution)/shard_map/ppermute | solution.py:155
  153.8 14.1 %collective-permute-start.29 = (bf16[2,192,384]{2,1,0:T(8,128)(2,1)}, bf16[2,192,384]{2,1,0:T(8,128)(2,1)S(1)}, u32[]{:S(2)}, u32[]{:S(2)}) collective-permute-start(bf16[2,192,384]{2,1,0:T(8,128)(2,1)} %bitcast.74), channel_id=1, source_target_pairs={{0,24},{1,25},{2,26},{3,27},{4,28},{5,29},{6,30},{7,31},{8,0},{9,1... | collective-permute-start | bytes 884744 | tf_op jit(solution)/shard_map/ppermute | solution.py:155
  153.8 11.7 %collective-permute-start.22 = (bf16[1,192,384]{2,1,0:T(8,128)(2,1)}, bf16[1,192,384]{2,1,0:T(8,128)(2,1)S(1)}, u32[]{:S(2)}, u32[]{:S(2)}) collective-permute-start(bf16[1,192,384]{2,1,0:T(8,128)(2,1)} %bitcast.78), channel_id=1, source_target_pairs={{0,16},{1,17},{2,18},{3,19},{4,20},{5,21},{6,22},{7,23},{8,24},{9,... | collective-permute-start | bytes 442376 | tf_op jit(solution)/shard_map/ppermute | solution.py:155
  155.4 12.6 %copy-start.22 = (bf16[1,192,384]{2,1,0:T(8,128)(2,1)}, bf16[1,192,384]{2,1,0:T(8,128)(2,1)S(1)}, u32[]{:S(2)}) copy-start(bf16[1,192,384]{2,1,0:T(8,128)(2,1)S(1)} %collective-permute-done.21.refs_5_) | copy-start | bytes 442372
  155.4 12.5 %collective-permute-start.23 = (bf16[1,192,384]{2,1,0:T(8,128)(2,1)}, bf16[1,192,384]{2,1,0:T(8,128)(2,1)S(1)}, u32[]{:S(2)}, u32[]{:S(2)}) collective-permute-start(bf16[1,192,384]{2,1,0:T(8,128)(2,1)} %bitcast.79), channel_id=1, source_target_pairs={{0,24},{1,25},{2,26},{3,27},{4,28},{5,29},{6,30},{7,31},{8,0},{9,1... | collective-permute-start | bytes 442376 | tf_op jit(solution)/shard_map/ppermute | solution.py:155
  175.4 5.2 %copy-start.15 = (bf16[384,384]{1,0:T(8,128)(2,1)S(1)}, bf16[384,384]{1,0:T(8,128)(2,1)}, u32[]{:S(2)}) copy-start(bf16[384,384]{1,0:T(8,128)(2,1)} %slice.80) | copy-start | bytes 884740
  175.4 5.2 %copy-start.16 = (bf16[192,384]{1,0:T(8,128)(2,1)S(1)}, bf16[192,384]{1,0:T(8,128)(2,1)}, u32[]{:S(2)}) copy-start(bf16[192,384]{1,0:T(8,128)(2,1)} %reduce_sum.40) | copy-start | bytes 442372
  175.4 38.8 %all-to-all-start.4 = ((bf16[8,3,96,384]{3,2,1,0:T(8,128)(2,1)}), bf16[8,3,96,384]{3,2,1,0:T(8,128)(2,1)}, u32[]{:S(2)}, u32[]{:S(2)}) async-start(bf16[8,3,96,384]{3,2,1,0:T(8,128)(2,1)} %weight_grads.2), calls=%async_computation.4 | async-start | bytes 3538944 | tf_op jit(solution)/shard_map/all_to_all | solution.py:149
  186.2 8.0 %collective-permute-start.18 = (bf16[192,768]{1,0:T(8,128)(2,1)S(1)}, bf16[192,768]{1,0:T(8,128)(2,1)S(1)}, u32[]{:S(2)}, u32[]{:S(2)}) collective-permute-start(bf16[192,768]{1,0:T(8,128)(2,1)S(1)} %get-tuple-element.72), channel_id=1, source_target_pairs={{0,32},{32,0},{64,96},{96,64},{1,33},{33,1},{65,97},{97,65},{2,34}... | collective-permute-start | bytes 884744 | tf_op jit(solution)/shard_map/ppermute | solution.py:320
  193.0 1.6 collective-permute-start.19
  194.8 18.3 %collective-permute-start.20 = (bf16[192,768]{1,0:T(8,128)(2,1)S(1)}, bf16[192,768]{1,0:T(8,128)(2,1)S(1)}, u32[]{:S(2)}, u32[]{:S(2)}) collective-permute-start(bf16[192,768]{1,0:T(8,128)(2,1)S(1)} %select_convert_fusion), channel_id=1, source_target_pairs={{0,64},{32,96},{64,0},{96,32},{1,65},{33,97},{65,1},{97,33},{2,66}... | collective-permute-start | bytes 884744 | tf_op jit(solution)/shard_map/ppermute | solution.py:325
  (17 other events, 25.7 us)

commit v3 on v2

--- a/solution.py
+++ b/solution.py
@@ -116,19 +116,15 @@
 
 def weights_kernel(*refs):
     xs, gs, o_ref = refs[:NY], refs[NY:-1], refs[-1]
-
-    def store(gs):
-        acc = tn_dot(xs[0][...], rows_of(gs[0]))
-        for y in range(1, NY):
-            acc += tn_dot(xs[y][...], rows_of(gs[y]))
-        o_ref[:, 0] = acc.astype(BF16).reshape(o_ref.shape[0], o_ref.shape[2], o_ref.shape[3])
-
-    if len(gs) == NY:
-        store(gs)
-    else:
-        first = pl.program_id(0) == 0
-        pl.when(first)(lambda: store(gs[:NY]))
-        pl.when(jnp.logical_not(first))(lambda: store(gs[NY:]))
+    acc = None
+    for y in range(NY):
+        g = [gs[y][c] for c in range(gs[y].shape[0])]
+        term = tn_dot(xs[y][...], g[0] if len(g) == 1 else jnp.concatenate(g, axis=1))
+        acc = term if acc is None else acc + term
+    width = o_ref.shape[3]
+    for c in range(o_ref.shape[1]):
+        part = acc[:, c * width : (c + 1) * width].astype(BF16)
+        o_ref[:, c] = part.reshape(o_ref.shape[0], o_ref.shape[2], width)
 
 
 def per_device(inputs, out_grad, qkv_weight, out_weight, text_keys, text_values, text_mask):
@@ -231,6 +227,7 @@
         ]
     )
     x_in = slices_around(in_parts)
+    kv_all, grad_parts = lax.optimization_barrier((kv_all, grad_parts))
     x_grad = slices_around(grad_parts)
     operands = (qg_all, qg_all, *kv_all, *kv_all, tk, tv, mask)
     stats, out_terms = pl.pallas_call(
@@ -282,38 +279,51 @@
     kv_sum = kv_terms[0].astype(F32)
     for by in range(1, NY):
         kv_sum += shift(kv_terms[by], NY - by).astype(F32)
-    dq = jnp.sum(exchange(dq_terms).astype(F32), axis=0).astype(BF16)
+    dq_all = exchange(dq_terms)
     kv = kv_sum[: 2 * rows].astype(BF16).reshape(2, rows, width)
     text_sum = kv_sum[2 * rows :].reshape(2, text_own, 1, width)
-    grad_projected = jnp.concatenate([dq[None], kv])
 
     own = part // NZX
 
-    def weight_grad(xs, gs, more=()):
-        count = 1 + (more[0].shape[0] if more else 0)
-        terms = pl.pallas_call(
+    def weight_terms(xs, gs):
+        count = gs[0].shape[0]
+        return pl.pallas_call(
             weights_kernel,
-            grid=(count,),
-            in_specs=[pl.BlockSpec((rows, part), lambda c: (0, 0))] * NY
-            + [pl.BlockSpec((1, rows, width), lambda c: (0, 0, 0))] * NY
-            + [pl.BlockSpec((1, rows, width), lambda c: (jnp.maximum(c - 1, 0), 0, 0))] * len(more),
-            out_specs=pl.BlockSpec((NZX, 1, own, width), lambda c: (0, c, 0, 0)),
+            grid=(2,),
+            in_specs=[pl.BlockSpec((rows, part // 2), lambda i: (0, i))] * NY
+            + [pl.BlockSpec((count, rows, width), lambda i: (0, 0, 0))] * NY,
+            out_specs=pl.BlockSpec((NZX // 2, count, own, width), lambda i: (i, 0, 0, 0)),
             out_shape=jax.ShapeDtypeStruct((NZX, count, own, width), BF16),
             compiler_params=pltpu.CompilerParams(vmem_limit_bytes=56 * 1024 * 1024),
             name="weight_grads",
-        )(*xs, *gs, *more)
-        return jnp.sum(exchange(terms).astype(F32), axis=0)
+        )(*xs, *gs)
+    def total(array):
+        return jnp.sum(array.astype(F32), axis=0)
 
     outs, kv = lax.optimization_barrier((around(attn_out[None]), kv))
-    out_sum = weight_grad(x_grad, outs)
-    qkv_sum = weight_grad(x_in, around(dq[None]), around(kv))
-
+    out_weights = weight_terms(x_grad, outs)
+    kvs = around(kv)
+    out_weights, first = lax.optimization_barrier((out_weights, kvs[1]))
+    kvs = [kvs[0], first] + kvs[2:]
+    out_received = exchange(out_weights)
+    dq_all, kv = lax.optimization_barrier((dq_all, kv))
+    dq = jnp.sum(dq_all.astype(F32), axis=0).astype(BF16)
+    grad_projected = jnp.concatenate([dq[None], kv])
     terms = jnp.einsum(
         "cvh,sdch->svd",
         grad_projected,
         qkv_weight.reshape(4, part, 3, width),
         preferred_element_type=F32,
     ).astype(BF16)
+    kvs, out_weights, terms = lax.optimization_barrier((kvs, out_weights, terms))
+    kv_weights = weight_terms(x_in, kvs)
+    kv_weights, out_received = lax.optimization_barrier((kv_weights, out_received))
+    kv_received = exchange(kv_weights)
+
+    dqs, kv_weights = lax.optimization_barrier((around(dq[None]), kv_weights))
+    q_weights = weight_terms(x_in, dqs)
+    q_weights, kv_received = lax.optimization_barrier((q_weights, kv_received))
+    qkv_sum = jnp.concatenate([total(exchange(q_weights)), total(kv_received)])
     keep = [jnp.where(core == 0, terms[2 * z], terms[2 * z + 1]) for z in range(2)]
     give = [jnp.where(core == 0, terms[2 * z + 1], terms[2 * z]) for z in range(2)]
     pair = [
@@ -327,7 +337,7 @@
     return (
         grad_inputs[:, None],
         jnp.transpose(qkv_sum, (1, 0, 2)),
-        out_sum[0],
+        total(out_received)[0],
         text_sum[0],
         text_sum[1],
     )

time: 218 us -> 208 us (0.954)
  waiting for transfers between devices: 54.1 us -> 32.5 us
  starting transfers between devices: 69.9 us -> 76.2 us
  other arithmetic: 15.2 us -> 18.4 us
    ppermute x21, waiting for transfers between devices: 31.5 us -> 13 us  [shift(): lax.ppermute(array, 'blk', [(i, (i + by * NZX) % (NY * NZX)) for i in ran...]
    ppermute x1, waiting for transfers between devices: 11.1 us -> 0.01 us  [per_device(): lax.ppermute(other, 'head', z_swap).astype(F32)]
    all_to_all x5 -> x6, waiting for transfers between devices: 2.7 us -> 12.1 us  [exchange(): lax.all_to_all(array, 'blk', 0, 0, tiled=True, axis_index_groups=along_zx)]
    all_to_all x5 -> x6, starting transfers between devices: 21.8 us -> 26.5 us  [exchange(): lax.all_to_all(array, 'blk', 0, 0, tiled=True, axis_index_groups=along_zx)]
    ppermute x21, starting transfers between devices: 27.2 us -> 30.5 us  [shift(): lax.ppermute(array, 'blk', [(i, (i + by * NZX) % (NY * NZX)) for i in ran...]
    pallas_call x2 -> x3, Pallas kernels: 9.18 us -> 10.9 us  [weight_terms(): pl.pallas_call(weights_kernel, grid=(2,), in_specs=[pl.BlockSpec((rows, p...]
    select_n x4 -> x3, other arithmetic: 7.13 us -> 6.45 us  [slice_for(): jnp.where(y < 2, jnp.where(y == 0, parts[0], parts[1]), jnp.where(y == 2,...]
    unnamed x62 -> x54, local copies, waits for them, and re-layouts: 5.68 us -> 5.51 us
  transfers between devices with their start and end apart: 35 -> 36, of which waited for: 15 -> 11; matrix products, arithmetic and copies ran while one was open for 14% -> 16% of each run, Pallas kernels for 17% -> 19%
where the time goes in v3:
time: 208 us; the launch traced here: 206 us
  starting transfers between devices  76.2 us (37%)
  Pallas kernels  39.3 us (19%)
  waiting for transfers between devices  32.5 us (16%)
  other arithmetic  18.4 us (9%)
  matrix products  14.1 us (7%)
  blocking collectives  13.1 us (6%)
  local copies, waits for them, and re-layouts  11.9 us (6%)
    ppermute x21, starting transfers between devices, shift(): lax.ppermute(array, 'blk', [(i, (i + by * NZX) % (NY * NZX)) for i in ran...  30.5 us
    all_to_all x6, starting transfers between devices, exchange(): lax.all_to_all(array, 'blk', 0, 0, tiled=True, axis_index_groups=along_zx)  26.5 us
    pallas_call x1, Pallas kernels, per_device(): pl.pallas_call(grads_kernel, grid=grid, in_specs=in_specs + [pl.BlockSpec...  14.5 us
    all_to_all x1, blocking collectives, exchange(): lax.all_to_all(array, 'blk', 0, 0, tiled=True, axis_index_groups=along_zx)  13.1 us
    ppermute x21, waiting for transfers between devices, shift(): lax.ppermute(array, 'blk', [(i, (i + by * NZX) % (NY * NZX)) for i in ran...  13 us
    all_to_all x6, waiting for transfers between devices, exchange(): lax.all_to_all(array, 'blk', 0, 0, tiled=True, axis_index_groups=along_zx)  12.1 us
    pallas_call x3, Pallas kernels, weight_terms(): pl.pallas_call(weights_kernel, grid=(2,), in_specs=[pl.BlockSpec((rows, p...  10.9 us
    pallas_call x1, Pallas kernels, per_device(): pl.pallas_call(stats_kernel, grid=grid, in_specs=in_specs, out_specs=[pl....  10.5 us
  transfers between devices with their start and end apart: 36, of which 11 were waited for; matrix products, arithmetic and copies ran while one was open for 16% of the time, Pallas kernels for 19%

profile of v3, /device:TPU:1, one launch (start us, length us, event | category | flops | bytes accessed | tf_op | source)
XLA Modules:
  0.0 206.5 jit_solution(9654779025201559149)
XLA Ops:
  0.6 4.5 %collective-permute-start.2 = (bf16[192,768]{1,0:T(8,128)(2,1)}, bf16[192,768]{1,0:T(8,128)(2,1)S(1)}, u32[]{:S(2)}, u32[]{:S(2)}) collective-permute-start(bf16[192,768]{1,0:T(8,128)(2,1)} %bitcast.80), channel_id=1, source_target_pairs={{0,64},{32,96},{64,0},{96,32},{1,65},{33,97},{65,1},{97,33},{2,66}... | collective-permute-start | bytes 884744 | tf_op jit(solution)/shard_map/ppermute | solution.py:180
  6.1 6.0 %collective-permute-done.2 = bf16[192,768]{1,0:T(8,128)(2,1)S(1)} collective-permute-done((bf16[192,768]{1,0:T(8,128)(2,1)}, bf16[192,768]{1,0:T(8,128)(2,1)S(1)}, u32[]{:S(2)}, u32[]{:S(2)}) %collective-permute-start.2) | collective-permute-done | bytes 294944 | tf_op jit(solution)/shard_map/ppermute | solution.py:180
  13.3 3.0 %collective-permute-start = (bf16[192,768]{1,0:T(8,128)(2,1)}, bf16[192,768]{1,0:T(8,128)(2,1)}, u32[]{:S(2)}, u32[]{:S(2)}) collective-permute-start(bf16[192,768]{1,0:T(8,128)(2,1)} %bitcast.83), channel_id=1, source_target_pairs={{0,64},{32,96},{64,0},{96,32},{1,65},{33,97},{65,1},{97,33},{2,66}... | collective-permute-start | bytes 884744 | tf_op jit(solution)/shard_map/ppermute | solution.py:181
  16.3 1.8 select_select_fusion.4
  18.1 5.1 %fusion.1 = bf16[3,192,384]{2,1,0:T(8,128)(2,1)S(1)} fusion(bf16[3072,3,384]{2,0,1:T(8,128)(2,1)} %param.9, bf16[192,768]{1,0:T(8,128)(2,1)S(1)} %get-tuple-element.115, bf16[192,768]{1,0:T(8,128)(2,1)S(1)} %get-tuple-element.114, bf16[192,768]{1,0:T(8,128)(2,1)S(1)} %get-tuple-element.113, bf16[192,768]{1,0:T(8,128)(2,1)S(1)} %get-tuple-element.112), kind=kOutput, calls=%fused_computation.4 | convolution fusion | flops 1363894272 | bytes 8699904 | tf_op jit(solution)/shard_map/vd,dch->cvh/dot_general | solution.py:183
  23.2 1.3 collective-permute-start.5
  24.6 1.4 collective-permute-done.5
  28.2 1.8 broadcast_in_dim.40
  30.0 4.7 %all-to-all-start = ((bf16[8,2,192,384]{3,2,1,0:T(8,128)(2,1)}), bf16[8,2,192,384]{3,2,1,0:T(8,128)(2,1)}, u32[]{:S(2)}, u32[]{:S(2)}) async-start(bf16[8,2,192,384]{3,2,1,0:T(8,128)(2,1)} %broadcast_in_dim.40), calls=%async_computation | async-start | bytes 4718592 | tf_op jit(solution)/shard_map/all_to_all | solution.py:145
  34.9 1.4 collective-permute-start.6
  36.2 2.6 %collective-permute-start.7 = (bf16[2,192,384]{2,1,0:T(8,128)(2,1)S(1)}, bf16[2,192,384]{2,1,0:T(8,128)(2,1)S(1)}, u32[]{:S(2)}, u32[]{:S(2)}) collective-permute-start(bf16[2,192,384]{2,1,0:T(8,128)(2,1)S(1)} %slice.38.refs_0_.refs_4_), channel_id=1, source_target_pairs={{0,16},{1,17},{2,18},{3,19},{4,20},{5,21},{6,22},{7,23},{8,24},{9,... | collective-permute-start | bytes 884744 | tf_op jit(solution)/shard_map/ppermute | solution.py:151
  39.9 2.1 select_select_fusion.5
  42.4 1.7 convolution_convert_fusion.2.refs_8_
  44.9 1.6 collective-permute-start.11
  46.5 5.2 %collective-permute-done.7.refs_2_.refs_6_ = bf16[2,192,384]{2,1,0:T(8,128)(2,1)S(1)} collective-permute-done((bf16[2,192,384]{2,1,0:T(8,128)(2,1)S(1)}, bf16[2,192,384]{2,1,0:T(8,128)(2,1)S(1)}, u32[]{:S(2)}, u32[]{:S(2)}) %collective-permute-start.7) | collective-permute-done | bytes 294944 | tf_op jit(solution)/shard_map/ppermute | solution.py:151
  51.7 2.6 %select_select_fusion = (bf16[192,768]{1,0:T(8,128)(2,1)}, bf16[192,768]{1,0:T(8,128)(2,1)}, bf16[192,768]{1,0:T(8,128)(2,1)}, bf16[192,768]{1,0:T(8,128)(2,1)}) fusion(bf16[192,768]{1,0:T(8,128)(2,1)} %copy-done.15, bf16[192,768]{1,0:T(8,128)(2,1)} %copy-done.14, bf16[192,768]{1,0:T(8,128)(2,1)} %copy-done.13, bf16[192,768]{1,0:T(8,128)(2,1)} %copy-done.16, ...), kind=kLoop, calls=%fused_computation.41 | loop fusion | flops 1769472 | bytes 2359308 | tf_op jit(solution)/shard_map/jit(_where)/select_n | solution.py:173
  55.4 4.0 %collective-permute-start.13 = (bf16[192,768]{1,0:T(8,128)(2,1)}, bf16[192,768]{1,0:T(8,128)(2,1)}, u32[]{:S(2)}, u32[]{:S(2)}) collective-permute-start(bf16[192,768]{1,0:T(8,128)(2,1)} %get-tuple-element.119), channel_id=1, source_target_pairs={{0,16},{1,17},{2,18},{3,19},{4,20},{5,21},{6,22},{7,23},{8,24},{9,... | collective-permute-start | bytes 884744 | tf_op jit(solution)/shard_map/ppermute | solution.py:151
  60.4 4.3 %all-to-all-done.q_ref.g_ref = bf16[8,2,192,384]{3,2,1,0:T(8,128)(2,1)} async-done(((bf16[8,2,192,384]{3,2,1,0:T(8,128)(2,1)}), bf16[8,2,192,384]{3,2,1,0:T(8,128)(2,1)}, u32[]{:S(2)}, u32[]{:S(2)}) %all-to-all-start) | async-done | bytes 2359328 | tf_op jit(solution)/shard_map/all_to_all | solution.py:145
  65.4 10.5 %attention_stats.1 = (f32[3,2,1536]{2,1,0:T(2,128)}, bf16[8,192,384]{2,1,0:T(8,128)(2,1)}) custom-call(bf16[8,2,192,384]{3,2,1,0:T(8,128)(2,1)} %all-to-all-done.q_ref.g_ref, bf16[8,2,192,384]{3,2,1,0:T(8,128)(2,1)} %all-to-all-done.q_ref.g_ref, bf16[2,192,384]{2,1,0:T(8,128)(2,1)} %copy-done.1, bf16[2,192,384]{2,1,0:T(8,128)(2,1)} %copy-done.2, ...), custom_call_target="tpu_custom_call" | custom-call | tf_op jit(solution)/shard_map/attention_stats/pallas_call | solution.py:233
  77.9 13.1 %all_to_all.35.refs_11_ = f32[8,3,2,1536]{3,2,1,0:T(2,128)} all-to-all(f32[8,3,2,1536]{3,2,1,0:T(2,128)S(1)} %broadcast_in_dim.44), channel_id=1, replica_groups={{0,1,2,3,4,5,6,7},{8,9,10,11,12,13,14,15},{16,17,18,19,20,21,22,23},{24..., dimensions={0} | all-to-all | bytes 589824 | tf_op jit(solution)/shard_map/all_to_all | solution.py:145
  91.0 3.7 %all-to-all-start.1 = ((bf16[8,192,384]{2,1,0:T(8,128)(2,1)}), bf16[8,192,384]{2,1,0:T(8,128)(2,1)S(1)}, u32[]{:S(2)}, u32[]{:S(2)}) async-start(bf16[8,192,384]{2,1,0:T(8,128)(2,1)} %get-tuple-element.59), calls=%async_computation.1 | async-start | bytes 2359296 | tf_op jit(solution)/shard_map/all_to_all | solution.py:145
  94.8 14.5 %attention_grads.1 = (bf16[8,192,384]{2,1,0:T(8,128)(2,1)}, bf16[400,384]{1,0:T(8,128)(2,1)}, bf16[400,384]{1,0:T(8,128)(2,1)}, bf16[400,384]{1,0:T(8,128)(2,1)}, bf16[400,384]{1,0:T(8,128)(2,1)}) custom-call(bf16[8,2,192,384]{3,2,1,0:T(8,128)(2,1)} %all-to-all-done.q_ref.g_ref, bf16[8,2,192,384]{3,2,1,0:T(8,128)(2,1)} %all-to-all-done.q_ref.g_ref, ...), custom_call_target="tpu_custom_call" | custom-call | tf_op jit(solution)/shard_map/attention_grads/pallas_call | solution.py:266
  109.3 2.5 %all-to-all-done.1.out_ref = bf16[8,192,384]{2,1,0:T(8,128)(2,1)S(1)} async-done(((bf16[8,192,384]{2,1,0:T(8,128)(2,1)}), bf16[8,192,384]{2,1,0:T(8,128)(2,1)S(1)}, u32[]{:S(2)}, u32[]{:S(2)}) %all-to-all-start.1) | async-done | bytes 1179680 | tf_op jit(solution)/shard_map/all_to_all | solution.py:145
  112.8 3.6 %all-to-all-start.3 = ((bf16[8,192,384]{2,1,0:T(8,128)(2,1)}), bf16[8,192,384]{2,1,0:T(8,128)(2,1)S(1)}, u32[]{:S(2)}, u32[]{:S(2)}) async-start(bf16[8,192,384]{2,1,0:T(8,128)(2,1)} %get-tuple-element.81), calls=%async_computation.3 | async-start | bytes 2359296 | tf_op jit(solution)/shard_map/all_to_all | solution.py:145
  117.7 2.7 %collective-permute-start.19 = (bf16[400,384]{1,0:T(8,128)(2,1)}, bf16[400,384]{1,0:T(8,128)(2,1)}, u32[]{:S(2)}, u32[]{:S(2)}) collective-permute-start(bf16[400,384]{1,0:T(8,128)(2,1)} %get-tuple-element.68), channel_id=1, source_target_pairs={{0,16},{1,17},{2,18},{3,19},{4,20},{5,21},{6,22},{7,23},{8,24},{9,... | collective-permute-start | bytes 921608 | tf_op jit(solution)/shard_map/ppermute | solution.py:151
  121.4 1.6 constant_dynamic-slice_fusion.stat_ref
  123.1 3.4 %combine_out.1 = bf16[192,384]{1,0:T(8,128)(2,1)} custom-call(bf16[8,192,384]{2,1,0:T(8,128)(2,1)} %copy-done.5, f32[8,3,2,192]{3,2,1,0:T(2,128)} %constant_dynamic-slice_fusion.stat_ref), custom_call_target="tpu_custom_call" | custom-call | tf_op jit(solution)/shard_map/combine_out/pallas_call | solution.py:252
  127.6 1.6 collective-permute-start.17
  129.2 3.1 %collective-permute-done.19 = bf16[400,384]{1,0:T(8,128)(2,1)} collective-permute-done((bf16[400,384]{1,0:T(8,128)(2,1)}, bf16[400,384]{1,0:T(8,128)(2,1)}, u32[]{:S(2)}, u32[]{:S(2)}) %collective-permute-start.19) | collective-permute-done | bytes 307232 | tf_op jit(solution)/shard_map/ppermute | solution.py:151
  132.3 1.8 collective-permute-done.18
  134.2 1.4 convert_add_fusion
  139.9 3.6 %collective-permute-start.22 = (bf16[2,192,384]{2,1,0:T(8,128)(2,1)}, bf16[2,192,384]{2,1,0:T(8,128)(2,1)}, u32[]{:S(2)}, u32[]{:S(2)}) collective-permute-start(bf16[2,192,384]{2,1,0:T(8,128)(2,1)} %bitcast.9.refs_4_), channel_id=1, source_target_pairs={{0,16},{1,17},{2,18},{3,19},{4,20},{5,21},{6,22},{7,23},{8,24},{9,... | collective-permute-start | bytes 884744 | tf_op jit(solution)/shard_map/ppermute | solution.py:151
  143.6 3.4 %weight_grads.3 = bf16[8,1,96,384]{3,2,1,0:T(8,128)(2,1)} custom-call(bf16[192,768]{1,0:T(8,128)(2,1)} %get-tuple-element.71.refs_0_, bf16[192,768]{1,0:T(8,128)(2,1)} %collective-permute-done.12.refs_1_, bf16[192,768]{1,0:T(8,128)(2,1)} %collective-permute-done.13.refs_2_, bf16[192,768]{1,0:T(8,128)(2,1)} %collective-permute-done.14.refs_3_, ...), custom_call_target="tpu_custom_call" | custom-call | tf_op jit(solution)/shard_map/weight_grads/pallas_call | solution.py:290
  147.8 4.4 %all-to-all-start.4 = ((bf16[8,1,96,384]{3,2,1,0:T(8,128)(2,1)}), bf16[8,1,96,384]{3,2,1,0:T(8,128)(2,1)}, u32[]{:S(2)}, u32[]{:S(2)}) async-start(bf16[8,1,96,384]{3,2,1,0:T(8,128)(2,1)} %weight_grads.3), calls=%async_computation.4 | async-start | bytes 1179648 | tf_op jit(solution)/shard_map/all_to_all | solution.py:145
  152.3 5.7 %fusion = bf16[4,192,768]{2,1,0:T(8,128)(2,1)S(1)} fusion(bf16[4,768,3,384]{3,1,0,2:T(8,128)(2,1)} %bitcast.85, bf16[2,192,384]{2,1,0:T(8,128)(2,1)} %bitcast.9.refs_4_, bf16[1,192,384]{2,1,0:T(8,128)(2,1)} %bitcast.70), kind=kOutput, calls=%fused_computation.2 | convolution fusion | flops 1360429056 | bytes 8699904 | tf_op jit(solution)/shard_map/cvh,sdch->svd/dot_general | solution.py:312
  158.0 4.1 %weight_grads.4 = bf16[8,2,96,384]{3,2,1,0:T(8,128)(2,1)} custom-call(bf16[192,768]{1,0:T(8,128)(2,1)} %get-tuple-element.85.refs_0_, bf16[192,768]{1,0:T(8,128)(2,1)} %collective-permute-done.9.refs_1_, bf16[192,768]{1,0:T(8,128)(2,1)} %copy-done.7, bf16[192,768]{1,0:T(8,128)(2,1)} %collective-permute-done.11.refs_3_, bf16[2,192,384]{2,1,0:T(8,128)(2,1)} %bitcast.9.refs_4_, ...), custom_call_target="tpu_custom_call" | custom-call | tf_op jit(solution)/shard_map/weight_grads/pallas_call | solution.py:290
  162.1 5.2 %all-to-all-start.5 = ((bf16[8,2,96,384]{3,2,1,0:T(8,128)(2,1)}), bf16[8,2,96,384]{3,2,1,0:T(8,128)(2,1)}, u32[]{:S(2)}, u32[]{:S(2)}) async-start(bf16[8,2,96,384]{3,2,1,0:T(8,128)(2,1)} %weight_grads.4), calls=%async_computation.5 | async-start | bytes 2359296 | tf_op jit(solution)/shard_map/all_to_all | solution.py:145
  167.3 4.9 %collective-permute-start.24 = (bf16[192,768]{1,0:T(8,128)(2,1)S(1)}, bf16[192,768]{1,0:T(8,128)(2,1)S(1)}, u32[]{:S(2)}, u32[]{:S(2)}) collective-permute-start(bf16[192,768]{1,0:T(8,128)(2,1)S(1)} %get-tuple-element.117), channel_id=1, source_target_pairs={{0,32},{32,0},{64,96},{96,64},{1,33},{33,1},{65,97},{97,65},{2,34}... | collective-permute-start | bytes 884744 | tf_op jit(solution)/shard_map/ppermute | solution.py:330
  172.3 1.5 collective-permute-start.27
  173.8 2.2 %collective-permute-start.28 = (bf16[1,192,384]{2,1,0:T(8,128)(2,1)}, bf16[1,192,384]{2,1,0:T(8,128)(2,1)S(1)}, u32[]{:S(2)}, u32[]{:S(2)}) collective-permute-start(bf16[1,192,384]{2,1,0:T(8,128)(2,1)} %bitcast.72), channel_id=1, source_target_pairs={{0,16},{1,17},{2,18},{3,19},{4,20},{5,21},{6,22},{7,23},{8,24},{9,... | collective-permute-start | bytes 442376 | tf_op jit(solution)/shard_map/ppermute | solution.py:151
  176.0 1.3 collective-permute-start.29
  179.0 3.3 %collective-permute-start.26 = (bf16[192,768]{1,0:T(8,128)(2,1)}, bf16[192,768]{1,0:T(8,128)(2,1)}, u32[]{:S(2)}, u32[]{:S(2)}) collective-permute-start(bf16[192,768]{1,0:T(8,128)(2,1)} %select_convert_fusion), channel_id=1, source_target_pairs={{0,64},{32,96},{64,0},{96,32},{1,65},{33,97},{65,1},{97,33},{2,66}... | collective-permute-start | bytes 884744 | tf_op jit(solution)/shard_map/ppermute | solution.py:335
  185.6 3.4 %weight_grads.5 = bf16[8,1,96,384]{3,2,1,0:T(8,128)(2,1)} custom-call(bf16[192,768]{1,0:T(8,128)(2,1)} %get-tuple-element.85.refs_0_, bf16[192,768]{1,0:T(8,128)(2,1)} %collective-permute-done.9.refs_1_, bf16[192,768]{1,0:T(8,128)(2,1)} %copy-done.7, bf16[192,768]{1,0:T(8,128)(2,1)} %collective-permute-done.11.refs_3_, bf16[1,192,384]{2,1,0:T(8,128)(2,1)} %bitcast.74, ...), custom_call_target="tpu_custom_call" | custom-call | tf_op jit(solution)/shard_map/weight_grads/pallas_call | solution.py:290
  189.0 4.8 %all-to-all-start.6 = ((bf16[8,1,96,384]{3,2,1,0:T(8,128)(2,1)}), bf16[8,1,96,384]{3,2,1,0:T(8,128)(2,1)}, u32[]{:S(2)}, u32[]{:S(2)}) async-start(bf16[8,1,96,384]{3,2,1,0:T(8,128)(2,1)} %weight_grads.5), calls=%async_computation.6 | async-start | bytes 1179648 | tf_op jit(solution)/shard_map/all_to_all | solution.py:145
  193.8 1.8 convert_reduce_fusion.1
  195.7 2.1 %fusion.26 = bf16[192,1,768]{2,0,1:T(8,128)(2,1)} fusion(bf16[192,768]{1,0:T(8,128)(2,1)} %collective-permute-done.26, bf16[192,768]{1,0:T(8,128)(2,1)} %copy-done.12, bf16[192,768]{1,0:T(8,128)(2,1)} %copy-done.11, pred[]{:T(512)S(6)} %eq.26, bf16[4,192,768]{2,1,0:T(8,128)(2,1)S(1)} %fusion, pred[]{:T(512)S(6)} %eq.27), kind=kLoop, calls=%fused_computation.37 | loop fusion | flops 1769472 | bytes 2359298 | tf_op jit(solution)/shard_map/broadcast_in_dim | solution.py:338
  197.8 1.5 convert_reduce_fusion
  199.2 5.3 %all-to-all-done.6 = bf16[8,1,96,384]{3,2,1,0:T(8,128)(2,1)} async-done(((bf16[8,1,96,384]{3,2,1,0:T(8,128)(2,1)}), bf16[8,1,96,384]{3,2,1,0:T(8,128)(2,1)}, u32[]{:S(2)}, u32[]{:S(2)}) %all-to-all-start.6) | async-done | bytes 589856 | tf_op jit(solution)/shard_map/all_to_all | solution.py:145
  (116 shorter events, 28.5 us)
Async XLA Ops:
  0.6 26.6 %copy-start = (bf16[3072,384]{1,0:T(8,128)(2,1)S(1)}, bf16[3072,384]{1,0:T(8,128)(2,1)}, u32[]{:S(2)}) copy-start(bf16[3072,384]{1,0:T(8,128)(2,1)} %param.10) | copy-start | bytes 7077892
  0.6 11.4 %collective-permute-start.2 = (bf16[192,768]{1,0:T(8,128)(2,1)}, bf16[192,768]{1,0:T(8,128)(2,1)S(1)}, u32[]{:S(2)}, u32[]{:S(2)}) collective-permute-start(bf16[192,768]{1,0:T(8,128)(2,1)} %bitcast.80), channel_id=1, source_target_pairs={{0,64},{32,96},{64,0},{96,32},{1,65},{33,97},{65,1},{97,33},{2,66}... | collective-permute-start | bytes 884744 | tf_op jit(solution)/shard_map/ppermute | solution.py:180
  5.2 11.1 %collective-permute-start.1 = (bf16[192,768]{1,0:T(8,128)(2,1)}, bf16[192,768]{1,0:T(8,128)(2,1)S(1)}, u32[]{:S(2)}, u32[]{:S(2)}) collective-permute-start(bf16[192,768]{1,0:T(8,128)(2,1)} %bitcast.81), channel_id=1, source_target_pairs={{0,32},{32,0},{64,96},{96,64},{1,33},{33,1},{65,97},{97,65},{2,34}... | collective-permute-start | bytes 884744 | tf_op jit(solution)/shard_map/ppermute | solution.py:159
  12.1 4.2 %collective-permute-start.3 = (bf16[192,768]{1,0:T(8,128)(2,1)S(1)}, bf16[192,768]{1,0:T(8,128)(2,1)S(1)}, u32[]{:S(2)}, u32[]{:S(2)}) collective-permute-start(bf16[192,768]{1,0:T(8,128)(2,1)S(1)} %collective-permute-done.2), channel_id=1, source_target_pairs={{0,32},{32,0},{64,96},{96,64},{1,33},{33,1},{65,97},{97,65},{2,34}... | collective-permute-start | bytes 884744 | tf_op jit(solution)/shard_map/ppermute | solution.py:160
  13.3 11.3 %collective-permute-start.4 = (bf16[192,768]{1,0:T(8,128)(2,1)}, bf16[192,768]{1,0:T(8,128)(2,1)}, u32[]{:S(2)}, u32[]{:S(2)}) collective-permute-start(bf16[192,768]{1,0:T(8,128)(2,1)} %bitcast.82), channel_id=1, source_target_pairs={{0,32},{32,0},{64,96},{96,64},{1,33},{33,1},{65,97},{97,65},{2,34}... | collective-permute-start | bytes 884744 | tf_op jit(solution)/shard_map/ppermute | solution.py:159
  13.3 9.9 %collective-permute-start = (bf16[192,768]{1,0:T(8,128)(2,1)}, bf16[192,768]{1,0:T(8,128)(2,1)}, u32[]{:S(2)}, u32[]{:S(2)}) collective-permute-start(bf16[192,768]{1,0:T(8,128)(2,1)} %bitcast.83), channel_id=1, source_target_pairs={{0,64},{32,96},{64,0},{96,32},{1,65},{33,97},{65,1},{97,33},{2,66}... | collective-permute-start | bytes 884744 | tf_op jit(solution)/shard_map/ppermute | solution.py:181
  18.1 5.1 %copy-start.10 = (bf16[192,768]{1,0:T(8,128)(2,1)}, bf16[192,768]{1,0:T(8,128)(2,1)S(1)}, u32[]{:S(2)}) copy-start(bf16[192,768]{1,0:T(8,128)(2,1)S(1)} %get-tuple-element.115) | copy-start | bytes 884740
  18.1 7.9 %copy-start.17 = (bf16[192,1,768]{2,0,1:T(8,128)(2,1)S(1)}, bf16[192,1,768]{2,0,1:T(8,128)(2,1)}, u32[]{:S(2)}) copy-start(bf16[192,1,768]{2,0,1:T(8,128)(2,1)} %param.8) | copy-start | bytes 884740
  23.2 2.8 %collective-permute-start.5 = (bf16[192,768]{1,0:T(8,128)(2,1)}, bf16[192,768]{1,0:T(8,128)(2,1)S(1)}, u32[]{:S(2)}, u32[]{:S(2)}) collective-permute-start(bf16[192,768]{1,0:T(8,128)(2,1)} %collective-permute-done), channel_id=1, source_target_pairs={{0,32},{32,0},{64,96},{96,64},{1,33},{33,1},{65,97},{97,65},{2,34}... | collective-permute-start | bytes 884744 | tf_op jit(solution)/shard_map/ppermute | solution.py:160
  30.0 34.7 %all-to-all-start = ((bf16[8,2,192,384]{3,2,1,0:T(8,128)(2,1)}), bf16[8,2,192,384]{3,2,1,0:T(8,128)(2,1)}, u32[]{:S(2)}, u32[]{:S(2)}) async-start(bf16[8,2,192,384]{3,2,1,0:T(8,128)(2,1)} %broadcast_in_dim.40), calls=%async_computation | async-start | bytes 4718592 | tf_op jit(solution)/shard_map/all_to_all | solution.py:145
  34.8 19.5 %copy-start.1 = (bf16[2,192,384]{2,1,0:T(8,128)(2,1)}, bf16[2,192,384]{2,1,0:T(8,128)(2,1)S(1)}, u32[]{:S(2)}) copy-start(bf16[2,192,384]{2,1,0:T(8,128)(2,1)S(1)} %slice.38.refs_0_.refs_4_) | copy-start | bytes 884740
  34.8 24.6 %copy-start.24 = (s32[256,1]{0,1:T(1,128)S(1)}, s32[256,1]{0,1:T(1,128)}, u32[]{:S(2)}) copy-start(s32[256,1]{0,1:T(1,128)} %param.13) | copy-start | bytes 3076
  34.8 24.8 %copy-start.25 = (bf16[256,1,384]{2,0,1:T(8,128)(2,1)S(1)}, bf16[256,1,384]{2,0,1:T(8,128)(2,1)}, u32[]{:S(2)}) copy-start(bf16[256,1,384]{2,0,1:T(8,128)(2,1)} %param.12) | copy-start | bytes 589828
  34.9 10.0 %collective-permute-start.6 = (bf16[2,192,384]{2,1,0:T(8,128)(2,1)S(1)}, bf16[2,192,384]{2,1,0:T(8,128)(2,1)S(1)}, u32[]{:S(2)}, u32[]{:S(2)}) collective-permute-start(bf16[2,192,384]{2,1,0:T(8,128)(2,1)S(1)} %slice.38.refs_0_.refs_4_), channel_id=1, source_target_pairs={{0,8},{1,9},{2,10},{3,11},{4,12},{5,13},{6,14},{7,15},{8,16},{9,17... | collective-permute-start | bytes 884744 | tf_op jit(solution)/shard_map/ppermute | solution.py:151
  36.2 15.5 %collective-permute-start.7 = (bf16[2,192,384]{2,1,0:T(8,128)(2,1)S(1)}, bf16[2,192,384]{2,1,0:T(8,128)(2,1)S(1)}, u32[]{:S(2)}, u32[]{:S(2)}) collective-permute-start(bf16[2,192,384]{2,1,0:T(8,128)(2,1)S(1)} %slice.38.refs_0_.refs_4_), channel_id=1, source_target_pairs={{0,16},{1,17},{2,18},{3,19},{4,20},{5,21},{6,22},{7,23},{8,24},{9,... | collective-permute-start | bytes 884744 | tf_op jit(solution)/shard_map/ppermute | solution.py:151
  38.8 12.9 %collective-permute-start.8 = (bf16[2,192,384]{2,1,0:T(8,128)(2,1)S(1)}, bf16[2,192,384]{2,1,0:T(8,128)(2,1)S(1)}, u32[]{:S(2)}, u32[]{:S(2)}) collective-permute-start(bf16[2,192,384]{2,1,0:T(8,128)(2,1)S(1)} %slice.38.refs_0_.refs_4_), channel_id=1, source_target_pairs={{0,24},{1,25},{2,26},{3,27},{4,28},{5,29},{6,30},{7,31},{8,0},{9,1... | collective-permute-start | bytes 884744 | tf_op jit(solution)/shard_map/ppermute | solution.py:151
  42.0 17.4 %collective-permute-start.9 = (bf16[192,768]{1,0:T(8,128)(2,1)S(1)}, bf16[192,768]{1,0:T(8,128)(2,1)}, u32[]{:S(2)}, u32[]{:S(2)}) collective-permute-start(bf16[192,768]{1,0:T(8,128)(2,1)S(1)} %get-tuple-element.123), channel_id=1, source_target_pairs={{0,8},{1,9},{2,10},{3,11},{4,12},{5,13},{6,14},{7,15},{8,16},{9,17... | collective-permute-start | bytes 884744 | tf_op jit(solution)/shard_map/ppermute | solution.py:151
  44.1 31.8 %collective-permute-start.10 = (bf16[192,768]{1,0:T(8,128)(2,1)}, bf16[192,768]{1,0:T(8,128)(2,1)S(1)}, u32[]{:S(2)}, u32[]{:S(2)}) collective-permute-start(bf16[192,768]{1,0:T(8,128)(2,1)} %get-tuple-element.122), channel_id=1, source_target_pairs={{0,16},{1,17},{2,18},{3,19},{4,20},{5,21},{6,22},{7,23},{8,24},{9,... | collective-permute-start | bytes 884744 | tf_op jit(solution)/shard_map/ppermute | solution.py:151
  44.9 20.5 %copy-start.2 = (bf16[2,192,384]{2,1,0:T(8,128)(2,1)}, bf16[2,192,384]{2,1,0:T(8,128)(2,1)S(1)}, u32[]{:S(2)}) copy-start(bf16[2,192,384]{2,1,0:T(8,128)(2,1)S(1)} %collective-permute-done.6.refs_1_.refs_5_) | copy-start | bytes 884740
  44.9 31.1 %collective-permute-start.11 = (bf16[192,768]{1,0:T(8,128)(2,1)}, bf16[192,768]{1,0:T(8,128)(2,1)}, u32[]{:S(2)}, u32[]{:S(2)}) collective-permute-start(bf16[192,768]{1,0:T(8,128)(2,1)} %get-tuple-element.111), channel_id=1, source_target_pairs={{0,24},{1,25},{2,26},{3,27},{4,28},{5,29},{6,30},{7,31},{8,0},{9,1... | collective-permute-start | bytes 884744 | tf_op jit(solution)/shard_map/ppermute | solution.py:151
  51.7 13.7 %copy-start.3 = (bf16[2,192,384]{2,1,0:T(8,128)(2,1)}, bf16[2,192,384]{2,1,0:T(8,128)(2,1)S(1)}, u32[]{:S(2)}) copy-start(bf16[2,192,384]{2,1,0:T(8,128)(2,1)S(1)} %collective-permute-done.7.refs_2_.refs_6_) | copy-start | bytes 884740
  51.7 13.7 %copy-start.4 = (bf16[2,192,384]{2,1,0:T(8,128)(2,1)}, bf16[2,192,384]{2,1,0:T(8,128)(2,1)S(1)}, u32[]{:S(2)}) copy-start(bf16[2,192,384]{2,1,0:T(8,128)(2,1)S(1)} %collective-permute-done.8.refs_3_.refs_7_) | copy-start | bytes 884740
  54.3 21.6 %collective-permute-start.12 = (bf16[192,768]{1,0:T(8,128)(2,1)}, bf16[192,768]{1,0:T(8,128)(2,1)}, u32[]{:S(2)}, u32[]{:S(2)}) collective-permute-start(bf16[192,768]{1,0:T(8,128)(2,1)} %get-tuple-element.120), channel_id=1, source_target_pairs={{0,8},{1,9},{2,10},{3,11},{4,12},{5,13},{6,14},{7,15},{8,16},{9,17... | collective-permute-start | bytes 884744 | tf_op jit(solution)/shard_map/ppermute | solution.py:151
  55.4 21.7 %collective-permute-start.13 = (bf16[192,768]{1,0:T(8,128)(2,1)}, bf16[192,768]{1,0:T(8,128)(2,1)}, u32[]{:S(2)}, u32[]{:S(2)}) collective-permute-start(bf16[192,768]{1,0:T(8,128)(2,1)} %get-tuple-element.119), channel_id=1, source_target_pairs={{0,16},{1,17},{2,18},{3,19},{4,20},{5,21},{6,22},{7,23},{8,24},{9,... | collective-permute-start | bytes 884744 | tf_op jit(solution)/shard_map/ppermute | solution.py:151
  59.4 17.7 %collective-permute-start.14 = (bf16[192,768]{1,0:T(8,128)(2,1)}, bf16[192,768]{1,0:T(8,128)(2,1)}, u32[]{:S(2)}, u32[]{:S(2)}) collective-permute-start(bf16[192,768]{1,0:T(8,128)(2,1)} %get-tuple-element.118), channel_id=1, source_target_pairs={{0,24},{1,25},{2,26},{3,27},{4,28},{5,29},{6,30},{7,31},{8,0},{9,1... | collective-permute-start | bytes 884744 | tf_op jit(solution)/shard_map/ppermute | solution.py:151
  76.0 15.1 %copy-start.7 = (bf16[192,768]{1,0:T(8,128)(2,1)}, bf16[192,768]{1,0:T(8,128)(2,1)S(1)}, u32[]{:S(2)}) copy-start(bf16[192,768]{1,0:T(8,128)(2,1)S(1)} %collective-permute-done.10.refs_2_) | copy-start | bytes 884740
  91.0 20.7 %all-to-all-start.1 = ((bf16[8,192,384]{2,1,0:T(8,128)(2,1)}), bf16[8,192,384]{2,1,0:T(8,128)(2,1)S(1)}, u32[]{:S(2)}, u32[]{:S(2)}) async-start(bf16[8,192,384]{2,1,0:T(8,128)(2,1)} %get-tuple-element.59), calls=%async_computation.1 | async-start | bytes 2359296 | tf_op jit(solution)/shard_map/all_to_all | solution.py:145
  112.8 34.2 %all-to-all-start.3 = ((bf16[8,192,384]{2,1,0:T(8,128)(2,1)}), bf16[8,192,384]{2,1,0:T(8,128)(2,1)S(1)}, u32[]{:S(2)}, u32[]{:S(2)}) async-start(bf16[8,192,384]{2,1,0:T(8,128)(2,1)} %get-tuple-element.81), calls=%async_computation.3 | async-start | bytes 2359296 | tf_op jit(solution)/shard_map/all_to_all | solution.py:145
  116.4 11.2 %collective-permute-start.20 = (bf16[400,384]{1,0:T(8,128)(2,1)}, bf16[400,384]{1,0:T(8,128)(2,1)}, u32[]{:S(2)}, u32[]{:S(2)}) collective-permute-start(bf16[400,384]{1,0:T(8,128)(2,1)} %get-tuple-element.69), channel_id=1, source_target_pairs={{0,8},{1,9},{2,10},{3,11},{4,12},{5,13},{6,14},{7,15},{8,16},{9,17... | collective-permute-start | bytes 921608 | tf_op jit(solution)/shard_map/ppermute | solution.py:151
  117.7 14.6 %collective-permute-start.19 = (bf16[400,384]{1,0:T(8,128)(2,1)}, bf16[400,384]{1,0:T(8,128)(2,1)}, u32[]{:S(2)}, u32[]{:S(2)}) collective-permute-start(bf16[400,384]{1,0:T(8,128)(2,1)} %get-tuple-element.68), channel_id=1, source_target_pairs={{0,16},{1,17},{2,18},{3,19},{4,20},{5,21},{6,22},{7,23},{8,24},{9,... | collective-permute-start | bytes 921608 | tf_op jit(solution)/shard_map/ppermute | solution.py:151
  120.4 13.8 %collective-permute-start.18 = (bf16[400,384]{1,0:T(8,128)(2,1)}, bf16[400,384]{1,0:T(8,128)(2,1)}, u32[]{:S(2)}, u32[]{:S(2)}) collective-permute-start(bf16[400,384]{1,0:T(8,128)(2,1)} %get-tuple-element.67), channel_id=1, source_target_pairs={{0,24},{1,25},{2,26},{3,27},{4,28},{5,29},{6,30},{7,31},{8,0},{9,1... | collective-permute-start | bytes 921608 | tf_op jit(solution)/shard_map/ppermute | solution.py:151
  126.4 10.7 %collective-permute-start.15 = (bf16[1,192,384]{2,1,0:T(8,128)(2,1)}, bf16[1,192,384]{2,1,0:T(8,128)(2,1)S(1)}, u32[]{:S(2)}, u32[]{:S(2)}) collective-permute-start(bf16[1,192,384]{2,1,0:T(8,128)(2,1)} %bitcast.75), channel_id=1, source_target_pairs={{0,8},{1,9},{2,10},{3,11},{4,12},{5,13},{6,14},{7,15},{8,16},{9,17... | collective-permute-start | bytes 442376 | tf_op jit(solution)/shard_map/ppermute | solution.py:151
  126.8 11.4 %collective-permute-start.16 = (bf16[1,192,384]{2,1,0:T(8,128)(2,1)}, bf16[1,192,384]{2,1,0:T(8,128)(2,1)S(1)}, u32[]{:S(2)}, u32[]{:S(2)}) collective-permute-start(bf16[1,192,384]{2,1,0:T(8,128)(2,1)} %bitcast.76), channel_id=1, source_target_pairs={{0,16},{1,17},{2,18},{3,19},{4,20},{5,21},{6,22},{7,23},{8,24},{9,... | collective-permute-start | bytes 442376 | tf_op jit(solution)/shard_map/ppermute | solution.py:151
  127.6 11.3 %collective-permute-start.17 = (bf16[1,192,384]{2,1,0:T(8,128)(2,1)}, bf16[1,192,384]{2,1,0:T(8,128)(2,1)S(1)}, u32[]{:S(2)}, u32[]{:S(2)}) collective-permute-start(bf16[1,192,384]{2,1,0:T(8,128)(2,1)} %bitcast.77), channel_id=1, source_target_pairs={{0,24},{1,25},{2,26},{3,27},{4,28},{5,29},{6,30},{7,31},{8,0},{9,1... | collective-permute-start | bytes 442376 | tf_op jit(solution)/shard_map/ppermute | solution.py:151
  137.2 6.4 %copy-start.18 = (bf16[1,192,384]{2,1,0:T(8,128)(2,1)}, bf16[1,192,384]{2,1,0:T(8,128)(2,1)S(1)}, u32[]{:S(2)}) copy-start(bf16[1,192,384]{2,1,0:T(8,128)(2,1)S(1)} %collective-permute-done.15.refs_5_) | copy-start | bytes 442372
  138.3 5.3 %copy-start.19 = (bf16[1,192,384]{2,1,0:T(8,128)(2,1)}, bf16[1,192,384]{2,1,0:T(8,128)(2,1)S(1)}, u32[]{:S(2)}) copy-start(bf16[1,192,384]{2,1,0:T(8,128)(2,1)S(1)} %collective-permute-done.16.refs_6_) | copy-start | bytes 442372
  138.9 8.9 %collective-permute-start.21 = (bf16[2,192,384]{2,1,0:T(8,128)(2,1)}, bf16[2,192,384]{2,1,0:T(8,128)(2,1)}, u32[]{:S(2)}, u32[]{:S(2)}) collective-permute-start(bf16[2,192,384]{2,1,0:T(8,128)(2,1)} %bitcast.9.refs_4_), channel_id=1, source_target_pairs={{0,8},{1,9},{2,10},{3,11},{4,12},{5,13},{6,14},{7,15},{8,16},{9,17... | collective-permute-start | bytes 884744 | tf_op jit(solution)/shard_map/ppermute | solution.py:151
  139.9 18.0 %collective-permute-start.22 = (bf16[2,192,384]{2,1,0:T(8,128)(2,1)}, bf16[2,192,384]{2,1,0:T(8,128)(2,1)}, u32[]{:S(2)}, u32[]{:S(2)}) collective-permute-start(bf16[2,192,384]{2,1,0:T(8,128)(2,1)} %bitcast.9.refs_4_), channel_id=1, source_target_pairs={{0,16},{1,17},{2,18},{3,19},{4,20},{5,21},{6,22},{7,23},{8,24},{9,... | collective-permute-start | bytes 884744 | tf_op jit(solution)/shard_map/ppermute | solution.py:151
  143.6 14.4 %collective-permute-start.23 = (bf16[2,192,384]{2,1,0:T(8,128)(2,1)}, bf16[2,192,384]{2,1,0:T(8,128)(2,1)}, u32[]{:S(2)}, u32[]{:S(2)}) collective-permute-start(bf16[2,192,384]{2,1,0:T(8,128)(2,1)} %bitcast.9.refs_4_), channel_id=1, source_target_pairs={{0,24},{1,25},{2,26},{3,27},{4,28},{5,29},{6,30},{7,31},{8,0},{9,1... | collective-permute-start | bytes 884744 | tf_op jit(solution)/shard_map/ppermute | solution.py:151
  147.8 14.2 %all-to-all-start.4 = ((bf16[8,1,96,384]{3,2,1,0:T(8,128)(2,1)}), bf16[8,1,96,384]{3,2,1,0:T(8,128)(2,1)}, u32[]{:S(2)}, u32[]{:S(2)}) async-start(bf16[8,1,96,384]{3,2,1,0:T(8,128)(2,1)} %weight_grads.3), calls=%async_computation.4 | async-start | bytes 1179648 | tf_op jit(solution)/shard_map/all_to_all | solution.py:145
  162.1 26.9 %all-to-all-start.5 = ((bf16[8,2,96,384]{3,2,1,0:T(8,128)(2,1)}), bf16[8,2,96,384]{3,2,1,0:T(8,128)(2,1)}, u32[]{:S(2)}, u32[]{:S(2)}) async-start(bf16[8,2,96,384]{3,2,1,0:T(8,128)(2,1)} %weight_grads.4), calls=%async_computation.5 | async-start | bytes 2359296 | tf_op jit(solution)/shard_map/all_to_all | solution.py:145
  167.3 10.0 %collective-permute-start.24 = (bf16[192,768]{1,0:T(8,128)(2,1)S(1)}, bf16[192,768]{1,0:T(8,128)(2,1)S(1)}, u32[]{:S(2)}, u32[]{:S(2)}) collective-permute-start(bf16[192,768]{1,0:T(8,128)(2,1)S(1)} %get-tuple-element.117), channel_id=1, source_target_pairs={{0,32},{32,0},{64,96},{96,64},{1,33},{33,1},{65,97},{97,65},{2,34}... | collective-permute-start | bytes 884744 | tf_op jit(solution)/shard_map/ppermute | solution.py:330
  172.2 5.2 %collective-permute-start.25 = (bf16[192,768]{1,0:T(8,128)(2,1)S(1)}, bf16[192,768]{1,0:T(8,128)(2,1)S(1)}, u32[]{:S(2)}, u32[]{:S(2)}) collective-permute-start(bf16[192,768]{1,0:T(8,128)(2,1)S(1)} %get-tuple-element.116), channel_id=1, source_target_pairs={{0,32},{32,0},{64,96},{96,64},{1,33},{33,1},{65,97},{97,65},{2,34}... | collective-permute-start | bytes 884744 | tf_op jit(solution)/shard_map/ppermute | solution.py:330
  172.3 12.0 %collective-permute-start.27 = (bf16[1,192,384]{2,1,0:T(8,128)(2,1)}, bf16[1,192,384]{2,1,0:T(8,128)(2,1)S(1)}, u32[]{:S(2)}, u32[]{:S(2)}) collective-permute-start(bf16[1,192,384]{2,1,0:T(8,128)(2,1)} %bitcast.71), channel_id=1, source_target_pairs={{0,8},{1,9},{2,10},{3,11},{4,12},{5,13},{6,14},{7,15},{8,16},{9,17... | collective-permute-start | bytes 442376 | tf_op jit(solution)/shard_map/ppermute | solution.py:151
  173.8 10.5 %collective-permute-start.28 = (bf16[1,192,384]{2,1,0:T(8,128)(2,1)}, bf16[1,192,384]{2,1,0:T(8,128)(2,1)S(1)}, u32[]{:S(2)}, u32[]{:S(2)}) collective-permute-start(bf16[1,192,384]{2,1,0:T(8,128)(2,1)} %bitcast.72), channel_id=1, source_target_pairs={{0,16},{1,17},{2,18},{3,19},{4,20},{5,21},{6,22},{7,23},{8,24},{9,... | collective-permute-start | bytes 442376 | tf_op jit(solution)/shard_map/ppermute | solution.py:151
  176.0 8.3 %collective-permute-start.29 = (bf16[1,192,384]{2,1,0:T(8,128)(2,1)}, bf16[1,192,384]{2,1,0:T(8,128)(2,1)S(1)}, u32[]{:S(2)}, u32[]{:S(2)}) collective-permute-start(bf16[1,192,384]{2,1,0:T(8,128)(2,1)} %bitcast.73), channel_id=1, source_target_pairs={{0,24},{1,25},{2,26},{3,27},{4,28},{5,29},{6,30},{7,31},{8,0},{9,1... | collective-permute-start | bytes 442376 | tf_op jit(solution)/shard_map/ppermute | solution.py:151
  179.0 16.7 %collective-permute-start.26 = (bf16[192,768]{1,0:T(8,128)(2,1)}, bf16[192,768]{1,0:T(8,128)(2,1)}, u32[]{:S(2)}, u32[]{:S(2)}) collective-permute-start(bf16[192,768]{1,0:T(8,128)(2,1)} %select_convert_fusion), channel_id=1, source_target_pairs={{0,64},{32,96},{64,0},{96,32},{1,65},{33,97},{65,1},{97,33},{2,66}... | collective-permute-start | bytes 884744 | tf_op jit(solution)/shard_map/ppermute | solution.py:335
  189.0 15.5 %all-to-all-start.6 = ((bf16[8,1,96,384]{3,2,1,0:T(8,128)(2,1)}), bf16[8,1,96,384]{3,2,1,0:T(8,128)(2,1)}, u32[]{:S(2)}, u32[]{:S(2)}) async-start(bf16[8,1,96,384]{3,2,1,0:T(8,128)(2,1)} %weight_grads.5), calls=%async_computation.6 | async-start | bytes 1179648 | tf_op jit(solution)/shard_map/all_to_all | solution.py:145
  (14 other events, 24.1 us)

commit v4 on v3

--- a/solution.py
+++ b/solution.py
@@ -81,8 +81,7 @@
 def grads_kernel(q_ref, g_ref, *refs):
     ks, vs = refs[:NY], refs[NY : 2 * NY]
     tk_ref, tv_ref, mask_ref, stat_ref, dq_ref = refs[2 * NY : 2 * NY + 5]
-    kv_refs, acc_ref = refs[2 * NY + 5 : -1], refs[-1]
-    step, steps = pl.program_id(1), pl.num_programs(1)
+    kv_refs = refs[2 * NY + 5 :]
     q, g = rows_of(q_ref), rows_of(g_ref)
     k, v = pick(ks, tk_ref[...]), pick(vs, tv_ref[...])
     keys = k.shape[0] - tk_ref.shape[0]
@@ -93,25 +92,15 @@
     dq = tn_dot(k, ds) * HD**-0.5
     dq_ref[...] = dq.T.astype(BF16).reshape(dq_ref.shape)
 
-    @pl.when(step == 0)
-    def _():
-        acc_ref[...] = jnp.zeros_like(acc_ref)
-
-    acc_ref[0] += nn_dot(ds, q)
-    acc_ref[1] += nn_dot(p.astype(BF16), g)
-
-    @pl.when(step == steps - 1)
-    def _():
-        per = keys // NY
-        text = (acc_ref.shape[1] - keys) // NY
-        for y in range(NY):
-            kv_ref = kv_refs[y]
-            kv_ref[:per] = (acc_ref[0, y * per : (y + 1) * per] * HD**-0.5).astype(BF16)
-            kv_ref[per : 2 * per] = acc_ref[1, y * per : (y + 1) * per].astype(BF16)
-            at = keys + y * text
-            kv_ref[2 * per :] = jnp.concatenate(
-                [acc_ref[0, at : at + text] * HD**-0.5, acc_ref[1, at : at + text]], axis=0
-            ).astype(BF16)
+    dk = nn_dot(ds, q) * HD**-0.5
+    dv = nn_dot(p.astype(BF16), g)
+    per = keys // NY
+    text = (dk.shape[0] - keys) // NY
+    for y in range(NY):
+        own, at = slice(y * per, (y + 1) * per), slice(keys + y * text, keys + (y + 1) * text)
+        kv_refs[y][:per] = dk[own].astype(BF16)
+        kv_refs[y][per : 2 * per] = dv[own].astype(BF16)
+        kv_refs[y][2 * per :] = jnp.concatenate([dk[at], dv[at]], axis=0).astype(BF16)
 
 
 def weights_kernel(*refs):
@@ -206,24 +195,22 @@
     mask = jnp.sum(jnp.where(chosen, text_mask[:, 0][None, :], 0), axis=1, keepdims=True)
     mask = jnp.broadcast_to(mask, (text_per, HD))
 
-    half = NZX // 2
-    q_rows = half * rows
-    steps = NZX // half
-    grid = (heads, steps)
+    q_rows = NZX * rows
+    grid = (heads,)
     params = pltpu.CompilerParams(
-        vmem_limit_bytes=56 * 1024 * 1024, dimension_semantics=("arbitrary", "arbitrary")
+        vmem_limit_bytes=56 * 1024 * 1024, dimension_semantics=("arbitrary",)
     )
     in_specs = (
         [
-            pl.BlockSpec((half, 1, rows, HD), lambda h, i: (i, 0, 0, h)),
-            pl.BlockSpec((half, 1, rows, HD), lambda h, i: (i, 1, 0, h)),
+            pl.BlockSpec((NZX, 1, rows, HD), lambda h: (0, 0, 0, h)),
+            pl.BlockSpec((NZX, 1, rows, HD), lambda h: (0, 1, 0, h)),
         ]
-        + [pl.BlockSpec((1, rows, HD), lambda h, i: (0, 0, h))] * NY
-        + [pl.BlockSpec((1, rows, HD), lambda h, i: (1, 0, h))] * NY
+        + [pl.BlockSpec((1, rows, HD), lambda h: (0, 0, h))] * NY
+        + [pl.BlockSpec((1, rows, HD), lambda h: (1, 0, h))] * NY
         + [
-            pl.BlockSpec((text_per, HD), lambda h, i: (0, h)),
-            pl.BlockSpec((text_per, HD), lambda h, i: (0, h)),
-            pl.BlockSpec((text_per, HD), lambda h, i: (0, 0)),
+            pl.BlockSpec((text_per, HD), lambda h: (0, h)),
+            pl.BlockSpec((text_per, HD), lambda h: (0, h)),
+            pl.BlockSpec((text_per, HD), lambda h: (0, 0)),
         ]
     )
     x_in = slices_around(in_parts)
@@ -235,11 +222,11 @@
         grid=grid,
         in_specs=in_specs,
         out_specs=[
-            pl.BlockSpec((1, 2, q_rows), lambda h, i: (h, 0, i)),
-            pl.BlockSpec((half, rows, HD), lambda h, i: (i, 0, h)),
+            pl.BlockSpec((1, 2, q_rows), lambda h: (h, 0, 0)),
+            pl.BlockSpec((NZX, rows, HD), lambda h: (0, 0, h)),
         ],
         out_shape=[
-            jax.ShapeDtypeStruct((heads, 2, steps * q_rows), F32),
+            jax.ShapeDtypeStruct((heads, 2, q_rows), F32),
             jax.ShapeDtypeStruct((NZX, rows, width), BF16),
         ],
         compiler_params=params,
@@ -266,12 +253,11 @@
     dq_terms, *kv_terms = pl.pallas_call(
         grads_kernel,
         grid=grid,
-        in_specs=in_specs + [pl.BlockSpec((NZX, 1, 2, q_rows), lambda h, i: (0, h, 0, i))],
-        out_specs=[pl.BlockSpec((half, rows, HD), lambda h, i: (i, 0, h))]
-        + [pl.BlockSpec((kv_rows, HD), lambda h, i: (0, h))] * NY,
+        in_specs=in_specs + [pl.BlockSpec((NZX, 1, 2, q_rows), lambda h: (0, h, 0, 0))],
+        out_specs=[pl.BlockSpec((NZX, rows, HD), lambda h: (0, 0, h))]
+        + [pl.BlockSpec((kv_rows, HD), lambda h: (0, h))] * NY,
         out_shape=[jax.ShapeDtypeStruct((NZX, rows, width), BF16)]
         + [jax.ShapeDtypeStruct((kv_rows, width), BF16)] * NY,
-        scratch_shapes=[pltpu.VMEM((2, NY * rows + text_per, HD), F32)],
         compiler_params=params,
         name="attention_grads",
     )(*operands, all_stats)

time: 208 us -> 207 us (level)
  waiting for transfers between devices: 32.5 us -> 36.5 us
  starting transfers between devices: 76.2 us -> 73.7 us
  Pallas kernels: 39.3 us -> 36.9 us
  transfers between devices with their start and end apart: 36 -> 36, of which waited for: 11 -> 12; matrix products, arithmetic and copies ran while one was open for 16% -> 16% of each run, Pallas kernels for 19% -> 18%
where the time goes in v4:
time: 207 us; the launch traced here: 205 us
  starting transfers between devices  73.7 us (36%)
  Pallas kernels  36.9 us (18%)
  waiting for transfers between devices  36.5 us (18%)
  other arithmetic  18.4 us (9%)
  matrix products  14.1 us (7%)
  blocking collectives  12.8 us (6%)
  local copies, waits for them, and re-layouts  11.9 us (6%)
    ppermute x21, starting transfers between devices, shift(): lax.ppermute(array, 'blk', [(i, (i + by * NZX) % (NY * NZX)) for i in ran...  29.2 us
    all_to_all x6, starting transfers between devices, exchange(): lax.all_to_all(array, 'blk', 0, 0, tiled=True, axis_index_groups=along_zx)  26.9 us
    ppermute x21, waiting for transfers between devices, shift(): lax.ppermute(array, 'blk', [(i, (i + by * NZX) % (NY * NZX)) for i in ran...  14.9 us
    all_to_all x6, waiting for transfers between devices, exchange(): lax.all_to_all(array, 'blk', 0, 0, tiled=True, axis_index_groups=along_zx)  14.2 us
    all_to_all x1, blocking collectives, exchange(): lax.all_to_all(array, 'blk', 0, 0, tiled=True, axis_index_groups=along_zx)  12.8 us
    pallas_call x1, Pallas kernels, per_device(): pl.pallas_call(grads_kernel, grid=grid, in_specs=in_specs + [pl.BlockSpec...  12.4 us
    pallas_call x3, Pallas kernels, weight_terms(): pl.pallas_call(weights_kernel, grid=(2,), in_specs=[pl.BlockSpec((rows, p...  10.9 us
    pallas_call x1, Pallas kernels, per_device(): pl.pallas_call(stats_kernel, grid=grid, in_specs=in_specs, out_specs=[pl....  10.2 us
  transfers between devices with their start and end apart: 36, of which 12 were waited for; matrix products, arithmetic and copies ran while one was open for 16% of the time, Pallas kernels for 18%

profile of v4, /device:TPU:1, one launch (start us, length us, event | category | flops | bytes accessed | tf_op | source)
XLA Modules:
  0.0 205.3 jit_solution(15236397188107496418)
XLA Ops:
  0.6 4.5 %collective-permute-start.2 = (bf16[192,768]{1,0:T(8,128)(2,1)}, bf16[192,768]{1,0:T(8,128)(2,1)S(1)}, u32[]{:S(2)}, u32[]{:S(2)}) collective-permute-start(bf16[192,768]{1,0:T(8,128)(2,1)} %bitcast.80), channel_id=1, source_target_pairs={{0,64},{32,96},{64,0},{96,32},{1,65},{33,97},{65,1},{97,33},{2,66}... | collective-permute-start | bytes 884744 | tf_op jit(solution)/shard_map/ppermute | solution.py:169
  6.1 6.0 %collective-permute-done.2 = bf16[192,768]{1,0:T(8,128)(2,1)S(1)} collective-permute-done((bf16[192,768]{1,0:T(8,128)(2,1)}, bf16[192,768]{1,0:T(8,128)(2,1)S(1)}, u32[]{:S(2)}, u32[]{:S(2)}) %collective-permute-start.2) | collective-permute-done | bytes 294944 | tf_op jit(solution)/shard_map/ppermute | solution.py:169
  13.3 3.0 %collective-permute-start = (bf16[192,768]{1,0:T(8,128)(2,1)}, bf16[192,768]{1,0:T(8,128)(2,1)}, u32[]{:S(2)}, u32[]{:S(2)}) collective-permute-start(bf16[192,768]{1,0:T(8,128)(2,1)} %bitcast.83), channel_id=1, source_target_pairs={{0,64},{32,96},{64,0},{96,32},{1,65},{33,97},{65,1},{97,33},{2,66}... | collective-permute-start | bytes 884744 | tf_op jit(solution)/shard_map/ppermute | solution.py:170
  16.3 1.8 select_select_fusion.4
  18.1 5.1 %fusion.1 = bf16[3,192,384]{2,1,0:T(8,128)(2,1)S(1)} fusion(bf16[3072,3,384]{2,0,1:T(8,128)(2,1)} %param.9, bf16[192,768]{1,0:T(8,128)(2,1)S(1)} %get-tuple-element.115, bf16[192,768]{1,0:T(8,128)(2,1)S(1)} %get-tuple-element.114, bf16[192,768]{1,0:T(8,128)(2,1)S(1)} %get-tuple-element.113, bf16[192,768]{1,0:T(8,128)(2,1)S(1)} %get-tuple-element.112), kind=kOutput, calls=%fused_computation.4 | convolution fusion | flops 1363894272 | bytes 8699904 | tf_op jit(solution)/shard_map/vd,dch->cvh/dot_general | solution.py:172
  24.6 1.4 collective-permute-done.5
  28.2 1.8 broadcast_in_dim.40
  30.0 4.7 %all-to-all-start = ((bf16[8,2,192,384]{3,2,1,0:T(8,128)(2,1)}), bf16[8,2,192,384]{3,2,1,0:T(8,128)(2,1)}, u32[]{:S(2)}, u32[]{:S(2)}) async-start(bf16[8,2,192,384]{3,2,1,0:T(8,128)(2,1)} %broadcast_in_dim.40), calls=%async_computation | async-start | bytes 4718592 | tf_op jit(solution)/shard_map/all_to_all | solution.py:134
  34.9 1.4 collective-permute-start.6
  36.2 2.6 %collective-permute-start.7 = (bf16[2,192,384]{2,1,0:T(8,128)(2,1)S(1)}, bf16[2,192,384]{2,1,0:T(8,128)(2,1)S(1)}, u32[]{:S(2)}, u32[]{:S(2)}) collective-permute-start(bf16[2,192,384]{2,1,0:T(8,128)(2,1)S(1)} %slice.38.refs_0_.refs_4_), channel_id=1, source_target_pairs={{0,16},{1,17},{2,18},{3,19},{4,20},{5,21},{6,22},{7,23},{8,24},{9,... | collective-permute-start | bytes 884744 | tf_op jit(solution)/shard_map/ppermute | solution.py:140
  39.9 2.1 %select_select_fusion.5 = (bf16[192,768]{1,0:T(8,128)(2,1)}, bf16[192,768]{1,0:T(8,128)(2,1)S(1)}, bf16[192,768]{1,0:T(8,128)(2,1)}) fusion(bf16[192,768]{1,0:T(8,128)(2,1)} %copy-done.9, bf16[192,768]{1,0:T(8,128)(2,1)} %copy-done.10, bf16[192,768]{1,0:T(8,128)(2,1)S(1)} %get-tuple-element.112, bf16[192,768]{1,0:T(8,128)(2,1)} %copy-done.8, pred[]{:T(512)S(6)} %eq.36, ...), kind=kLoop, calls=%fused_computation.46 | loop fusion | flops 1327104 | bytes 2064393 | tf_op jit(solution)/shard_map/jit(_where)/select_n | solution.py:162
  42.4 1.7 convolution_convert_fusion.2.refs_8_
  44.9 1.6 collective-permute-start.11
  46.5 5.2 %collective-permute-done.7.refs_2_.refs_6_ = bf16[2,192,384]{2,1,0:T(8,128)(2,1)S(1)} collective-permute-done((bf16[2,192,384]{2,1,0:T(8,128)(2,1)S(1)}, bf16[2,192,384]{2,1,0:T(8,128)(2,1)S(1)}, u32[]{:S(2)}, u32[]{:S(2)}) %collective-permute-start.7) | collective-permute-done | bytes 294944 | tf_op jit(solution)/shard_map/ppermute | solution.py:140
  51.7 2.6 %select_select_fusion = (bf16[192,768]{1,0:T(8,128)(2,1)}, bf16[192,768]{1,0:T(8,128)(2,1)}, bf16[192,768]{1,0:T(8,128)(2,1)}, bf16[192,768]{1,0:T(8,128)(2,1)}) fusion(bf16[192,768]{1,0:T(8,128)(2,1)} %copy-done.15, bf16[192,768]{1,0:T(8,128)(2,1)} %copy-done.14, bf16[192,768]{1,0:T(8,128)(2,1)} %copy-done.13, bf16[192,768]{1,0:T(8,128)(2,1)} %copy-done.16, ...), kind=kLoop, calls=%fused_computation.41 | loop fusion | flops 1769472 | bytes 2359308 | tf_op jit(solution)/shard_map/jit(_where)/select_n | solution.py:162
  55.4 4.0 %collective-permute-start.13 = (bf16[192,768]{1,0:T(8,128)(2,1)}, bf16[192,768]{1,0:T(8,128)(2,1)}, u32[]{:S(2)}, u32[]{:S(2)}) collective-permute-start(bf16[192,768]{1,0:T(8,128)(2,1)} %get-tuple-element.119), channel_id=1, source_target_pairs={{0,16},{1,17},{2,18},{3,19},{4,20},{5,21},{6,22},{7,23},{8,24},{9,... | collective-permute-start | bytes 884744 | tf_op jit(solution)/shard_map/ppermute | solution.py:140
  60.4 4.3 %all-to-all-done.q_ref.g_ref = bf16[8,2,192,384]{3,2,1,0:T(8,128)(2,1)} async-done(((bf16[8,2,192,384]{3,2,1,0:T(8,128)(2,1)}), bf16[8,2,192,384]{3,2,1,0:T(8,128)(2,1)}, u32[]{:S(2)}, u32[]{:S(2)}) %all-to-all-start) | async-done | bytes 2359328 | tf_op jit(solution)/shard_map/all_to_all | solution.py:134
  65.4 10.2 %attention_stats.1 = (f32[3,2,1536]{2,1,0:T(2,128)}, bf16[8,192,384]{2,1,0:T(8,128)(2,1)}) custom-call(bf16[8,2,192,384]{3,2,1,0:T(8,128)(2,1)} %all-to-all-done.q_ref.g_ref, bf16[8,2,192,384]{3,2,1,0:T(8,128)(2,1)} %all-to-all-done.q_ref.g_ref, bf16[2,192,384]{2,1,0:T(8,128)(2,1)} %copy-done.1, bf16[2,192,384]{2,1,0:T(8,128)(2,1)} %copy-done.2, ...), custom_call_target="tpu_custom_call" | custom-call | tf_op jit(solution)/shard_map/attention_stats/pallas_call | solution.py:220
  75.7 1.4 collective-permute-done.13.refs_2_
  77.9 12.8 %all_to_all.35.refs_11_ = f32[8,3,2,1536]{3,2,1,0:T(2,128)} all-to-all(f32[8,3,2,1536]{3,2,1,0:T(2,128)S(1)} %broadcast_in_dim.44), channel_id=1, replica_groups={{0,1,2,3,4,5,6,7},{8,9,10,11,12,13,14,15},{16,17,18,19,20,21,22,23},{24..., dimensions={0} | all-to-all | bytes 589824 | tf_op jit(solution)/shard_map/all_to_all | solution.py:134
  90.7 3.7 %all-to-all-start.1 = ((bf16[8,192,384]{2,1,0:T(8,128)(2,1)}), bf16[8,192,384]{2,1,0:T(8,128)(2,1)S(1)}, u32[]{:S(2)}, u32[]{:S(2)}) async-start(bf16[8,192,384]{2,1,0:T(8,128)(2,1)} %get-tuple-element.59), calls=%async_computation.1 | async-start | bytes 2359296 | tf_op jit(solution)/shard_map/all_to_all | solution.py:134
  94.5 12.4 %attention_grads.1 = (bf16[8,192,384]{2,1,0:T(8,128)(2,1)}, bf16[400,384]{1,0:T(8,128)(2,1)}, bf16[400,384]{1,0:T(8,128)(2,1)}, bf16[400,384]{1,0:T(8,128)(2,1)}, bf16[400,384]{1,0:T(8,128)(2,1)}) custom-call(bf16[8,2,192,384]{3,2,1,0:T(8,128)(2,1)} %all-to-all-done.q_ref.g_ref, bf16[8,2,192,384]{3,2,1,0:T(8,128)(2,1)} %all-to-all-done.q_ref.g_ref, ...), custom_call_target="tpu_custom_call" | custom-call | tf_op jit(solution)/shard_map/attention_grads/pallas_call | solution.py:253
  106.9 4.5 %all-to-all-done.1.out_ref = bf16[8,192,384]{2,1,0:T(8,128)(2,1)S(1)} async-done(((bf16[8,192,384]{2,1,0:T(8,128)(2,1)}), bf16[8,192,384]{2,1,0:T(8,128)(2,1)S(1)}, u32[]{:S(2)}, u32[]{:S(2)}) %all-to-all-start.1) | async-done | bytes 1179680 | tf_op jit(solution)/shard_map/all_to_all | solution.py:134
  112.5 3.6 %all-to-all-start.3 = ((bf16[8,192,384]{2,1,0:T(8,128)(2,1)}), bf16[8,192,384]{2,1,0:T(8,128)(2,1)S(1)}, u32[]{:S(2)}, u32[]{:S(2)}) async-start(bf16[8,192,384]{2,1,0:T(8,128)(2,1)} %get-tuple-element.81), calls=%async_computation.3 | async-start | bytes 2359296 | tf_op jit(solution)/shard_map/all_to_all | solution.py:134
  116.1 1.4 collective-permute-start.20
  117.5 2.6 %collective-permute-start.19 = (bf16[400,384]{1,0:T(8,128)(2,1)}, bf16[400,384]{1,0:T(8,128)(2,1)}, u32[]{:S(2)}, u32[]{:S(2)}) collective-permute-start(bf16[400,384]{1,0:T(8,128)(2,1)} %get-tuple-element.68), channel_id=1, source_target_pairs={{0,16},{1,17},{2,18},{3,19},{4,20},{5,21},{6,22},{7,23},{8,24},{9,... | collective-permute-start | bytes 921608 | tf_op jit(solution)/shard_map/ppermute | solution.py:140
  121.2 1.6 constant_dynamic-slice_fusion.stat_ref
  122.8 3.4 %combine_out.1 = bf16[192,384]{1,0:T(8,128)(2,1)} custom-call(bf16[8,192,384]{2,1,0:T(8,128)(2,1)} %copy-done.5, f32[8,3,2,192]{3,2,1,0:T(2,128)} %constant_dynamic-slice_fusion.stat_ref), custom_call_target="tpu_custom_call" | custom-call | tf_op jit(solution)/shard_map/combine_out/pallas_call | solution.py:239
  127.3 1.6 collective-permute-start.17
  129.0 4.5 %collective-permute-done.19 = bf16[400,384]{1,0:T(8,128)(2,1)} collective-permute-done((bf16[400,384]{1,0:T(8,128)(2,1)}, bf16[400,384]{1,0:T(8,128)(2,1)}, u32[]{:S(2)}, u32[]{:S(2)}) %collective-permute-start.19) | collective-permute-done | bytes 307232 | tf_op jit(solution)/shard_map/ppermute | solution.py:140
  134.0 1.4 convert_add_fusion
  137.0 2.0 collective-permute-done.15.refs_5_
  141.1 2.9 %collective-permute-start.22 = (bf16[2,192,384]{2,1,0:T(8,128)(2,1)}, bf16[2,192,384]{2,1,0:T(8,128)(2,1)}, u32[]{:S(2)}, u32[]{:S(2)}) collective-permute-start(bf16[2,192,384]{2,1,0:T(8,128)(2,1)} %bitcast.9.refs_4_), channel_id=1, source_target_pairs={{0,16},{1,17},{2,18},{3,19},{4,20},{5,21},{6,22},{7,23},{8,24},{9,... | collective-permute-start | bytes 884744 | tf_op jit(solution)/shard_map/ppermute | solution.py:140
  144.0 3.4 %weight_grads.3 = bf16[8,1,96,384]{3,2,1,0:T(8,128)(2,1)} custom-call(bf16[192,768]{1,0:T(8,128)(2,1)} %get-tuple-element.71.refs_0_, bf16[192,768]{1,0:T(8,128)(2,1)} %collective-permute-done.12.refs_1_, bf16[192,768]{1,0:T(8,128)(2,1)} %collective-permute-done.13.refs_2_, bf16[192,768]{1,0:T(8,128)(2,1)} %collective-permute-done.14.refs_3_, ...), custom_call_target="tpu_custom_call" | custom-call | tf_op jit(solution)/shard_map/weight_grads/pallas_call | solution.py:276
  148.8 4.8 %all-to-all-start.4 = ((bf16[8,1,96,384]{3,2,1,0:T(8,128)(2,1)}), bf16[8,1,96,384]{3,2,1,0:T(8,128)(2,1)}, u32[]{:S(2)}, u32[]{:S(2)}) async-start(bf16[8,1,96,384]{3,2,1,0:T(8,128)(2,1)} %weight_grads.3), calls=%async_computation.4 | async-start | bytes 1179648 | tf_op jit(solution)/shard_map/all_to_all | solution.py:134
  153.6 5.7 %fusion = bf16[4,192,768]{2,1,0:T(8,128)(2,1)S(1)} fusion(bf16[4,768,3,384]{3,1,0,2:T(8,128)(2,1)} %bitcast.85, bf16[2,192,384]{2,1,0:T(8,128)(2,1)} %bitcast.9.refs_4_, bf16[1,192,384]{2,1,0:T(8,128)(2,1)} %bitcast.70), kind=kOutput, calls=%fused_computation.2 | convolution fusion | flops 1360429056 | bytes 8699904 | tf_op jit(solution)/shard_map/cvh,sdch->svd/dot_general | solution.py:298
  159.3 4.1 %weight_grads.4 = bf16[8,2,96,384]{3,2,1,0:T(8,128)(2,1)} custom-call(bf16[192,768]{1,0:T(8,128)(2,1)} %get-tuple-element.85.refs_0_, bf16[192,768]{1,0:T(8,128)(2,1)} %collective-permute-done.9.refs_1_, bf16[192,768]{1,0:T(8,128)(2,1)} %copy-done.7, bf16[192,768]{1,0:T(8,128)(2,1)} %collective-permute-done.11.refs_3_, bf16[2,192,384]{2,1,0:T(8,128)(2,1)} %bitcast.9.refs_4_, ...), custom_call_target="tpu_custom_call" | custom-call | tf_op jit(solution)/shard_map/weight_grads/pallas_call | solution.py:276
  163.4 5.2 %all-to-all-start.5 = ((bf16[8,2,96,384]{3,2,1,0:T(8,128)(2,1)}), bf16[8,2,96,384]{3,2,1,0:T(8,128)(2,1)}, u32[]{:S(2)}, u32[]{:S(2)}) async-start(bf16[8,2,96,384]{3,2,1,0:T(8,128)(2,1)} %weight_grads.4), calls=%async_computation.5 | async-start | bytes 2359296 | tf_op jit(solution)/shard_map/all_to_all | solution.py:134
  168.6 3.3 %collective-permute-start.24 = (bf16[192,768]{1,0:T(8,128)(2,1)S(1)}, bf16[192,768]{1,0:T(8,128)(2,1)S(1)}, u32[]{:S(2)}, u32[]{:S(2)}) collective-permute-start(bf16[192,768]{1,0:T(8,128)(2,1)S(1)} %get-tuple-element.117), channel_id=1, source_target_pairs={{0,32},{32,0},{64,96},{96,64},{1,33},{33,1},{65,97},{97,65},{2,34}... | collective-permute-start | bytes 884744 | tf_op jit(solution)/shard_map/ppermute | solution.py:316
  172.0 1.6 collective-permute-start.27
  173.6 2.0 collective-permute-start.28
  177.8 3.3 %collective-permute-start.26 = (bf16[192,768]{1,0:T(8,128)(2,1)}, bf16[192,768]{1,0:T(8,128)(2,1)}, u32[]{:S(2)}, u32[]{:S(2)}) collective-permute-start(bf16[192,768]{1,0:T(8,128)(2,1)} %select_convert_fusion), channel_id=1, source_target_pairs={{0,64},{32,96},{64,0},{96,32},{1,65},{33,97},{65,1},{97,33},{2,66}... | collective-permute-start | bytes 884744 | tf_op jit(solution)/shard_map/ppermute | solution.py:321
  184.5 3.4 %weight_grads.5 = bf16[8,1,96,384]{3,2,1,0:T(8,128)(2,1)} custom-call(bf16[192,768]{1,0:T(8,128)(2,1)} %get-tuple-element.85.refs_0_, bf16[192,768]{1,0:T(8,128)(2,1)} %collective-permute-done.9.refs_1_, bf16[192,768]{1,0:T(8,128)(2,1)} %copy-done.7, bf16[192,768]{1,0:T(8,128)(2,1)} %collective-permute-done.11.refs_3_, bf16[1,192,384]{2,1,0:T(8,128)(2,1)} %bitcast.74, ...), custom_call_target="tpu_custom_call" | custom-call | tf_op jit(solution)/shard_map/weight_grads/pallas_call | solution.py:276
  187.9 4.8 %all-to-all-start.6 = ((bf16[8,1,96,384]{3,2,1,0:T(8,128)(2,1)}), bf16[8,1,96,384]{3,2,1,0:T(8,128)(2,1)}, u32[]{:S(2)}, u32[]{:S(2)}) async-start(bf16[8,1,96,384]{3,2,1,0:T(8,128)(2,1)} %weight_grads.5), calls=%async_computation.6 | async-start | bytes 1179648 | tf_op jit(solution)/shard_map/all_to_all | solution.py:134
  192.7 1.8 convert_reduce_fusion.1
  194.5 2.1 %fusion.26 = bf16[192,1,768]{2,0,1:T(8,128)(2,1)} fusion(bf16[192,768]{1,0:T(8,128)(2,1)} %collective-permute-done.26, bf16[192,768]{1,0:T(8,128)(2,1)} %copy-done.12, bf16[192,768]{1,0:T(8,128)(2,1)} %copy-done.11, pred[]{:T(512)S(6)} %eq.26, bf16[4,192,768]{2,1,0:T(8,128)(2,1)S(1)} %fusion, pred[]{:T(512)S(6)} %eq.27), kind=kLoop, calls=%fused_computation.37 | loop fusion | flops 1769472 | bytes 2359298 | tf_op jit(solution)/shard_map/broadcast_in_dim | solution.py:324
  196.6 1.5 convert_reduce_fusion
  198.1 5.3 %all-to-all-done.6 = bf16[8,1,96,384]{3,2,1,0:T(8,128)(2,1)} async-done(((bf16[8,1,96,384]{3,2,1,0:T(8,128)(2,1)}), bf16[8,1,96,384]{3,2,1,0:T(8,128)(2,1)}, u32[]{:S(2)}, u32[]{:S(2)}) %all-to-all-start.6) | async-done | bytes 589856 | tf_op jit(solution)/shard_map/all_to_all | solution.py:134
  (116 shorter events, 28.3 us)
Async XLA Ops:
  0.6 26.6 %copy-start = (bf16[3072,384]{1,0:T(8,128)(2,1)S(1)}, bf16[3072,384]{1,0:T(8,128)(2,1)}, u32[]{:S(2)}) copy-start(bf16[3072,384]{1,0:T(8,128)(2,1)} %param.10) | copy-start | bytes 7077892
  0.6 11.4 %collective-permute-start.2 = (bf16[192,768]{1,0:T(8,128)(2,1)}, bf16[192,768]{1,0:T(8,128)(2,1)S(1)}, u32[]{:S(2)}, u32[]{:S(2)}) collective-permute-start(bf16[192,768]{1,0:T(8,128)(2,1)} %bitcast.80), channel_id=1, source_target_pairs={{0,64},{32,96},{64,0},{96,32},{1,65},{33,97},{65,1},{97,33},{2,66}... | collective-permute-start | bytes 884744 | tf_op jit(solution)/shard_map/ppermute | solution.py:169
  5.2 11.1 %collective-permute-start.1 = (bf16[192,768]{1,0:T(8,128)(2,1)}, bf16[192,768]{1,0:T(8,128)(2,1)S(1)}, u32[]{:S(2)}, u32[]{:S(2)}) collective-permute-start(bf16[192,768]{1,0:T(8,128)(2,1)} %bitcast.81), channel_id=1, source_target_pairs={{0,32},{32,0},{64,96},{96,64},{1,33},{33,1},{65,97},{97,65},{2,34}... | collective-permute-start | bytes 884744 | tf_op jit(solution)/shard_map/ppermute | solution.py:148
  12.1 4.2 %collective-permute-start.3 = (bf16[192,768]{1,0:T(8,128)(2,1)S(1)}, bf16[192,768]{1,0:T(8,128)(2,1)S(1)}, u32[]{:S(2)}, u32[]{:S(2)}) collective-permute-start(bf16[192,768]{1,0:T(8,128)(2,1)S(1)} %collective-permute-done.2), channel_id=1, source_target_pairs={{0,32},{32,0},{64,96},{96,64},{1,33},{33,1},{65,97},{97,65},{2,34}... | collective-permute-start | bytes 884744 | tf_op jit(solution)/shard_map/ppermute | solution.py:149
  13.3 11.3 %collective-permute-start.4 = (bf16[192,768]{1,0:T(8,128)(2,1)}, bf16[192,768]{1,0:T(8,128)(2,1)}, u32[]{:S(2)}, u32[]{:S(2)}) collective-permute-start(bf16[192,768]{1,0:T(8,128)(2,1)} %bitcast.82), channel_id=1, source_target_pairs={{0,32},{32,0},{64,96},{96,64},{1,33},{33,1},{65,97},{97,65},{2,34}... | collective-permute-start | bytes 884744 | tf_op jit(solution)/shard_map/ppermute | solution.py:148
  13.3 9.9 %collective-permute-start = (bf16[192,768]{1,0:T(8,128)(2,1)}, bf16[192,768]{1,0:T(8,128)(2,1)}, u32[]{:S(2)}, u32[]{:S(2)}) collective-permute-start(bf16[192,768]{1,0:T(8,128)(2,1)} %bitcast.83), channel_id=1, source_target_pairs={{0,64},{32,96},{64,0},{96,32},{1,65},{33,97},{65,1},{97,33},{2,66}... | collective-permute-start | bytes 884744 | tf_op jit(solution)/shard_map/ppermute | solution.py:170
  18.1 5.1 %copy-start.8 = (bf16[192,768]{1,0:T(8,128)(2,1)}, bf16[192,768]{1,0:T(8,128)(2,1)S(1)}, u32[]{:S(2)}) copy-start(bf16[192,768]{1,0:T(8,128)(2,1)S(1)} %get-tuple-element.113) | copy-start | bytes 884740
  18.1 5.1 %copy-start.9 = (bf16[192,768]{1,0:T(8,128)(2,1)}, bf16[192,768]{1,0:T(8,128)(2,1)S(1)}, u32[]{:S(2)}) copy-start(bf16[192,768]{1,0:T(8,128)(2,1)S(1)} %get-tuple-element.114) | copy-start | bytes 884740
  18.1 5.1 %copy-start.10 = (bf16[192,768]{1,0:T(8,128)(2,1)}, bf16[192,768]{1,0:T(8,128)(2,1)S(1)}, u32[]{:S(2)}) copy-start(bf16[192,768]{1,0:T(8,128)(2,1)S(1)} %get-tuple-element.115) | copy-start | bytes 884740
  18.1 7.9 %copy-start.17 = (bf16[192,1,768]{2,0,1:T(8,128)(2,1)S(1)}, bf16[192,1,768]{2,0,1:T(8,128)(2,1)}, u32[]{:S(2)}) copy-start(bf16[192,1,768]{2,0,1:T(8,128)(2,1)} %param.8) | copy-start | bytes 884740
  23.2 2.8 %collective-permute-start.5 = (bf16[192,768]{1,0:T(8,128)(2,1)}, bf16[192,768]{1,0:T(8,128)(2,1)S(1)}, u32[]{:S(2)}, u32[]{:S(2)}) collective-permute-start(bf16[192,768]{1,0:T(8,128)(2,1)} %collective-permute-done), channel_id=1, source_target_pairs={{0,32},{32,0},{64,96},{96,64},{1,33},{33,1},{65,97},{97,65},{2,34}... | collective-permute-start | bytes 884744 | tf_op jit(solution)/shard_map/ppermute | solution.py:149
  30.0 34.7 %all-to-all-start = ((bf16[8,2,192,384]{3,2,1,0:T(8,128)(2,1)}), bf16[8,2,192,384]{3,2,1,0:T(8,128)(2,1)}, u32[]{:S(2)}, u32[]{:S(2)}) async-start(bf16[8,2,192,384]{3,2,1,0:T(8,128)(2,1)} %broadcast_in_dim.40), calls=%async_computation | async-start | bytes 4718592 | tf_op jit(solution)/shard_map/all_to_all | solution.py:134
  34.8 19.5 %copy-start.1 = (bf16[2,192,384]{2,1,0:T(8,128)(2,1)}, bf16[2,192,384]{2,1,0:T(8,128)(2,1)S(1)}, u32[]{:S(2)}) copy-start(bf16[2,192,384]{2,1,0:T(8,128)(2,1)S(1)} %slice.38.refs_0_.refs_4_) | copy-start | bytes 884740
  34.8 24.6 %copy-start.24 = (s32[256,1]{0,1:T(1,128)S(1)}, s32[256,1]{0,1:T(1,128)}, u32[]{:S(2)}) copy-start(s32[256,1]{0,1:T(1,128)} %param.13) | copy-start | bytes 3076
  34.8 24.8 %copy-start.25 = (bf16[256,1,384]{2,0,1:T(8,128)(2,1)S(1)}, bf16[256,1,384]{2,0,1:T(8,128)(2,1)}, u32[]{:S(2)}) copy-start(bf16[256,1,384]{2,0,1:T(8,128)(2,1)} %param.12) | copy-start | bytes 589828
  34.9 10.0 %collective-permute-start.6 = (bf16[2,192,384]{2,1,0:T(8,128)(2,1)S(1)}, bf16[2,192,384]{2,1,0:T(8,128)(2,1)S(1)}, u32[]{:S(2)}, u32[]{:S(2)}) collective-permute-start(bf16[2,192,384]{2,1,0:T(8,128)(2,1)S(1)} %slice.38.refs_0_.refs_4_), channel_id=1, source_target_pairs={{0,8},{1,9},{2,10},{3,11},{4,12},{5,13},{6,14},{7,15},{8,16},{9,17... | collective-permute-start | bytes 884744 | tf_op jit(solution)/shard_map/ppermute | solution.py:140
  36.2 15.5 %collective-permute-start.7 = (bf16[2,192,384]{2,1,0:T(8,128)(2,1)S(1)}, bf16[2,192,384]{2,1,0:T(8,128)(2,1)S(1)}, u32[]{:S(2)}, u32[]{:S(2)}) collective-permute-start(bf16[2,192,384]{2,1,0:T(8,128)(2,1)S(1)} %slice.38.refs_0_.refs_4_), channel_id=1, source_target_pairs={{0,16},{1,17},{2,18},{3,19},{4,20},{5,21},{6,22},{7,23},{8,24},{9,... | collective-permute-start | bytes 884744 | tf_op jit(solution)/shard_map/ppermute | solution.py:140
  38.8 12.9 %collective-permute-start.8 = (bf16[2,192,384]{2,1,0:T(8,128)(2,1)S(1)}, bf16[2,192,384]{2,1,0:T(8,128)(2,1)S(1)}, u32[]{:S(2)}, u32[]{:S(2)}) collective-permute-start(bf16[2,192,384]{2,1,0:T(8,128)(2,1)S(1)} %slice.38.refs_0_.refs_4_), channel_id=1, source_target_pairs={{0,24},{1,25},{2,26},{3,27},{4,28},{5,29},{6,30},{7,31},{8,0},{9,1... | collective-permute-start | bytes 884744 | tf_op jit(solution)/shard_map/ppermute | solution.py:140
  42.0 17.4 %collective-permute-start.9 = (bf16[192,768]{1,0:T(8,128)(2,1)S(1)}, bf16[192,768]{1,0:T(8,128)(2,1)}, u32[]{:S(2)}, u32[]{:S(2)}) collective-permute-start(bf16[192,768]{1,0:T(8,128)(2,1)S(1)} %get-tuple-element.123), channel_id=1, source_target_pairs={{0,8},{1,9},{2,10},{3,11},{4,12},{5,13},{6,14},{7,15},{8,16},{9,17... | collective-permute-start | bytes 884744 | tf_op jit(solution)/shard_map/ppermute | solution.py:140
  44.1 31.5 %collective-permute-start.10 = (bf16[192,768]{1,0:T(8,128)(2,1)}, bf16[192,768]{1,0:T(8,128)(2,1)S(1)}, u32[]{:S(2)}, u32[]{:S(2)}) collective-permute-start(bf16[192,768]{1,0:T(8,128)(2,1)} %get-tuple-element.122), channel_id=1, source_target_pairs={{0,16},{1,17},{2,18},{3,19},{4,20},{5,21},{6,22},{7,23},{8,24},{9,... | collective-permute-start | bytes 884744 | tf_op jit(solution)/shard_map/ppermute | solution.py:140
  44.9 20.5 %copy-start.2 = (bf16[2,192,384]{2,1,0:T(8,128)(2,1)}, bf16[2,192,384]{2,1,0:T(8,128)(2,1)S(1)}, u32[]{:S(2)}) copy-start(bf16[2,192,384]{2,1,0:T(8,128)(2,1)S(1)} %collective-permute-done.6.refs_1_.refs_5_) | copy-start | bytes 884740
  44.9 30.8 %collective-permute-start.11 = (bf16[192,768]{1,0:T(8,128)(2,1)}, bf16[192,768]{1,0:T(8,128)(2,1)}, u32[]{:S(2)}, u32[]{:S(2)}) collective-permute-start(bf16[192,768]{1,0:T(8,128)(2,1)} %get-tuple-element.111), channel_id=1, source_target_pairs={{0,24},{1,25},{2,26},{3,27},{4,28},{5,29},{6,30},{7,31},{8,0},{9,1... | collective-permute-start | bytes 884744 | tf_op jit(solution)/shard_map/ppermute | solution.py:140
  51.7 13.7 %copy-start.3 = (bf16[2,192,384]{2,1,0:T(8,128)(2,1)}, bf16[2,192,384]{2,1,0:T(8,128)(2,1)S(1)}, u32[]{:S(2)}) copy-start(bf16[2,192,384]{2,1,0:T(8,128)(2,1)S(1)} %collective-permute-done.7.refs_2_.refs_6_) | copy-start | bytes 884740
  51.7 13.7 %copy-start.4 = (bf16[2,192,384]{2,1,0:T(8,128)(2,1)}, bf16[2,192,384]{2,1,0:T(8,128)(2,1)S(1)}, u32[]{:S(2)}) copy-start(bf16[2,192,384]{2,1,0:T(8,128)(2,1)S(1)} %collective-permute-done.8.refs_3_.refs_7_) | copy-start | bytes 884740
  54.3 21.3 %collective-permute-start.12 = (bf16[192,768]{1,0:T(8,128)(2,1)}, bf16[192,768]{1,0:T(8,128)(2,1)}, u32[]{:S(2)}, u32[]{:S(2)}) collective-permute-start(bf16[192,768]{1,0:T(8,128)(2,1)} %get-tuple-element.120), channel_id=1, source_target_pairs={{0,8},{1,9},{2,10},{3,11},{4,12},{5,13},{6,14},{7,15},{8,16},{9,17... | collective-permute-start | bytes 884744 | tf_op jit(solution)/shard_map/ppermute | solution.py:140
  55.4 21.7 %collective-permute-start.13 = (bf16[192,768]{1,0:T(8,128)(2,1)}, bf16[192,768]{1,0:T(8,128)(2,1)}, u32[]{:S(2)}, u32[]{:S(2)}) collective-permute-start(bf16[192,768]{1,0:T(8,128)(2,1)} %get-tuple-element.119), channel_id=1, source_target_pairs={{0,16},{1,17},{2,18},{3,19},{4,20},{5,21},{6,22},{7,23},{8,24},{9,... | collective-permute-start | bytes 884744 | tf_op jit(solution)/shard_map/ppermute | solution.py:140
  59.4 17.7 %collective-permute-start.14 = (bf16[192,768]{1,0:T(8,128)(2,1)}, bf16[192,768]{1,0:T(8,128)(2,1)}, u32[]{:S(2)}, u32[]{:S(2)}) collective-permute-start(bf16[192,768]{1,0:T(8,128)(2,1)} %get-tuple-element.118), channel_id=1, source_target_pairs={{0,24},{1,25},{2,26},{3,27},{4,28},{5,29},{6,30},{7,31},{8,0},{9,1... | collective-permute-start | bytes 884744 | tf_op jit(solution)/shard_map/ppermute | solution.py:140
  75.6 15.1 %copy-start.7 = (bf16[192,768]{1,0:T(8,128)(2,1)}, bf16[192,768]{1,0:T(8,128)(2,1)S(1)}, u32[]{:S(2)}) copy-start(bf16[192,768]{1,0:T(8,128)(2,1)S(1)} %collective-permute-done.10.refs_2_) | copy-start | bytes 884740
  90.7 20.7 %all-to-all-start.1 = ((bf16[8,192,384]{2,1,0:T(8,128)(2,1)}), bf16[8,192,384]{2,1,0:T(8,128)(2,1)S(1)}, u32[]{:S(2)}, u32[]{:S(2)}) async-start(bf16[8,192,384]{2,1,0:T(8,128)(2,1)} %get-tuple-element.59), calls=%async_computation.1 | async-start | bytes 2359296 | tf_op jit(solution)/shard_map/all_to_all | solution.py:134
  112.5 34.9 %all-to-all-start.3 = ((bf16[8,192,384]{2,1,0:T(8,128)(2,1)}), bf16[8,192,384]{2,1,0:T(8,128)(2,1)S(1)}, u32[]{:S(2)}, u32[]{:S(2)}) async-start(bf16[8,192,384]{2,1,0:T(8,128)(2,1)} %get-tuple-element.81), calls=%async_computation.3 | async-start | bytes 2359296 | tf_op jit(solution)/shard_map/all_to_all | solution.py:134
  116.1 11.3 %collective-permute-start.20 = (bf16[400,384]{1,0:T(8,128)(2,1)}, bf16[400,384]{1,0:T(8,128)(2,1)}, u32[]{:S(2)}, u32[]{:S(2)}) collective-permute-start(bf16[400,384]{1,0:T(8,128)(2,1)} %get-tuple-element.69), channel_id=1, source_target_pairs={{0,8},{1,9},{2,10},{3,11},{4,12},{5,13},{6,14},{7,15},{8,16},{9,17... | collective-permute-start | bytes 921608 | tf_op jit(solution)/shard_map/ppermute | solution.py:140
  117.5 16.0 %collective-permute-start.19 = (bf16[400,384]{1,0:T(8,128)(2,1)}, bf16[400,384]{1,0:T(8,128)(2,1)}, u32[]{:S(2)}, u32[]{:S(2)}) collective-permute-start(bf16[400,384]{1,0:T(8,128)(2,1)} %get-tuple-element.68), channel_id=1, source_target_pairs={{0,16},{1,17},{2,18},{3,19},{4,20},{5,21},{6,22},{7,23},{8,24},{9,... | collective-permute-start | bytes 921608 | tf_op jit(solution)/shard_map/ppermute | solution.py:140
  120.1 13.9 %collective-permute-start.18 = (bf16[400,384]{1,0:T(8,128)(2,1)}, bf16[400,384]{1,0:T(8,128)(2,1)}, u32[]{:S(2)}, u32[]{:S(2)}) collective-permute-start(bf16[400,384]{1,0:T(8,128)(2,1)} %get-tuple-element.67), channel_id=1, source_target_pairs={{0,24},{1,25},{2,26},{3,27},{4,28},{5,29},{6,30},{7,31},{8,0},{9,1... | collective-permute-start | bytes 921608 | tf_op jit(solution)/shard_map/ppermute | solution.py:140
  126.2 12.8 %collective-permute-start.15 = (bf16[1,192,384]{2,1,0:T(8,128)(2,1)}, bf16[1,192,384]{2,1,0:T(8,128)(2,1)S(1)}, u32[]{:S(2)}, u32[]{:S(2)}) collective-permute-start(bf16[1,192,384]{2,1,0:T(8,128)(2,1)} %bitcast.75), channel_id=1, source_target_pairs={{0,8},{1,9},{2,10},{3,11},{4,12},{5,13},{6,14},{7,15},{8,16},{9,17... | collective-permute-start | bytes 442376 | tf_op jit(solution)/shard_map/ppermute | solution.py:140
  126.6 13.2 %collective-permute-start.16 = (bf16[1,192,384]{2,1,0:T(8,128)(2,1)}, bf16[1,192,384]{2,1,0:T(8,128)(2,1)S(1)}, u32[]{:S(2)}, u32[]{:S(2)}) collective-permute-start(bf16[1,192,384]{2,1,0:T(8,128)(2,1)} %bitcast.76), channel_id=1, source_target_pairs={{0,16},{1,17},{2,18},{3,19},{4,20},{5,21},{6,22},{7,23},{8,24},{9,... | collective-permute-start | bytes 442376 | tf_op jit(solution)/shard_map/ppermute | solution.py:140
  127.3 12.4 %collective-permute-start.17 = (bf16[1,192,384]{2,1,0:T(8,128)(2,1)}, bf16[1,192,384]{2,1,0:T(8,128)(2,1)S(1)}, u32[]{:S(2)}, u32[]{:S(2)}) collective-permute-start(bf16[1,192,384]{2,1,0:T(8,128)(2,1)} %bitcast.77), channel_id=1, source_target_pairs={{0,24},{1,25},{2,26},{3,27},{4,28},{5,29},{6,30},{7,31},{8,0},{9,1... | collective-permute-start | bytes 442376 | tf_op jit(solution)/shard_map/ppermute | solution.py:140
  139.7 9.0 %collective-permute-start.21 = (bf16[2,192,384]{2,1,0:T(8,128)(2,1)}, bf16[2,192,384]{2,1,0:T(8,128)(2,1)}, u32[]{:S(2)}, u32[]{:S(2)}) collective-permute-start(bf16[2,192,384]{2,1,0:T(8,128)(2,1)} %bitcast.9.refs_4_), channel_id=1, source_target_pairs={{0,8},{1,9},{2,10},{3,11},{4,12},{5,13},{6,14},{7,15},{8,16},{9,17... | collective-permute-start | bytes 884744 | tf_op jit(solution)/shard_map/ppermute | solution.py:140
  141.1 18.2 %collective-permute-start.22 = (bf16[2,192,384]{2,1,0:T(8,128)(2,1)}, bf16[2,192,384]{2,1,0:T(8,128)(2,1)}, u32[]{:S(2)}, u32[]{:S(2)}) collective-permute-start(bf16[2,192,384]{2,1,0:T(8,128)(2,1)} %bitcast.9.refs_4_), channel_id=1, source_target_pairs={{0,16},{1,17},{2,18},{3,19},{4,20},{5,21},{6,22},{7,23},{8,24},{9,... | collective-permute-start | bytes 884744 | tf_op jit(solution)/shard_map/ppermute | solution.py:140
  144.0 15.3 %collective-permute-start.23 = (bf16[2,192,384]{2,1,0:T(8,128)(2,1)}, bf16[2,192,384]{2,1,0:T(8,128)(2,1)}, u32[]{:S(2)}, u32[]{:S(2)}) collective-permute-start(bf16[2,192,384]{2,1,0:T(8,128)(2,1)} %bitcast.9.refs_4_), channel_id=1, source_target_pairs={{0,24},{1,25},{2,26},{3,27},{4,28},{5,29},{6,30},{7,31},{8,0},{9,1... | collective-permute-start | bytes 884744 | tf_op jit(solution)/shard_map/ppermute | solution.py:140
  148.8 14.6 %all-to-all-start.4 = ((bf16[8,1,96,384]{3,2,1,0:T(8,128)(2,1)}), bf16[8,1,96,384]{3,2,1,0:T(8,128)(2,1)}, u32[]{:S(2)}, u32[]{:S(2)}) async-start(bf16[8,1,96,384]{3,2,1,0:T(8,128)(2,1)} %weight_grads.3), calls=%async_computation.4 | async-start | bytes 1179648 | tf_op jit(solution)/shard_map/all_to_all | solution.py:134
  163.4 24.5 %all-to-all-start.5 = ((bf16[8,2,96,384]{3,2,1,0:T(8,128)(2,1)}), bf16[8,2,96,384]{3,2,1,0:T(8,128)(2,1)}, u32[]{:S(2)}, u32[]{:S(2)}) async-start(bf16[8,2,96,384]{3,2,1,0:T(8,128)(2,1)} %weight_grads.4), calls=%async_computation.5 | async-start | bytes 2359296 | tf_op jit(solution)/shard_map/all_to_all | solution.py:134
  168.6 7.5 %collective-permute-start.24 = (bf16[192,768]{1,0:T(8,128)(2,1)S(1)}, bf16[192,768]{1,0:T(8,128)(2,1)S(1)}, u32[]{:S(2)}, u32[]{:S(2)}) collective-permute-start(bf16[192,768]{1,0:T(8,128)(2,1)S(1)} %get-tuple-element.117), channel_id=1, source_target_pairs={{0,32},{32,0},{64,96},{96,64},{1,33},{33,1},{65,97},{97,65},{2,34}... | collective-permute-start | bytes 884744 | tf_op jit(solution)/shard_map/ppermute | solution.py:316
  172.0 4.2 %collective-permute-start.25 = (bf16[192,768]{1,0:T(8,128)(2,1)S(1)}, bf16[192,768]{1,0:T(8,128)(2,1)S(1)}, u32[]{:S(2)}, u32[]{:S(2)}) collective-permute-start(bf16[192,768]{1,0:T(8,128)(2,1)S(1)} %get-tuple-element.116), channel_id=1, source_target_pairs={{0,32},{32,0},{64,96},{96,64},{1,33},{33,1},{65,97},{97,65},{2,34}... | collective-permute-start | bytes 884744 | tf_op jit(solution)/shard_map/ppermute | solution.py:316
  172.0 11.0 %collective-permute-start.27 = (bf16[1,192,384]{2,1,0:T(8,128)(2,1)}, bf16[1,192,384]{2,1,0:T(8,128)(2,1)S(1)}, u32[]{:S(2)}, u32[]{:S(2)}) collective-permute-start(bf16[1,192,384]{2,1,0:T(8,128)(2,1)} %bitcast.71), channel_id=1, source_target_pairs={{0,8},{1,9},{2,10},{3,11},{4,12},{5,13},{6,14},{7,15},{8,16},{9,17... | collective-permute-start | bytes 442376 | tf_op jit(solution)/shard_map/ppermute | solution.py:140
  173.6 9.5 %collective-permute-start.28 = (bf16[1,192,384]{2,1,0:T(8,128)(2,1)}, bf16[1,192,384]{2,1,0:T(8,128)(2,1)S(1)}, u32[]{:S(2)}, u32[]{:S(2)}) collective-permute-start(bf16[1,192,384]{2,1,0:T(8,128)(2,1)} %bitcast.72), channel_id=1, source_target_pairs={{0,16},{1,17},{2,18},{3,19},{4,20},{5,21},{6,22},{7,23},{8,24},{9,... | collective-permute-start | bytes 442376 | tf_op jit(solution)/shard_map/ppermute | solution.py:140
  175.6 7.5 %collective-permute-start.29 = (bf16[1,192,384]{2,1,0:T(8,128)(2,1)}, bf16[1,192,384]{2,1,0:T(8,128)(2,1)S(1)}, u32[]{:S(2)}, u32[]{:S(2)}) collective-permute-start(bf16[1,192,384]{2,1,0:T(8,128)(2,1)} %bitcast.73), channel_id=1, source_target_pairs={{0,24},{1,25},{2,26},{3,27},{4,28},{5,29},{6,30},{7,31},{8,0},{9,1... | collective-permute-start | bytes 442376 | tf_op jit(solution)/shard_map/ppermute | solution.py:140
  177.8 16.7 %collective-permute-start.26 = (bf16[192,768]{1,0:T(8,128)(2,1)}, bf16[192,768]{1,0:T(8,128)(2,1)}, u32[]{:S(2)}, u32[]{:S(2)}) collective-permute-start(bf16[192,768]{1,0:T(8,128)(2,1)} %select_convert_fusion), channel_id=1, source_target_pairs={{0,64},{32,96},{64,0},{96,32},{1,65},{33,97},{65,1},{97,33},{2,66}... | collective-permute-start | bytes 884744 | tf_op jit(solution)/shard_map/ppermute | solution.py:321
  187.9 15.5 %all-to-all-start.6 = ((bf16[8,1,96,384]{3,2,1,0:T(8,128)(2,1)}), bf16[8,1,96,384]{3,2,1,0:T(8,128)(2,1)}, u32[]{:S(2)}, u32[]{:S(2)}) async-start(bf16[8,1,96,384]{3,2,1,0:T(8,128)(2,1)} %weight_grads.5), calls=%async_computation.6 | async-start | bytes 1179648 | tf_op jit(solution)/shard_map/all_to_all | solution.py:134
  (14 other events, 22.9 us)

commit v5 on v4

--- a/solution.py
+++ b/solution.py
@@ -275,10 +275,10 @@
         count = gs[0].shape[0]
         return pl.pallas_call(
             weights_kernel,
-            grid=(2,),
-            in_specs=[pl.BlockSpec((rows, part // 2), lambda i: (0, i))] * NY
+            grid=(1,),
+            in_specs=[pl.BlockSpec((rows, part), lambda i: (0, i))] * NY
             + [pl.BlockSpec((count, rows, width), lambda i: (0, 0, 0))] * NY,
-            out_specs=pl.BlockSpec((NZX // 2, count, own, width), lambda i: (i, 0, 0, 0)),
+            out_specs=pl.BlockSpec((NZX, count, own, width), lambda i: (i, 0, 0, 0)),
             out_shape=jax.ShapeDtypeStruct((NZX, count, own, width), BF16),
             compiler_params=pltpu.CompilerParams(vmem_limit_bytes=56 * 1024 * 1024),
             name="weight_grads",

time: 207 us -> 206 us (level)
  transfers between devices with their start and end apart: 36 -> 36, of which waited for: 12 -> 13; matrix products, arithmetic and copies ran while one was open for 16% -> 16% of each run, Pallas kernels for 18% -> 18%
where the time goes in v5:
time: 206 us; the launch traced here: 205 us
  starting transfers between devices  73.7 us (36%)
  waiting for transfers between devices  36.7 us (18%)
  Pallas kernels  36.6 us (18%)
  other arithmetic  18.4 us (9%)
  matrix products  14.1 us (7%)
  blocking collectives  12.8 us (6%)
  local copies, waits for them, and re-layouts  11.9 us (6%)
    ppermute x21, starting transfers between devices, shift(): lax.ppermute(array, 'blk', [(i, (i + by * NZX) % (NY * NZX)) for i in ran...  29.2 us
    all_to_all x6, starting transfers between devices, exchange(): lax.all_to_all(array, 'blk', 0, 0, tiled=True, axis_index_groups=along_zx)  26.8 us
    ppermute x21, waiting for transfers between devices, shift(): lax.ppermute(array, 'blk', [(i, (i + by * NZX) % (NY * NZX)) for i in ran...  15.1 us
    all_to_all x6, waiting for transfers between devices, exchange(): lax.all_to_all(array, 'blk', 0, 0, tiled=True, axis_index_groups=along_zx)  14.1 us
    all_to_all x1, blocking collectives, exchange(): lax.all_to_all(array, 'blk', 0, 0, tiled=True, axis_index_groups=along_zx)  12.8 us
    pallas_call x1, Pallas kernels, per_device(): pl.pallas_call(grads_kernel, grid=grid, in_specs=in_specs + [pl.BlockSpec...  12.4 us
    pallas_call x3, Pallas kernels, weight_terms(): pl.pallas_call(weights_kernel, grid=(1,), in_specs=[pl.BlockSpec((rows, p...  10.6 us
    pallas_call x1, Pallas kernels, per_device(): pl.pallas_call(stats_kernel, grid=grid, in_specs=in_specs, out_specs=[pl....  10.2 us
  transfers between devices with their start and end apart: 36, of which 13 were waited for; matrix products, arithmetic and copies ran while one was open for 16% of the time, Pallas kernels for 18%

profile of v5, /device:TPU:1, one launch (start us, length us, event | category | flops | bytes accessed | tf_op | source)
XLA Modules:
  0.0 205.2 jit_solution(17107154743078202462)
XLA Ops:
  0.6 4.5 %collective-permute-start.2 = (bf16[192,768]{1,0:T(8,128)(2,1)}, bf16[192,768]{1,0:T(8,128)(2,1)S(1)}, u32[]{:S(2)}, u32[]{:S(2)}) collective-permute-start(bf16[192,768]{1,0:T(8,128)(2,1)} %bitcast.80), channel_id=1, source_target_pairs={{0,64},{32,96},{64,0},{96,32},{1,65},{33,97},{65,1},{97,33},{2,66}... | collective-permute-start | bytes 884744 | tf_op jit(solution)/shard_map/ppermute | solution.py:169
  6.1 6.0 %collective-permute-done.2 = bf16[192,768]{1,0:T(8,128)(2,1)S(1)} collective-permute-done((bf16[192,768]{1,0:T(8,128)(2,1)}, bf16[192,768]{1,0:T(8,128)(2,1)S(1)}, u32[]{:S(2)}, u32[]{:S(2)}) %collective-permute-start.2) | collective-permute-done | bytes 294944 | tf_op jit(solution)/shard_map/ppermute | solution.py:169
  13.3 3.0 %collective-permute-start = (bf16[192,768]{1,0:T(8,128)(2,1)}, bf16[192,768]{1,0:T(8,128)(2,1)}, u32[]{:S(2)}, u32[]{:S(2)}) collective-permute-start(bf16[192,768]{1,0:T(8,128)(2,1)} %bitcast.83), channel_id=1, source_target_pairs={{0,64},{32,96},{64,0},{96,32},{1,65},{33,97},{65,1},{97,33},{2,66}... | collective-permute-start | bytes 884744 | tf_op jit(solution)/shard_map/ppermute | solution.py:170
  16.3 1.8 select_select_fusion.4
  18.1 5.1 %fusion.1 = bf16[3,192,384]{2,1,0:T(8,128)(2,1)S(1)} fusion(bf16[3072,3,384]{2,0,1:T(8,128)(2,1)} %param.9, bf16[192,768]{1,0:T(8,128)(2,1)S(1)} %get-tuple-element.115, bf16[192,768]{1,0:T(8,128)(2,1)S(1)} %get-tuple-element.114, bf16[192,768]{1,0:T(8,128)(2,1)S(1)} %get-tuple-element.113, bf16[192,768]{1,0:T(8,128)(2,1)S(1)} %get-tuple-element.112), kind=kOutput, calls=%fused_computation.4 | convolution fusion | flops 1363894272 | bytes 8699904 | tf_op jit(solution)/shard_map/vd,dch->cvh/dot_general | solution.py:172
  24.6 1.4 collective-permute-done.5
  28.2 1.8 broadcast_in_dim.40
  30.0 4.7 %all-to-all-start = ((bf16[8,2,192,384]{3,2,1,0:T(8,128)(2,1)}), bf16[8,2,192,384]{3,2,1,0:T(8,128)(2,1)}, u32[]{:S(2)}, u32[]{:S(2)}) async-start(bf16[8,2,192,384]{3,2,1,0:T(8,128)(2,1)} %broadcast_in_dim.40), calls=%async_computation | async-start | bytes 4718592 | tf_op jit(solution)/shard_map/all_to_all | solution.py:134
  34.9 1.4 collective-permute-start.6
  36.2 2.6 %collective-permute-start.7 = (bf16[2,192,384]{2,1,0:T(8,128)(2,1)S(1)}, bf16[2,192,384]{2,1,0:T(8,128)(2,1)S(1)}, u32[]{:S(2)}, u32[]{:S(2)}) collective-permute-start(bf16[2,192,384]{2,1,0:T(8,128)(2,1)S(1)} %slice.38.refs_0_.refs_4_), channel_id=1, source_target_pairs={{0,16},{1,17},{2,18},{3,19},{4,20},{5,21},{6,22},{7,23},{8,24},{9,... | collective-permute-start | bytes 884744 | tf_op jit(solution)/shard_map/ppermute | solution.py:140
  39.9 2.1 %select_select_fusion.5 = (bf16[192,768]{1,0:T(8,128)(2,1)}, bf16[192,768]{1,0:T(8,128)(2,1)S(1)}, bf16[192,768]{1,0:T(8,128)(2,1)}) fusion(bf16[192,768]{1,0:T(8,128)(2,1)} %copy-done.9, bf16[192,768]{1,0:T(8,128)(2,1)} %copy-done.10, bf16[192,768]{1,0:T(8,128)(2,1)S(1)} %get-tuple-element.112, bf16[192,768]{1,0:T(8,128)(2,1)} %copy-done.8, pred[]{:T(512)S(6)} %eq.36, ...), kind=kLoop, calls=%fused_computation.46 | loop fusion | flops 1327104 | bytes 2064393 | tf_op jit(solution)/shard_map/jit(_where)/select_n | solution.py:162
  42.4 1.7 convolution_convert_fusion.2.refs_8_
  44.9 1.6 collective-permute-start.11
  46.5 5.2 %collective-permute-done.7.refs_2_.refs_6_ = bf16[2,192,384]{2,1,0:T(8,128)(2,1)S(1)} collective-permute-done((bf16[2,192,384]{2,1,0:T(8,128)(2,1)S(1)}, bf16[2,192,384]{2,1,0:T(8,128)(2,1)S(1)}, u32[]{:S(2)}, u32[]{:S(2)}) %collective-permute-start.7) | collective-permute-done | bytes 294944 | tf_op jit(solution)/shard_map/ppermute | solution.py:140
  51.7 2.6 %select_select_fusion = (bf16[192,768]{1,0:T(8,128)(2,1)}, bf16[192,768]{1,0:T(8,128)(2,1)}, bf16[192,768]{1,0:T(8,128)(2,1)}, bf16[192,768]{1,0:T(8,128)(2,1)}) fusion(bf16[192,768]{1,0:T(8,128)(2,1)} %copy-done.15, bf16[192,768]{1,0:T(8,128)(2,1)} %copy-done.14, bf16[192,768]{1,0:T(8,128)(2,1)} %copy-done.13, bf16[192,768]{1,0:T(8,128)(2,1)} %copy-done.16, ...), kind=kLoop, calls=%fused_computation.41 | loop fusion | flops 1769472 | bytes 2359308 | tf_op jit(solution)/shard_map/jit(_where)/select_n | solution.py:162
  55.4 4.0 %collective-permute-start.13 = (bf16[192,768]{1,0:T(8,128)(2,1)}, bf16[192,768]{1,0:T(8,128)(2,1)}, u32[]{:S(2)}, u32[]{:S(2)}) collective-permute-start(bf16[192,768]{1,0:T(8,128)(2,1)} %get-tuple-element.119), channel_id=1, source_target_pairs={{0,16},{1,17},{2,18},{3,19},{4,20},{5,21},{6,22},{7,23},{8,24},{9,... | collective-permute-start | bytes 884744 | tf_op jit(solution)/shard_map/ppermute | solution.py:140
  60.4 4.3 %all-to-all-done.q_ref.g_ref = bf16[8,2,192,384]{3,2,1,0:T(8,128)(2,1)} async-done(((bf16[8,2,192,384]{3,2,1,0:T(8,128)(2,1)}), bf16[8,2,192,384]{3,2,1,0:T(8,128)(2,1)}, u32[]{:S(2)}, u32[]{:S(2)}) %all-to-all-start) | async-done | bytes 2359328 | tf_op jit(solution)/shard_map/all_to_all | solution.py:134
  65.4 10.2 %attention_stats.1 = (f32[3,2,1536]{2,1,0:T(2,128)}, bf16[8,192,384]{2,1,0:T(8,128)(2,1)}) custom-call(bf16[8,2,192,384]{3,2,1,0:T(8,128)(2,1)} %all-to-all-done.q_ref.g_ref, bf16[8,2,192,384]{3,2,1,0:T(8,128)(2,1)} %all-to-all-done.q_ref.g_ref, bf16[2,192,384]{2,1,0:T(8,128)(2,1)} %copy-done.1, bf16[2,192,384]{2,1,0:T(8,128)(2,1)} %copy-done.2, ...), custom_call_target="tpu_custom_call" | custom-call | tf_op jit(solution)/shard_map/attention_stats/pallas_call | solution.py:220
  75.7 1.4 collective-permute-done.13.refs_2_
  77.9 12.8 %all_to_all.35.refs_11_ = f32[8,3,2,1536]{3,2,1,0:T(2,128)} all-to-all(f32[8,3,2,1536]{3,2,1,0:T(2,128)S(1)} %broadcast_in_dim.44), channel_id=1, replica_groups={{0,1,2,3,4,5,6,7},{8,9,10,11,12,13,14,15},{16,17,18,19,20,21,22,23},{24..., dimensions={0} | all-to-all | bytes 589824 | tf_op jit(solution)/shard_map/all_to_all | solution.py:134
  90.7 3.7 %all-to-all-start.1 = ((bf16[8,192,384]{2,1,0:T(8,128)(2,1)}), bf16[8,192,384]{2,1,0:T(8,128)(2,1)S(1)}, u32[]{:S(2)}, u32[]{:S(2)}) async-start(bf16[8,192,384]{2,1,0:T(8,128)(2,1)} %get-tuple-element.59), calls=%async_computation.1 | async-start | bytes 2359296 | tf_op jit(solution)/shard_map/all_to_all | solution.py:134
  94.5 12.4 %attention_grads.1 = (bf16[8,192,384]{2,1,0:T(8,128)(2,1)}, bf16[400,384]{1,0:T(8,128)(2,1)}, bf16[400,384]{1,0:T(8,128)(2,1)}, bf16[400,384]{1,0:T(8,128)(2,1)}, bf16[400,384]{1,0:T(8,128)(2,1)}) custom-call(bf16[8,2,192,384]{3,2,1,0:T(8,128)(2,1)} %all-to-all-done.q_ref.g_ref, bf16[8,2,192,384]{3,2,1,0:T(8,128)(2,1)} %all-to-all-done.q_ref.g_ref, ...), custom_call_target="tpu_custom_call" | custom-call | tf_op jit(solution)/shard_map/attention_grads/pallas_call | solution.py:253
  106.9 4.5 %all-to-all-done.1.out_ref = bf16[8,192,384]{2,1,0:T(8,128)(2,1)S(1)} async-done(((bf16[8,192,384]{2,1,0:T(8,128)(2,1)}), bf16[8,192,384]{2,1,0:T(8,128)(2,1)S(1)}, u32[]{:S(2)}, u32[]{:S(2)}) %all-to-all-start.1) | async-done | bytes 1179680 | tf_op jit(solution)/shard_map/all_to_all | solution.py:134
  112.5 3.6 %all-to-all-start.3 = ((bf16[8,192,384]{2,1,0:T(8,128)(2,1)}), bf16[8,192,384]{2,1,0:T(8,128)(2,1)S(1)}, u32[]{:S(2)}, u32[]{:S(2)}) async-start(bf16[8,192,384]{2,1,0:T(8,128)(2,1)} %get-tuple-element.81), calls=%async_computation.3 | async-start | bytes 2359296 | tf_op jit(solution)/shard_map/all_to_all | solution.py:134
  116.1 1.4 collective-permute-start.20
  117.5 2.6 %collective-permute-start.19 = (bf16[400,384]{1,0:T(8,128)(2,1)}, bf16[400,384]{1,0:T(8,128)(2,1)}, u32[]{:S(2)}, u32[]{:S(2)}) collective-permute-start(bf16[400,384]{1,0:T(8,128)(2,1)} %get-tuple-element.68), channel_id=1, source_target_pairs={{0,16},{1,17},{2,18},{3,19},{4,20},{5,21},{6,22},{7,23},{8,24},{9,... | collective-permute-start | bytes 921608 | tf_op jit(solution)/shard_map/ppermute | solution.py:140
  121.2 1.6 constant_dynamic-slice_fusion.stat_ref
  122.8 3.4 %combine_out.1 = bf16[192,384]{1,0:T(8,128)(2,1)} custom-call(bf16[8,192,384]{2,1,0:T(8,128)(2,1)} %copy-done.5, f32[8,3,2,192]{3,2,1,0:T(2,128)} %constant_dynamic-slice_fusion.stat_ref), custom_call_target="tpu_custom_call" | custom-call | tf_op jit(solution)/shard_map/combine_out/pallas_call | solution.py:239
  127.3 1.6 collective-permute-start.17
  129.0 4.5 %collective-permute-done.19 = bf16[400,384]{1,0:T(8,128)(2,1)} collective-permute-done((bf16[400,384]{1,0:T(8,128)(2,1)}, bf16[400,384]{1,0:T(8,128)(2,1)}, u32[]{:S(2)}, u32[]{:S(2)}) %collective-permute-start.19) | collective-permute-done | bytes 307232 | tf_op jit(solution)/shard_map/ppermute | solution.py:140
  134.0 1.4 convert_add_fusion
  137.0 2.0 collective-permute-done.15.refs_5_
  141.1 2.9 %collective-permute-start.22 = (bf16[2,192,384]{2,1,0:T(8,128)(2,1)}, bf16[2,192,384]{2,1,0:T(8,128)(2,1)}, u32[]{:S(2)}, u32[]{:S(2)}) collective-permute-start(bf16[2,192,384]{2,1,0:T(8,128)(2,1)} %bitcast.9.refs_4_), channel_id=1, source_target_pairs={{0,16},{1,17},{2,18},{3,19},{4,20},{5,21},{6,22},{7,23},{8,24},{9,... | collective-permute-start | bytes 884744 | tf_op jit(solution)/shard_map/ppermute | solution.py:140
  144.0 3.3 %weight_grads.3 = bf16[8,1,96,384]{3,2,1,0:T(8,128)(2,1)} custom-call(bf16[192,768]{1,0:T(8,128)(2,1)} %get-tuple-element.71.refs_0_, bf16[192,768]{1,0:T(8,128)(2,1)} %collective-permute-done.12.refs_1_, bf16[192,768]{1,0:T(8,128)(2,1)} %collective-permute-done.13.refs_2_, bf16[192,768]{1,0:T(8,128)(2,1)} %collective-permute-done.14.refs_3_, ...), custom_call_target="tpu_custom_call" | custom-call | tf_op jit(solution)/shard_map/weight_grads/pallas_call | solution.py:276
  148.8 4.8 %all-to-all-start.4 = ((bf16[8,1,96,384]{3,2,1,0:T(8,128)(2,1)}), bf16[8,1,96,384]{3,2,1,0:T(8,128)(2,1)}, u32[]{:S(2)}, u32[]{:S(2)}) async-start(bf16[8,1,96,384]{3,2,1,0:T(8,128)(2,1)} %weight_grads.3), calls=%async_computation.4 | async-start | bytes 1179648 | tf_op jit(solution)/shard_map/all_to_all | solution.py:134
  153.6 5.7 %fusion = bf16[4,192,768]{2,1,0:T(8,128)(2,1)S(1)} fusion(bf16[4,768,3,384]{3,1,0,2:T(8,128)(2,1)} %bitcast.85, bf16[2,192,384]{2,1,0:T(8,128)(2,1)} %bitcast.9.refs_4_, bf16[1,192,384]{2,1,0:T(8,128)(2,1)} %bitcast.70), kind=kOutput, calls=%fused_computation.2 | convolution fusion | flops 1360429056 | bytes 8699904 | tf_op jit(solution)/shard_map/cvh,sdch->svd/dot_general | solution.py:298
  159.3 4.1 %weight_grads.4 = bf16[8,2,96,384]{3,2,1,0:T(8,128)(2,1)} custom-call(bf16[192,768]{1,0:T(8,128)(2,1)} %get-tuple-element.85.refs_0_, bf16[192,768]{1,0:T(8,128)(2,1)} %collective-permute-done.9.refs_1_, bf16[192,768]{1,0:T(8,128)(2,1)} %copy-done.7, bf16[192,768]{1,0:T(8,128)(2,1)} %collective-permute-done.11.refs_3_, bf16[2,192,384]{2,1,0:T(8,128)(2,1)} %bitcast.9.refs_4_, ...), custom_call_target="tpu_custom_call" | custom-call | tf_op jit(solution)/shard_map/weight_grads/pallas_call | solution.py:276
  163.4 5.1 %all-to-all-start.5 = ((bf16[8,2,96,384]{3,2,1,0:T(8,128)(2,1)}), bf16[8,2,96,384]{3,2,1,0:T(8,128)(2,1)}, u32[]{:S(2)}, u32[]{:S(2)}) async-start(bf16[8,2,96,384]{3,2,1,0:T(8,128)(2,1)} %weight_grads.4), calls=%async_computation.5 | async-start | bytes 2359296 | tf_op jit(solution)/shard_map/all_to_all | solution.py:134
  168.6 3.3 %collective-permute-start.24 = (bf16[192,768]{1,0:T(8,128)(2,1)S(1)}, bf16[192,768]{1,0:T(8,128)(2,1)S(1)}, u32[]{:S(2)}, u32[]{:S(2)}) collective-permute-start(bf16[192,768]{1,0:T(8,128)(2,1)S(1)} %get-tuple-element.117), channel_id=1, source_target_pairs={{0,32},{32,0},{64,96},{96,64},{1,33},{33,1},{65,97},{97,65},{2,34}... | collective-permute-start | bytes 884744 | tf_op jit(solution)/shard_map/ppermute | solution.py:316
  172.0 1.6 collective-permute-start.27
  173.5 2.0 collective-permute-start.28
  177.8 3.3 %collective-permute-start.26 = (bf16[192,768]{1,0:T(8,128)(2,1)}, bf16[192,768]{1,0:T(8,128)(2,1)}, u32[]{:S(2)}, u32[]{:S(2)}) collective-permute-start(bf16[192,768]{1,0:T(8,128)(2,1)} %select_convert_fusion), channel_id=1, source_target_pairs={{0,64},{32,96},{64,0},{96,32},{1,65},{33,97},{65,1},{97,33},{2,66}... | collective-permute-start | bytes 884744 | tf_op jit(solution)/shard_map/ppermute | solution.py:321
  184.4 3.2 %weight_grads.5 = bf16[8,1,96,384]{3,2,1,0:T(8,128)(2,1)} custom-call(bf16[192,768]{1,0:T(8,128)(2,1)} %get-tuple-element.85.refs_0_, bf16[192,768]{1,0:T(8,128)(2,1)} %collective-permute-done.9.refs_1_, bf16[192,768]{1,0:T(8,128)(2,1)} %copy-done.7, bf16[192,768]{1,0:T(8,128)(2,1)} %collective-permute-done.11.refs_3_, bf16[1,192,384]{2,1,0:T(8,128)(2,1)} %bitcast.74, ...), custom_call_target="tpu_custom_call" | custom-call | tf_op jit(solution)/shard_map/weight_grads/pallas_call | solution.py:276
  187.7 4.8 %all-to-all-start.6 = ((bf16[8,1,96,384]{3,2,1,0:T(8,128)(2,1)}), bf16[8,1,96,384]{3,2,1,0:T(8,128)(2,1)}, u32[]{:S(2)}, u32[]{:S(2)}) async-start(bf16[8,1,96,384]{3,2,1,0:T(8,128)(2,1)} %weight_grads.5), calls=%async_computation.6 | async-start | bytes 1179648 | tf_op jit(solution)/shard_map/all_to_all | solution.py:134
  192.5 1.8 convert_reduce_fusion.1
  194.4 2.1 %fusion.26 = bf16[192,1,768]{2,0,1:T(8,128)(2,1)} fusion(bf16[192,768]{1,0:T(8,128)(2,1)} %collective-permute-done.26, bf16[192,768]{1,0:T(8,128)(2,1)} %copy-done.12, bf16[192,768]{1,0:T(8,128)(2,1)} %copy-done.11, pred[]{:T(512)S(6)} %eq.26, bf16[4,192,768]{2,1,0:T(8,128)(2,1)S(1)} %fusion, pred[]{:T(512)S(6)} %eq.27), kind=kLoop, calls=%fused_computation.37 | loop fusion | flops 1769472 | bytes 2359298 | tf_op jit(solution)/shard_map/broadcast_in_dim | solution.py:324
  196.5 1.5 convert_reduce_fusion
  198.0 5.2 %all-to-all-done.6 = bf16[8,1,96,384]{3,2,1,0:T(8,128)(2,1)} async-done(((bf16[8,1,96,384]{3,2,1,0:T(8,128)(2,1)}), bf16[8,1,96,384]{3,2,1,0:T(8,128)(2,1)}, u32[]{:S(2)}, u32[]{:S(2)}) %all-to-all-start.6) | async-done | bytes 589856 | tf_op jit(solution)/shard_map/all_to_all | solution.py:134
  (116 shorter events, 28.5 us)
Async XLA Ops:
  0.6 26.6 %copy-start = (bf16[3072,384]{1,0:T(8,128)(2,1)S(1)}, bf16[3072,384]{1,0:T(8,128)(2,1)}, u32[]{:S(2)}) copy-start(bf16[3072,384]{1,0:T(8,128)(2,1)} %param.10) | copy-start | bytes 7077892
  0.6 11.4 %collective-permute-start.2 = (bf16[192,768]{1,0:T(8,128)(2,1)}, bf16[192,768]{1,0:T(8,128)(2,1)S(1)}, u32[]{:S(2)}, u32[]{:S(2)}) collective-permute-start(bf16[192,768]{1,0:T(8,128)(2,1)} %bitcast.80), channel_id=1, source_target_pairs={{0,64},{32,96},{64,0},{96,32},{1,65},{33,97},{65,1},{97,33},{2,66}... | collective-permute-start | bytes 884744 | tf_op jit(solution)/shard_map/ppermute | solution.py:169
  5.2 11.1 %collective-permute-start.1 = (bf16[192,768]{1,0:T(8,128)(2,1)}, bf16[192,768]{1,0:T(8,128)(2,1)S(1)}, u32[]{:S(2)}, u32[]{:S(2)}) collective-permute-start(bf16[192,768]{1,0:T(8,128)(2,1)} %bitcast.81), channel_id=1, source_target_pairs={{0,32},{32,0},{64,96},{96,64},{1,33},{33,1},{65,97},{97,65},{2,34}... | collective-permute-start | bytes 884744 | tf_op jit(solution)/shard_map/ppermute | solution.py:148
  12.1 4.2 %collective-permute-start.3 = (bf16[192,768]{1,0:T(8,128)(2,1)S(1)}, bf16[192,768]{1,0:T(8,128)(2,1)S(1)}, u32[]{:S(2)}, u32[]{:S(2)}) collective-permute-start(bf16[192,768]{1,0:T(8,128)(2,1)S(1)} %collective-permute-done.2), channel_id=1, source_target_pairs={{0,32},{32,0},{64,96},{96,64},{1,33},{33,1},{65,97},{97,65},{2,34}... | collective-permute-start | bytes 884744 | tf_op jit(solution)/shard_map/ppermute | solution.py:149
  13.3 11.3 %collective-permute-start.4 = (bf16[192,768]{1,0:T(8,128)(2,1)}, bf16[192,768]{1,0:T(8,128)(2,1)}, u32[]{:S(2)}, u32[]{:S(2)}) collective-permute-start(bf16[192,768]{1,0:T(8,128)(2,1)} %bitcast.82), channel_id=1, source_target_pairs={{0,32},{32,0},{64,96},{96,64},{1,33},{33,1},{65,97},{97,65},{2,34}... | collective-permute-start | bytes 884744 | tf_op jit(solution)/shard_map/ppermute | solution.py:148
  13.3 9.9 %collective-permute-start = (bf16[192,768]{1,0:T(8,128)(2,1)}, bf16[192,768]{1,0:T(8,128)(2,1)}, u32[]{:S(2)}, u32[]{:S(2)}) collective-permute-start(bf16[192,768]{1,0:T(8,128)(2,1)} %bitcast.83), channel_id=1, source_target_pairs={{0,64},{32,96},{64,0},{96,32},{1,65},{33,97},{65,1},{97,33},{2,66}... | collective-permute-start | bytes 884744 | tf_op jit(solution)/shard_map/ppermute | solution.py:170
  18.1 5.1 %copy-start.8 = (bf16[192,768]{1,0:T(8,128)(2,1)}, bf16[192,768]{1,0:T(8,128)(2,1)S(1)}, u32[]{:S(2)}) copy-start(bf16[192,768]{1,0:T(8,128)(2,1)S(1)} %get-tuple-element.113) | copy-start | bytes 884740
  18.1 5.1 %copy-start.9 = (bf16[192,768]{1,0:T(8,128)(2,1)}, bf16[192,768]{1,0:T(8,128)(2,1)S(1)}, u32[]{:S(2)}) copy-start(bf16[192,768]{1,0:T(8,128)(2,1)S(1)} %get-tuple-element.114) | copy-start | bytes 884740
  18.1 5.1 %copy-start.10 = (bf16[192,768]{1,0:T(8,128)(2,1)}, bf16[192,768]{1,0:T(8,128)(2,1)S(1)}, u32[]{:S(2)}) copy-start(bf16[192,768]{1,0:T(8,128)(2,1)S(1)} %get-tuple-element.115) | copy-start | bytes 884740
  18.1 7.9 %copy-start.17 = (bf16[192,1,768]{2,0,1:T(8,128)(2,1)S(1)}, bf16[192,1,768]{2,0,1:T(8,128)(2,1)}, u32[]{:S(2)}) copy-start(bf16[192,1,768]{2,0,1:T(8,128)(2,1)} %param.8) | copy-start | bytes 884740
  23.2 2.8 %collective-permute-start.5 = (bf16[192,768]{1,0:T(8,128)(2,1)}, bf16[192,768]{1,0:T(8,128)(2,1)S(1)}, u32[]{:S(2)}, u32[]{:S(2)}) collective-permute-start(bf16[192,768]{1,0:T(8,128)(2,1)} %collective-permute-done), channel_id=1, source_target_pairs={{0,32},{32,0},{64,96},{96,64},{1,33},{33,1},{65,97},{97,65},{2,34}... | collective-permute-start | bytes 884744 | tf_op jit(solution)/shard_map/ppermute | solution.py:149
  30.0 34.7 %all-to-all-start = ((bf16[8,2,192,384]{3,2,1,0:T(8,128)(2,1)}), bf16[8,2,192,384]{3,2,1,0:T(8,128)(2,1)}, u32[]{:S(2)}, u32[]{:S(2)}) async-start(bf16[8,2,192,384]{3,2,1,0:T(8,128)(2,1)} %broadcast_in_dim.40), calls=%async_computation | async-start | bytes 4718592 | tf_op jit(solution)/shard_map/all_to_all | solution.py:134
  34.8 19.5 %copy-start.1 = (bf16[2,192,384]{2,1,0:T(8,128)(2,1)}, bf16[2,192,384]{2,1,0:T(8,128)(2,1)S(1)}, u32[]{:S(2)}) copy-start(bf16[2,192,384]{2,1,0:T(8,128)(2,1)S(1)} %slice.38.refs_0_.refs_4_) | copy-start | bytes 884740
  34.8 24.6 %copy-start.24 = (s32[256,1]{0,1:T(1,128)S(1)}, s32[256,1]{0,1:T(1,128)}, u32[]{:S(2)}) copy-start(s32[256,1]{0,1:T(1,128)} %param.13) | copy-start | bytes 3076
  34.8 24.8 %copy-start.25 = (bf16[256,1,384]{2,0,1:T(8,128)(2,1)S(1)}, bf16[256,1,384]{2,0,1:T(8,128)(2,1)}, u32[]{:S(2)}) copy-start(bf16[256,1,384]{2,0,1:T(8,128)(2,1)} %param.12) | copy-start | bytes 589828
  34.9 10.0 %collective-permute-start.6 = (bf16[2,192,384]{2,1,0:T(8,128)(2,1)S(1)}, bf16[2,192,384]{2,1,0:T(8,128)(2,1)S(1)}, u32[]{:S(2)}, u32[]{:S(2)}) collective-permute-start(bf16[2,192,384]{2,1,0:T(8,128)(2,1)S(1)} %slice.38.refs_0_.refs_4_), channel_id=1, source_target_pairs={{0,8},{1,9},{2,10},{3,11},{4,12},{5,13},{6,14},{7,15},{8,16},{9,17... | collective-permute-start | bytes 884744 | tf_op jit(solution)/shard_map/ppermute | solution.py:140
  36.2 15.5 %collective-permute-start.7 = (bf16[2,192,384]{2,1,0:T(8,128)(2,1)S(1)}, bf16[2,192,384]{2,1,0:T(8,128)(2,1)S(1)}, u32[]{:S(2)}, u32[]{:S(2)}) collective-permute-start(bf16[2,192,384]{2,1,0:T(8,128)(2,1)S(1)} %slice.38.refs_0_.refs_4_), channel_id=1, source_target_pairs={{0,16},{1,17},{2,18},{3,19},{4,20},{5,21},{6,22},{7,23},{8,24},{9,... | collective-permute-start | bytes 884744 | tf_op jit(solution)/shard_map/ppermute | solution.py:140
  38.8 12.9 %collective-permute-start.8 = (bf16[2,192,384]{2,1,0:T(8,128)(2,1)S(1)}, bf16[2,192,384]{2,1,0:T(8,128)(2,1)S(1)}, u32[]{:S(2)}, u32[]{:S(2)}) collective-permute-start(bf16[2,192,384]{2,1,0:T(8,128)(2,1)S(1)} %slice.38.refs_0_.refs_4_), channel_id=1, source_target_pairs={{0,24},{1,25},{2,26},{3,27},{4,28},{5,29},{6,30},{7,31},{8,0},{9,1... | collective-permute-start | bytes 884744 | tf_op jit(solution)/shard_map/ppermute | solution.py:140
  42.0 17.4 %collective-permute-start.9 = (bf16[192,768]{1,0:T(8,128)(2,1)S(1)}, bf16[192,768]{1,0:T(8,128)(2,1)}, u32[]{:S(2)}, u32[]{:S(2)}) collective-permute-start(bf16[192,768]{1,0:T(8,128)(2,1)S(1)} %get-tuple-element.123), channel_id=1, source_target_pairs={{0,8},{1,9},{2,10},{3,11},{4,12},{5,13},{6,14},{7,15},{8,16},{9,17... | collective-permute-start | bytes 884744 | tf_op jit(solution)/shard_map/ppermute | solution.py:140
  44.1 31.5 %collective-permute-start.10 = (bf16[192,768]{1,0:T(8,128)(2,1)}, bf16[192,768]{1,0:T(8,128)(2,1)S(1)}, u32[]{:S(2)}, u32[]{:S(2)}) collective-permute-start(bf16[192,768]{1,0:T(8,128)(2,1)} %get-tuple-element.122), channel_id=1, source_target_pairs={{0,16},{1,17},{2,18},{3,19},{4,20},{5,21},{6,22},{7,23},{8,24},{9,... | collective-permute-start | bytes 884744 | tf_op jit(solution)/shard_map/ppermute | solution.py:140
  44.9 20.5 %copy-start.2 = (bf16[2,192,384]{2,1,0:T(8,128)(2,1)}, bf16[2,192,384]{2,1,0:T(8,128)(2,1)S(1)}, u32[]{:S(2)}) copy-start(bf16[2,192,384]{2,1,0:T(8,128)(2,1)S(1)} %collective-permute-done.6.refs_1_.refs_5_) | copy-start | bytes 884740
  44.9 30.8 %collective-permute-start.11 = (bf16[192,768]{1,0:T(8,128)(2,1)}, bf16[192,768]{1,0:T(8,128)(2,1)}, u32[]{:S(2)}, u32[]{:S(2)}) collective-permute-start(bf16[192,768]{1,0:T(8,128)(2,1)} %get-tuple-element.111), channel_id=1, source_target_pairs={{0,24},{1,25},{2,26},{3,27},{4,28},{5,29},{6,30},{7,31},{8,0},{9,1... | collective-permute-start | bytes 884744 | tf_op jit(solution)/shard_map/ppermute | solution.py:140
  51.7 13.7 %copy-start.3 = (bf16[2,192,384]{2,1,0:T(8,128)(2,1)}, bf16[2,192,384]{2,1,0:T(8,128)(2,1)S(1)}, u32[]{:S(2)}) copy-start(bf16[2,192,384]{2,1,0:T(8,128)(2,1)S(1)} %collective-permute-done.7.refs_2_.refs_6_) | copy-start | bytes 884740
  51.7 13.7 %copy-start.4 = (bf16[2,192,384]{2,1,0:T(8,128)(2,1)}, bf16[2,192,384]{2,1,0:T(8,128)(2,1)S(1)}, u32[]{:S(2)}) copy-start(bf16[2,192,384]{2,1,0:T(8,128)(2,1)S(1)} %collective-permute-done.8.refs_3_.refs_7_) | copy-start | bytes 884740
  54.3 21.3 %collective-permute-start.12 = (bf16[192,768]{1,0:T(8,128)(2,1)}, bf16[192,768]{1,0:T(8,128)(2,1)}, u32[]{:S(2)}, u32[]{:S(2)}) collective-permute-start(bf16[192,768]{1,0:T(8,128)(2,1)} %get-tuple-element.120), channel_id=1, source_target_pairs={{0,8},{1,9},{2,10},{3,11},{4,12},{5,13},{6,14},{7,15},{8,16},{9,17... | collective-permute-start | bytes 884744 | tf_op jit(solution)/shard_map/ppermute | solution.py:140
  55.4 21.7 %collective-permute-start.13 = (bf16[192,768]{1,0:T(8,128)(2,1)}, bf16[192,768]{1,0:T(8,128)(2,1)}, u32[]{:S(2)}, u32[]{:S(2)}) collective-permute-start(bf16[192,768]{1,0:T(8,128)(2,1)} %get-tuple-element.119), channel_id=1, source_target_pairs={{0,16},{1,17},{2,18},{3,19},{4,20},{5,21},{6,22},{7,23},{8,24},{9,... | collective-permute-start | bytes 884744 | tf_op jit(solution)/shard_map/ppermute | solution.py:140
  59.4 17.7 %collective-permute-start.14 = (bf16[192,768]{1,0:T(8,128)(2,1)}, bf16[192,768]{1,0:T(8,128)(2,1)}, u32[]{:S(2)}, u32[]{:S(2)}) collective-permute-start(bf16[192,768]{1,0:T(8,128)(2,1)} %get-tuple-element.118), channel_id=1, source_target_pairs={{0,24},{1,25},{2,26},{3,27},{4,28},{5,29},{6,30},{7,31},{8,0},{9,1... | collective-permute-start | bytes 884744 | tf_op jit(solution)/shard_map/ppermute | solution.py:140
  75.6 15.1 %copy-start.7 = (bf16[192,768]{1,0:T(8,128)(2,1)}, bf16[192,768]{1,0:T(8,128)(2,1)S(1)}, u32[]{:S(2)}) copy-start(bf16[192,768]{1,0:T(8,128)(2,1)S(1)} %collective-permute-done.10.refs_2_) | copy-start | bytes 884740
  90.7 20.7 %all-to-all-start.1 = ((bf16[8,192,384]{2,1,0:T(8,128)(2,1)}), bf16[8,192,384]{2,1,0:T(8,128)(2,1)S(1)}, u32[]{:S(2)}, u32[]{:S(2)}) async-start(bf16[8,192,384]{2,1,0:T(8,128)(2,1)} %get-tuple-element.59), calls=%async_computation.1 | async-start | bytes 2359296 | tf_op jit(solution)/shard_map/all_to_all | solution.py:134
  112.5 34.8 %all-to-all-start.3 = ((bf16[8,192,384]{2,1,0:T(8,128)(2,1)}), bf16[8,192,384]{2,1,0:T(8,128)(2,1)S(1)}, u32[]{:S(2)}, u32[]{:S(2)}) async-start(bf16[8,192,384]{2,1,0:T(8,128)(2,1)} %get-tuple-element.81), calls=%async_computation.3 | async-start | bytes 2359296 | tf_op jit(solution)/shard_map/all_to_all | solution.py:134
  116.1 11.3 %collective-permute-start.20 = (bf16[400,384]{1,0:T(8,128)(2,1)}, bf16[400,384]{1,0:T(8,128)(2,1)}, u32[]{:S(2)}, u32[]{:S(2)}) collective-permute-start(bf16[400,384]{1,0:T(8,128)(2,1)} %get-tuple-element.69), channel_id=1, source_target_pairs={{0,8},{1,9},{2,10},{3,11},{4,12},{5,13},{6,14},{7,15},{8,16},{9,17... | collective-permute-start | bytes 921608 | tf_op jit(solution)/shard_map/ppermute | solution.py:140
  117.5 16.0 %collective-permute-start.19 = (bf16[400,384]{1,0:T(8,128)(2,1)}, bf16[400,384]{1,0:T(8,128)(2,1)}, u32[]{:S(2)}, u32[]{:S(2)}) collective-permute-start(bf16[400,384]{1,0:T(8,128)(2,1)} %get-tuple-element.68), channel_id=1, source_target_pairs={{0,16},{1,17},{2,18},{3,19},{4,20},{5,21},{6,22},{7,23},{8,24},{9,... | collective-permute-start | bytes 921608 | tf_op jit(solution)/shard_map/ppermute | solution.py:140
  120.1 13.9 %collective-permute-start.18 = (bf16[400,384]{1,0:T(8,128)(2,1)}, bf16[400,384]{1,0:T(8,128)(2,1)}, u32[]{:S(2)}, u32[]{:S(2)}) collective-permute-start(bf16[400,384]{1,0:T(8,128)(2,1)} %get-tuple-element.67), channel_id=1, source_target_pairs={{0,24},{1,25},{2,26},{3,27},{4,28},{5,29},{6,30},{7,31},{8,0},{9,1... | collective-permute-start | bytes 921608 | tf_op jit(solution)/shard_map/ppermute | solution.py:140
  126.2 12.8 %collective-permute-start.15 = (bf16[1,192,384]{2,1,0:T(8,128)(2,1)}, bf16[1,192,384]{2,1,0:T(8,128)(2,1)S(1)}, u32[]{:S(2)}, u32[]{:S(2)}) collective-permute-start(bf16[1,192,384]{2,1,0:T(8,128)(2,1)} %bitcast.75), channel_id=1, source_target_pairs={{0,8},{1,9},{2,10},{3,11},{4,12},{5,13},{6,14},{7,15},{8,16},{9,17... | collective-permute-start | bytes 442376 | tf_op jit(solution)/shard_map/ppermute | solution.py:140
  126.6 13.2 %collective-permute-start.16 = (bf16[1,192,384]{2,1,0:T(8,128)(2,1)}, bf16[1,192,384]{2,1,0:T(8,128)(2,1)S(1)}, u32[]{:S(2)}, u32[]{:S(2)}) collective-permute-start(bf16[1,192,384]{2,1,0:T(8,128)(2,1)} %bitcast.76), channel_id=1, source_target_pairs={{0,16},{1,17},{2,18},{3,19},{4,20},{5,21},{6,22},{7,23},{8,24},{9,... | collective-permute-start | bytes 442376 | tf_op jit(solution)/shard_map/ppermute | solution.py:140
  127.3 12.4 %collective-permute-start.17 = (bf16[1,192,384]{2,1,0:T(8,128)(2,1)}, bf16[1,192,384]{2,1,0:T(8,128)(2,1)S(1)}, u32[]{:S(2)}, u32[]{:S(2)}) collective-permute-start(bf16[1,192,384]{2,1,0:T(8,128)(2,1)} %bitcast.77), channel_id=1, source_target_pairs={{0,24},{1,25},{2,26},{3,27},{4,28},{5,29},{6,30},{7,31},{8,0},{9,1... | collective-permute-start | bytes 442376 | tf_op jit(solution)/shard_map/ppermute | solution.py:140
  139.7 9.0 %collective-permute-start.21 = (bf16[2,192,384]{2,1,0:T(8,128)(2,1)}, bf16[2,192,384]{2,1,0:T(8,128)(2,1)}, u32[]{:S(2)}, u32[]{:S(2)}) collective-permute-start(bf16[2,192,384]{2,1,0:T(8,128)(2,1)} %bitcast.9.refs_4_), channel_id=1, source_target_pairs={{0,8},{1,9},{2,10},{3,11},{4,12},{5,13},{6,14},{7,15},{8,16},{9,17... | collective-permute-start | bytes 884744 | tf_op jit(solution)/shard_map/ppermute | solution.py:140
  141.1 18.2 %collective-permute-start.22 = (bf16[2,192,384]{2,1,0:T(8,128)(2,1)}, bf16[2,192,384]{2,1,0:T(8,128)(2,1)}, u32[]{:S(2)}, u32[]{:S(2)}) collective-permute-start(bf16[2,192,384]{2,1,0:T(8,128)(2,1)} %bitcast.9.refs_4_), channel_id=1, source_target_pairs={{0,16},{1,17},{2,18},{3,19},{4,20},{5,21},{6,22},{7,23},{8,24},{9,... | collective-permute-start | bytes 884744 | tf_op jit(solution)/shard_map/ppermute | solution.py:140
  144.0 15.3 %collective-permute-start.23 = (bf16[2,192,384]{2,1,0:T(8,128)(2,1)}, bf16[2,192,384]{2,1,0:T(8,128)(2,1)}, u32[]{:S(2)}, u32[]{:S(2)}) collective-permute-start(bf16[2,192,384]{2,1,0:T(8,128)(2,1)} %bitcast.9.refs_4_), channel_id=1, source_target_pairs={{0,24},{1,25},{2,26},{3,27},{4,28},{5,29},{6,30},{7,31},{8,0},{9,1... | collective-permute-start | bytes 884744 | tf_op jit(solution)/shard_map/ppermute | solution.py:140
  148.8 14.6 %all-to-all-start.4 = ((bf16[8,1,96,384]{3,2,1,0:T(8,128)(2,1)}), bf16[8,1,96,384]{3,2,1,0:T(8,128)(2,1)}, u32[]{:S(2)}, u32[]{:S(2)}) async-start(bf16[8,1,96,384]{3,2,1,0:T(8,128)(2,1)} %weight_grads.3), calls=%async_computation.4 | async-start | bytes 1179648 | tf_op jit(solution)/shard_map/all_to_all | solution.py:134
  163.4 24.3 %all-to-all-start.5 = ((bf16[8,2,96,384]{3,2,1,0:T(8,128)(2,1)}), bf16[8,2,96,384]{3,2,1,0:T(8,128)(2,1)}, u32[]{:S(2)}, u32[]{:S(2)}) async-start(bf16[8,2,96,384]{3,2,1,0:T(8,128)(2,1)} %weight_grads.4), calls=%async_computation.5 | async-start | bytes 2359296 | tf_op jit(solution)/shard_map/all_to_all | solution.py:134
  168.6 7.6 %collective-permute-start.24 = (bf16[192,768]{1,0:T(8,128)(2,1)S(1)}, bf16[192,768]{1,0:T(8,128)(2,1)S(1)}, u32[]{:S(2)}, u32[]{:S(2)}) collective-permute-start(bf16[192,768]{1,0:T(8,128)(2,1)S(1)} %get-tuple-element.117), channel_id=1, source_target_pairs={{0,32},{32,0},{64,96},{96,64},{1,33},{33,1},{65,97},{97,65},{2,34}... | collective-permute-start | bytes 884744 | tf_op jit(solution)/shard_map/ppermute | solution.py:316
  171.9 4.2 %collective-permute-start.25 = (bf16[192,768]{1,0:T(8,128)(2,1)S(1)}, bf16[192,768]{1,0:T(8,128)(2,1)S(1)}, u32[]{:S(2)}, u32[]{:S(2)}) collective-permute-start(bf16[192,768]{1,0:T(8,128)(2,1)S(1)} %get-tuple-element.116), channel_id=1, source_target_pairs={{0,32},{32,0},{64,96},{96,64},{1,33},{33,1},{65,97},{97,65},{2,34}... | collective-permute-start | bytes 884744 | tf_op jit(solution)/shard_map/ppermute | solution.py:316
  172.0 11.0 %collective-permute-start.27 = (bf16[1,192,384]{2,1,0:T(8,128)(2,1)}, bf16[1,192,384]{2,1,0:T(8,128)(2,1)S(1)}, u32[]{:S(2)}, u32[]{:S(2)}) collective-permute-start(bf16[1,192,384]{2,1,0:T(8,128)(2,1)} %bitcast.71), channel_id=1, source_target_pairs={{0,8},{1,9},{2,10},{3,11},{4,12},{5,13},{6,14},{7,15},{8,16},{9,17... | collective-permute-start | bytes 442376 | tf_op jit(solution)/shard_map/ppermute | solution.py:140
  173.5 9.5 %collective-permute-start.28 = (bf16[1,192,384]{2,1,0:T(8,128)(2,1)}, bf16[1,192,384]{2,1,0:T(8,128)(2,1)S(1)}, u32[]{:S(2)}, u32[]{:S(2)}) collective-permute-start(bf16[1,192,384]{2,1,0:T(8,128)(2,1)} %bitcast.72), channel_id=1, source_target_pairs={{0,16},{1,17},{2,18},{3,19},{4,20},{5,21},{6,22},{7,23},{8,24},{9,... | collective-permute-start | bytes 442376 | tf_op jit(solution)/shard_map/ppermute | solution.py:140
  175.6 7.5 %collective-permute-start.29 = (bf16[1,192,384]{2,1,0:T(8,128)(2,1)}, bf16[1,192,384]{2,1,0:T(8,128)(2,1)S(1)}, u32[]{:S(2)}, u32[]{:S(2)}) collective-permute-start(bf16[1,192,384]{2,1,0:T(8,128)(2,1)} %bitcast.73), channel_id=1, source_target_pairs={{0,24},{1,25},{2,26},{3,27},{4,28},{5,29},{6,30},{7,31},{8,0},{9,1... | collective-permute-start | bytes 442376 | tf_op jit(solution)/shard_map/ppermute | solution.py:140
  177.8 16.7 %collective-permute-start.26 = (bf16[192,768]{1,0:T(8,128)(2,1)}, bf16[192,768]{1,0:T(8,128)(2,1)}, u32[]{:S(2)}, u32[]{:S(2)}) collective-permute-start(bf16[192,768]{1,0:T(8,128)(2,1)} %select_convert_fusion), channel_id=1, source_target_pairs={{0,64},{32,96},{64,0},{96,32},{1,65},{33,97},{65,1},{97,33},{2,66}... | collective-permute-start | bytes 884744 | tf_op jit(solution)/shard_map/ppermute | solution.py:321
  187.7 15.5 %all-to-all-start.6 = ((bf16[8,1,96,384]{3,2,1,0:T(8,128)(2,1)}), bf16[8,1,96,384]{3,2,1,0:T(8,128)(2,1)}, u32[]{:S(2)}, u32[]{:S(2)}) async-start(bf16[8,1,96,384]{3,2,1,0:T(8,128)(2,1)} %weight_grads.5), calls=%async_computation.6 | async-start | bytes 1179648 | tf_op jit(solution)/shard_map/all_to_all | solution.py:134
  (14 other events, 22.9 us)
